TPU v7x, 128 devices: a whole 4x4x4 slice. The times are simulated.
128 devices in a mesh: row: 8 (over x, z_hi), col: 16 (over y, z_lo, core).
Axes of the slice: x: 4, y: 4, z: 4 (z_hi: 2, z_lo: 2; z = z_hi * 2 + z_lo), core: 2. Of those that a mesh axis runs over, the one named last changes fastest.
Arguments:
- tokens: bfloat16 [128, 1024, 256], P('row', 'col'), may hold values from -6 to 6
- grad_out: bfloat16 [128, 1024, 256], P('row', 'col'), may hold values from -6 to 6
- scales: float32 [2, 256], replicated, may hold values from 0.1 to 1.9
- w_qkv: bfloat16 [256, 768], replicated
- w_out: bfloat16 [256, 256], replicated, may hold values from -0.375 to 0.375
- w_up: bfloat16 [256, 768], replicated, may hold values from -0.375 to 0.375
- w_down: bfloat16 [768, 256], replicated, may hold values from -0.21875 to 0.21875
Outputs:
- grad_tokens: bfloat16 [128, 1024, 256], P('row', 'col')
- grad_qkv: float32 [256, 768], P(('row', 'col'))
- grad_wout: float32 [256, 256], P(('row', 'col'))
- grad_up: float32 [256, 768], P(('row', 'col'))
- grad_down: float32 [768, 256], P(('row', 'col'))
- grad_scales: float32 [2, 256], replicated
All inputs are finite; a program needn't handle non-finite values.
Results may differ from a plain program's by a relative error of at most 0.015.
Values may be sent and summed in bfloat16 or wider, within the bound.
No kernel may reach another device: no remote copies, remote signals or barrier semaphores. Data moves between devices by JAX's collectives and lax.ppermute only.
A program may use at most 128 MiB of HBM per device.

v0:
```python
from functools import partial
import math

import jax
import jax.numpy as jnp
from jax import lax
from jax.sharding import PartitionSpec as P

HEADS = 4
FF = 768


def extended_2(cells, sides, width):
    for axis, dim in sides:
        count = lax.axis_size(axis)
        ends = count - 1
        head = lax.slice_in_dim(cells, 0, width, axis=dim)
        tail = lax.slice_in_dim(cells, cells.shape[dim] - width, cells.shape[dim], axis=dim)
        cells = jnp.concatenate(
            [
                lax.ppermute(tail, axis, [(i, (i + 1) % count) for i in range(ends)]),
                cells,
                lax.ppermute(head, axis, [((i + 1) % count, i) for i in range(ends)]),
            ],
            axis=dim,
        )
    return cells


def passed_along(x, axis, by):
    size = lax.axis_size(axis)
    pairs = [(i, i + by) for i in range(size) if 0 <= i + by < size]
    return lax.ppermute(x, axis, pairs)


def norm_parts(values):
    inverse = lax.rsqrt(jnp.mean(values * values, axis=-1, keepdims=True) + 1e-06)
    return (values * inverse, inverse)


def norm_back(grad_h, gain, normed, inverse):
    grad_n = grad_h * gain
    grad_x = inverse * (grad_n - normed * jnp.mean(grad_n * normed, axis=-1, keepdims=True))
    return (grad_x, jnp.sum(grad_h * normed, axis=(0, 1)))


def window_start(position, total):
    return jnp.clip(position - 3, 0, total - 7)


def band_table(
    row_start, col_start, row_base, col_base, rows_total, cols_total, block_rows, block_cols
):
    query_rows = row_base + row_start + jnp.arange(block_rows, dtype=jnp.int32)
    first_row = window_start(query_rows, rows_total)
    key_rows = row_base + row_start - 3 + jnp.arange(block_rows + 6, dtype=jnp.int32)
    row_ok = (key_rows[None, :] >= first_row[:, None]) & (
        key_rows[None, :] <= first_row[:, None] + 6
    )
    query_cols = col_base + col_start + jnp.arange(block_cols, dtype=jnp.int32)
    first_col = window_start(query_cols, cols_total)
    key_cols = col_base + col_start - 3 + jnp.arange(block_cols + 6, dtype=jnp.int32)
    col_ok = (key_cols[None, :] >= first_col[:, None]) & (
        key_cols[None, :] <= first_col[:, None] + 6
    )
    allowed = row_ok[:, None, :, None] & col_ok[None, :, None, :]
    return allowed.reshape(block_rows * block_cols, (block_rows + 6) * (block_cols + 6))


def softmax_weights(query_mat, key_mat, allowed, factor):
    scores = (
        jnp.einsum("qhd,khd->hqk", query_mat, key_mat, preferred_element_type=jnp.float32) * factor
    )
    scores = jnp.where(allowed[None], scores, -1e30)
    top = jnp.max(scores, axis=-1, keepdims=True)
    expon = jnp.exp(scores - top)
    return expon / jnp.sum(expon, axis=-1, keepdims=True)


def body(tokens, grad_out, scales, w_qkv, w_out, w_up, w_down):
    tile_rows, tile_cols, width = tokens.shape
    head_dim = width // HEADS
    factor = 1.0 / math.sqrt(head_dim)
    rows_total = tile_rows * lax.axis_size("row")
    cols_total = tile_cols * lax.axis_size("col")
    row_base = lax.axis_index("row") * tile_rows
    col_base = lax.axis_index("col") * tile_cols
    flat = tile_rows * tile_cols
    block_rows = 16
    block_cols = min(tile_cols, 512 // block_rows)
    count_rows = tile_rows // block_rows
    count_cols = tile_cols // block_cols
    slab_rows = block_rows + 6
    slab_cols = block_cols + 6
    blocks = jnp.arange(count_rows * count_cols, dtype=jnp.int32)
    zero = jnp.zeros((), jnp.int32)
    tokens_f = tokens.astype(jnp.float32)
    normed1, inverse1 = norm_parts(tokens_f)
    hidden1 = (normed1 * scales[0]).astype(jnp.bfloat16)
    projected = jnp.dot(
        hidden1.reshape(flat, width), w_qkv, preferred_element_type=jnp.float32
    ).astype(jnp.bfloat16)
    projected = projected.reshape(tile_rows, tile_cols, 3 * width)
    queries = projected[..., :width]
    keys_values = projected[..., width:]
    extended = extended_2(keys_values, (("row", 0), ("col", 1)), 3)

    def block_place(index):
        return (index // count_cols * block_rows, index % count_cols * block_cols)

    def block_inputs(index):
        row_start, col_start = block_place(index)
        query_mat = lax.dynamic_slice(
            queries, (row_start, col_start, zero), (block_rows, block_cols, width)
        )
        query_mat = query_mat.reshape(block_rows * block_cols, HEADS, head_dim)
        key_slab = lax.dynamic_slice(
            extended, (row_start, col_start, zero), (slab_rows, slab_cols, 2 * width)
        )
        key_slab = key_slab.reshape(slab_rows * slab_cols, 2 * HEADS, head_dim)
        allowed = band_table(
            row_start, col_start, row_base, col_base, rows_total, cols_total, block_rows, block_cols
        )
        weights_soft = softmax_weights(query_mat, key_slab[:, :HEADS], allowed, factor)
        return (query_mat, key_slab, weights_soft)

    def assemble(pieces):
        pieces = pieces.reshape(count_rows, count_cols, block_rows, block_cols, width)
        return jnp.transpose(pieces, (0, 2, 1, 3, 4)).reshape(tile_rows, tile_cols, width)

    def forward_block(index):
        query_mat, key_slab, weights_soft = block_inputs(index)
        rounded = weights_soft.astype(jnp.bfloat16)
        out = jnp.einsum(
            "hqk,khd->qhd", rounded, key_slab[:, HEADS:], preferred_element_type=jnp.float32
        )
        return out.astype(jnp.bfloat16).reshape(block_rows, block_cols, width)

    attended = assemble(lax.map(forward_block, blocks))
    attended_flat = attended.reshape(flat, width)
    mixed = jnp.dot(attended_flat, w_out, preferred_element_type=jnp.float32).reshape(
        tile_rows, tile_cols, width
    )
    resid = (tokens_f + mixed).astype(jnp.bfloat16)
    normed2, inverse2 = norm_parts(resid.astype(jnp.float32))
    hidden2 = (normed2 * scales[1]).astype(jnp.bfloat16).reshape(flat, width)
    pre_act = jnp.dot(hidden2, w_up, preferred_element_type=jnp.float32)
    activ, gelu_back = jax.vjp(partial(jax.nn.gelu, approximate=True), pre_act)
    activ = activ.astype(jnp.bfloat16)
    grad_flat = grad_out.reshape(flat, width)
    g_down = jnp.einsum("tf,tc->fc", activ, grad_flat, preferred_element_type=jnp.float32)
    grad_act = jnp.einsum("tc,fc->tf", grad_flat, w_down, preferred_element_type=jnp.float32)
    grad_pre = gelu_back(grad_act)[0].astype(jnp.bfloat16)
    g_up = jnp.einsum("tc,tf->cf", hidden2, grad_pre, preferred_element_type=jnp.float32)
    grad_h2 = jnp.einsum("tf,cf->tc", grad_pre, w_up, preferred_element_type=jnp.float32)
    back2, g_scale2 = norm_back(
        grad_h2.reshape(tile_rows, tile_cols, width), scales[1], normed2, inverse2
    )
    grad_resid = (grad_out.astype(jnp.float32) + back2).astype(jnp.bfloat16)
    resid_flat = grad_resid.reshape(flat, width)
    g_out = jnp.einsum("tc,te->ce", attended_flat, resid_flat, preferred_element_type=jnp.float32)
    grad_att = jnp.einsum(
        "te,ce->tc", resid_flat, w_out, preferred_element_type=jnp.float32
    ).astype(jnp.bfloat16)
    grad_att = grad_att.reshape(tile_rows, tile_cols, width)

    def backward_block(accum, index):
        query_mat, key_slab, weights_soft = block_inputs(index)
        rounded = weights_soft.astype(jnp.bfloat16)
        row_start, col_start = block_place(index)
        grad_mat = lax.dynamic_slice(
            grad_att, (row_start, col_start, zero), (block_rows, block_cols, width)
        )
        grad_mat = grad_mat.reshape(block_rows * block_cols, HEADS, head_dim)
        out_mat = lax.dynamic_slice(
            attended, (row_start, col_start, zero), (block_rows, block_cols, width)
        )
        out_mat = out_mat.reshape(block_rows * block_cols, HEADS, head_dim)
        grad_soft = jnp.einsum(
            "qhd,khd->hqk", grad_mat, key_slab[:, HEADS:], preferred_element_type=jnp.float32
        )
        inner = jnp.sum(grad_mat.astype(jnp.float32) * out_mat.astype(jnp.float32), axis=-1).T[
            :, :, None
        ]
        grad_scores = (weights_soft * (grad_soft - inner)).astype(jnp.bfloat16)
        grad_query = (
            jnp.einsum(
                "hqk,khd->qhd", grad_scores, key_slab[:, :HEADS], preferred_element_type=jnp.float32
            )
            * factor
        )
        grad_query = grad_query.astype(jnp.bfloat16).reshape(block_rows, block_cols, width)
        grad_keys = (
            jnp.einsum("hqk,qhd->khd", grad_scores, query_mat, preferred_element_type=jnp.float32)
            * factor
        )
        grad_vals = jnp.einsum(
            "hqk,qhd->khd", rounded, grad_mat, preferred_element_type=jnp.float32
        )
        grad_slab = jnp.concatenate((grad_keys, grad_vals), axis=1).reshape(
            slab_rows, slab_cols, 2 * width
        )
        current = lax.dynamic_slice(
            accum, (row_start, col_start, zero), (slab_rows, slab_cols, 2 * width)
        )
        accum = lax.dynamic_update_slice(accum, current + grad_slab, (row_start, col_start, zero))
        return (accum, grad_query)

    accum0 = jnp.zeros((tile_rows + 6, tile_cols + 6, 2 * width), jnp.float32)
    inner_grad, grad_q_blocks = lax.scan(backward_block, accum0, blocks)
    grad_q = assemble(grad_q_blocks)
    left_rim = inner_grad[:, :3]
    right_rim = inner_grad[:, tile_cols + 3 :]
    middle = inner_grad[:, 3 : tile_cols + 3]
    from_right = passed_along(left_rim.astype(jnp.bfloat16), "col", -1).astype(left_rim.dtype)
    from_left = passed_along(right_rim.astype(jnp.bfloat16), "col", 1).astype(right_rim.dtype)
    middle = middle.at[:, :3].add(from_left).at[:, tile_cols - 3 :].add(from_right)
    top_rim = middle[:3]
    bottom_rim = middle[tile_rows + 3 :]
    core = middle[3 : tile_rows + 3]
    from_below = passed_along(top_rim.astype(jnp.bfloat16), "row", -1).astype(top_rim.dtype)
    from_above = passed_along(bottom_rim.astype(jnp.bfloat16), "row", 1).astype(bottom_rim.dtype)
    core = core.at[:3].add(from_above).at[tile_rows - 3 :].add(from_below)
    grad_proj = jnp.concatenate((grad_q, core.astype(jnp.bfloat16)), axis=-1).reshape(
        flat, 3 * width
    )
    g_qkv = jnp.einsum(
        "tc,te->ce", hidden1.reshape(flat, width), grad_proj, preferred_element_type=jnp.float32
    )
    grad_h1 = jnp.einsum("te,ce->tc", grad_proj, w_qkv, preferred_element_type=jnp.float32)
    back1, g_scale1 = norm_back(
        grad_h1.reshape(tile_rows, tile_cols, width), scales[0], normed1, inverse1
    )
    grad_tokens = (grad_resid.astype(jnp.float32) + back1).astype(jnp.bfloat16)
    loss_scale = 1.0 / math.sqrt(rows_total * cols_total)
    g_qkv = g_qkv * loss_scale
    g_out = g_out * loss_scale
    g_up = g_up * loss_scale
    g_down = g_down * loss_scale
    g_scales = jnp.stack((g_scale1, g_scale2)) * loss_scale
    devices = lax.axis_size(("row", "col"))
    position = lax.axis_index(("row", "col"))
    totals = lax.psum((g_qkv, g_out, g_up, g_down, g_scales), ("row", "col"))
    share_qkv = lax.dynamic_slice_in_dim(
        totals[0], position * (width // devices), width // devices, 0
    )
    share_out = lax.dynamic_slice_in_dim(
        totals[1], position * (width // devices), width // devices, 0
    )
    share_up = lax.dynamic_slice_in_dim(
        totals[2], position * (width // devices), width // devices, 0
    )
    share_down = lax.dynamic_slice_in_dim(totals[3], position * (FF // devices), FF // devices, 0)
    scale_total = totals[4]
    return (grad_tokens, share_qkv, share_out, share_up, share_down, scale_total)


def solution(mesh):
    return jax.shard_map(
        body,
        mesh=mesh,
        in_specs=(P("row", "col", None), P("row", "col", None), P(), P(), P(), P(), P()),
        out_specs=(
            P("row", "col", None),
            P(("row", "col"), None),
            P(("row", "col"), None),
            P(("row", "col"), None),
            P(("row", "col"), None),
            P(),
        ),
        check_vma=False,
    )
```

profile of v0, /device:TPU:1, one launch (start us, length us, event | category | flops | bytes accessed | tf_op | source)
XLA Modules:
  0.0 401.9 jit_solution(8039534428484167093)
XLA Ops:
  11.2 6.3 %collective-permute-start = (bf16[3,64,512]{2,1,0:T(8,128)(2,1)S(1)}, bf16[3,64,512]{2,1,0:T(8,128)(2,1)S(1)}, u32[]{:S(2)}, u32[]{:S(2)}) collective-permute-start(bf16[3,64,512]{2,1,0:T(8,128)(2,1)S(1)} %get-tuple-element.418), channel_id=1, source_target_pairs={{0,16},{16,32},{32,48},{48,64},{64,80},{80,96},{96,112},{1,17},{17... | collective-permute-start | bytes 589832 | tf_op jit(solution)/shard_map/ppermute | solution.py:21
  21.1 5.3 %collective-permute-done.1 = bf16[3,64,512]{2,1,0:T(8,128)(2,1)S(1)} collective-permute-done((bf16[3,64,512]{2,1,0:T(8,128)(2,1)S(1)}, bf16[3,64,512]{2,1,0:T(8,128)(2,1)S(1)}, u32[]{:S(2)}, u32[]{:S(2)}) %collective-permute-start.1) | collective-permute-done | bytes 196640 | tf_op jit(solution)/shard_map/ppermute | solution.py:23
  27.1 4.4 %collective-permute-start.2 = (bf16[22,3,512]{2,1,0:T(4,128)(2,1)}, bf16[22,3,512]{2,1,0:T(4,128)(2,1)S(1)}, u32[]{:S(2)}, u32[]{:S(2)}) collective-permute-start(bf16[22,3,512]{2,1,0:T(4,128)(2,1)} %get-tuple-element.422), channel_id=1, source_target_pairs={{0,1},{1,2},{2,3},{3,4},{4,5},{5,6},{6,7},{7,8},{8,9},{9,10},{10,1... | collective-permute-start | bytes 202760 | tf_op jit(solution)/shard_map/ppermute | solution.py:21
  34.3 3.4 collective-permute-done.3
  37.7 3.0 pad_maximum_fusion.1
  40.7 42.2 %while.32 = (s32[]{:T(128)}, bf16[2,16,32,256]{3,2,0,1:T(8,128)(2,1)}, s32[2]{0:T(128)S(1)}, bf16[22,70,512]{2,1,0:T(8,128)(2,1)}, s32[]{:T(128)}, /*index=5*/s3...) while((s32[]{:T(128)}, ...), condition=%wide.region_4.5_spmd, body=%wide.region_1.4_spmd.sunk | while | flops 452566688 | bytes 40833852 | solution.py:139
  50.2 2.8 and.189
  55.8 3.6 fusion.142
  71.2 2.8 and.189
  76.9 3.6 fusion.142
  88.3 2.5 fusion.38
  97.0 104.9 %while.33 = (s32[]{:T(128)}, f32[22,70,512]{2,1,0:T(8,128)}, bf16[2,16,32,256]{3,2,1,0:T(8,128)(2,1)}, s32[2]{0:T(128)S(1)}, bf16[16,64,256]{2,1,0:T(8,128)(2,1)...) while((s32[]{:T(128)}, f32[22,70,512]{2,1,0:T(8,128)}, ...), condition=%wide.region_11.12_spmd, body=%wide.region_7.11_spmd.sunk | while | flops 1115171584 | bytes 101125040 | solution.py:210
  117.0 5.5 %fusion.155 = (f32[4,512]{1,0:T(4,128)S(1)}, f32[4,512,836]{1,2,0:T(8,128)}) fusion(pred[512,836]{0,1:T(8,128)(4,1)S(1)} %copy.91, bf16[512,4,64]{0,2,1:T(8,128)(2,1)S(1)} %copy-done.2, bf16[836,4,64]{0,2,1:T(8,128)(2,1)S(1)} %copy.93), kind=kOutput, calls=%fused_computation.147.clone.1 | convolution fusion | flops 226001728 | bytes 7974912 | tf_op jit(solution)/shard_map/while/body/eval_jaxpr/sub | solution.py:76
  122.5 4.2 %fusion.156 = f32[836,4,64]{0,2,1:T(8,128)S(1)} fusion(bf16[512,4,64]{0,2,1:T(8,128)(2,1)S(1)} %copy-done.5, f32[4,512,836]{1,2,0:T(8,128)} %get-tuple-element.567, f32[4,512]{1,0:T(4,128)S(1)} %get-tuple-element.568), kind=kOutput, calls=%fused_computation.43.clone.1 | convolution fusion | flops 222576640 | bytes 7974912 | tf_op jit(solution)/shard_map/while/body/eval_jaxpr/hqk,qhd->khd/dot_general | solution.py:197
  132.2 2.6 copy.95
  134.8 4.1 %reshape.612 = f32[22,38,512]{2,1,0:T(8,128)} reshape(f32[836,8,64]{2,1,0:T(8,128)} %copy.95) | data formatting | bytes 3424256 | tf_op jit(solution)/shard_map/while/body/eval_jaxpr/reshape | solution.py:200
  138.9 2.6 dynamic-slice_add_fusion.2
  141.5 8.4 %dynamic_update_slice.30 = f32[22,70,512]{2,1,0:T(8,128)} dynamic-update-slice(f32[22,70,512]{2,1,0:T(8,128)} %get-tuple-element.639, f32[22,38,512]{2,1,0:T(8,128)S(1)} %dynamic-slice_add_fusion.2, s32[]{:T(128)} %constant.414.clone.1..sunk.1, s32[]{:T(128)S(6)} %select_n.145, s32[]{:T(128)} %constant.414.clone.1..sunk.1) | dynamic-update-slice | bytes 3424260 | tf_op jit(solution)/shard_map/while/body/eval_jaxpr/dynamic_update_slice | solution.py:206
  169.9 5.5 %fusion.155 = (f32[4,512]{1,0:T(4,128)S(1)}, f32[4,512,836]{1,2,0:T(8,128)}) fusion(pred[512,836]{0,1:T(8,128)(4,1)S(1)} %copy.91, bf16[512,4,64]{0,2,1:T(8,128)(2,1)S(1)} %copy-done.2, bf16[836,4,64]{0,2,1:T(8,128)(2,1)S(1)} %copy.93), kind=kOutput, calls=%fused_computation.147.clone.1 | convolution fusion | flops 226001728 | bytes 7974912 | tf_op jit(solution)/shard_map/while/body/eval_jaxpr/sub | solution.py:76
  175.4 4.2 %fusion.156 = f32[836,4,64]{0,2,1:T(8,128)S(1)} fusion(bf16[512,4,64]{0,2,1:T(8,128)(2,1)S(1)} %copy-done.5, f32[4,512,836]{1,2,0:T(8,128)} %get-tuple-element.567, f32[4,512]{1,0:T(4,128)S(1)} %get-tuple-element.568), kind=kOutput, calls=%fused_computation.43.clone.1 | convolution fusion | flops 222576640 | bytes 7974912 | tf_op jit(solution)/shard_map/while/body/eval_jaxpr/hqk,qhd->khd/dot_general | solution.py:197
  185.0 2.6 copy.95
  187.6 4.1 %reshape.612 = f32[22,38,512]{2,1,0:T(8,128)} reshape(f32[836,8,64]{2,1,0:T(8,128)} %copy.95) | data formatting | bytes 3424256 | tf_op jit(solution)/shard_map/while/body/eval_jaxpr/reshape | solution.py:200
  191.7 2.5 dynamic-slice_add_fusion.2
  194.2 7.7 %dynamic_update_slice.30 = f32[22,70,512]{2,1,0:T(8,128)} dynamic-update-slice(f32[22,70,512]{2,1,0:T(8,128)} %get-tuple-element.639, f32[22,38,512]{2,1,0:T(8,128)S(1)} %dynamic-slice_add_fusion.2, s32[]{:T(128)} %constant.414.clone.1..sunk.1, s32[]{:T(128)S(6)} %select_n.145, s32[]{:T(128)} %constant.414.clone.1..sunk.1) | dynamic-update-slice | bytes 3424260 | tf_op jit(solution)/shard_map/while/body/eval_jaxpr/dynamic_update_slice | solution.py:206
  201.9 2.3 convert.9
  210.3 2.4 collective-permute-start.5
  214.1 3.5 collective-permute-done.5
  219.1 4.2 %collective-permute-start.6 = (bf16[3,64,512]{2,1,0:T(8,128)(2,1)S(1)}, bf16[3,64,512]{2,1,0:T(8,128)(2,1)S(1)}, u32[]{:S(2)}, u32[]{:S(2)}) collective-permute-start(bf16[3,64,512]{2,1,0:T(8,128)(2,1)S(1)} %get-tuple-element.421), channel_id=1, source_target_pairs={{0,16},{16,32},{32,48},{48,64},{64,80},{80,96},{96,112},{1,17},{17... | collective-permute-start | bytes 589832 | tf_op jit(solution)/shard_map/ppermute | solution.py:33
  227.2 6.5 %collective-permute-done.7 = bf16[3,64,512]{2,1,0:T(8,128)(2,1)S(1)} collective-permute-done((bf16[3,64,512]{2,1,0:T(8,128)(2,1)S(1)}, bf16[3,64,512]{2,1,0:T(8,128)(2,1)S(1)}, u32[]{:S(2)}, u32[]{:S(2)}) %collective-permute-start.7) | collective-permute-done | bytes 196640 | tf_op jit(solution)/shard_map/ppermute | solution.py:33
  235.6 2.4 fusion.65
  238.0 67.4 %psum.39 = f32[2,256]{1,0:T(2,128)} all-reduce(f32[2,256]{1,0:T(2,128)S(1)} %maximum_multiply_fusion), channel_id=1, replica_groups=mesh['row'=8,'col'=16] {'row','col'}, use_global_device_ids=true, to_apply=%region_19.20 | all-reduce | flops 512 | bytes 4096 | tf_op jit(solution)/shard_map/psum | solution.py:243
  307.3 83.8 %all-reduce.3.cloned.1.call-done = (f32[256,768]{1,0:T(8,128)}, f32[256,256]{1,0:T(8,128)}, f32[256,768]{1,0:T(8,128)}, f32[768,256]{1,0:T(8,128)}) async-done(((f32[256,768]{1,0:T(8,128)}, f32[256,256]{1,0:T(8,128)}, f32[256,768]{1,0:T(8,128)}, f32[768,256]{1,0:T(8,128)}), (f32[256,768]{1,0:T(8,128)}, f32[256,256]{1,0:T(8,128)}, f32[256,768]{1,0:T(8,128)}, ...) | async-done | bytes 2621456 | tf_op jit(solution)/shard_map/psum | solution.py:243
  (220 shorter events, 112.6 us)
Async XLA Ops:
  7.2 3.4 copy-start
  7.2 383.9 %all-reduce.3.cloned.1.call-start = ((), (), s32[]{:S(2)}) async-start(), calls=%async_computation | async-start | bytes 5242880 | tf_op jit(solution)/shard_map/psum | solution.py:243
  8.0 2.5 copy-start.23
  10.5 16.6 %copy-start.14 = (bf16[16,64,256]{2,1,0:T(8,128)(2,1)}, bf16[16,64,256]{2,1,0:T(8,128)(2,1)S(1)}, u32[]{:S(2)}) copy-start(bf16[16,64,256]{2,1,0:T(8,128)(2,1)S(1)} %fusion.59) | copy-start | bytes 1572868
  11.2 9.9 %collective-permute-start = (bf16[3,64,512]{2,1,0:T(8,128)(2,1)S(1)}, bf16[3,64,512]{2,1,0:T(8,128)(2,1)S(1)}, u32[]{:S(2)}, u32[]{:S(2)}) collective-permute-start(bf16[3,64,512]{2,1,0:T(8,128)(2,1)S(1)} %get-tuple-element.418), channel_id=1, source_target_pairs={{0,16},{16,32},{32,48},{48,64},{64,80},{80,96},{96,112},{1,17},{17... | collective-permute-start | bytes 589832 | tf_op jit(solution)/shard_map/ppermute | solution.py:21
  17.5 8.8 %collective-permute-start.1 = (bf16[3,64,512]{2,1,0:T(8,128)(2,1)S(1)}, bf16[3,64,512]{2,1,0:T(8,128)(2,1)S(1)}, u32[]{:S(2)}, u32[]{:S(2)}) collective-permute-start(bf16[3,64,512]{2,1,0:T(8,128)(2,1)S(1)} %get-tuple-element.419), channel_id=1, source_target_pairs={{16,0},{32,16},{48,32},{64,48},{80,64},{96,80},{112,96},{17,1},{33... | collective-permute-start | bytes 589832 | tf_op jit(solution)/shard_map/ppermute | solution.py:23
  27.1 7.2 %collective-permute-start.2 = (bf16[22,3,512]{2,1,0:T(4,128)(2,1)}, bf16[22,3,512]{2,1,0:T(4,128)(2,1)S(1)}, u32[]{:S(2)}, u32[]{:S(2)}) collective-permute-start(bf16[22,3,512]{2,1,0:T(4,128)(2,1)} %get-tuple-element.422), channel_id=1, source_target_pairs={{0,1},{1,2},{2,3},{3,4},{4,5},{5,6},{6,7},{7,8},{8,9},{9,10},{10,1... | collective-permute-start | bytes 202760 | tf_op jit(solution)/shard_map/ppermute | solution.py:21
  31.5 6.2 %collective-permute-start.3 = (bf16[22,3,512]{2,1,0:T(4,128)(2,1)}, bf16[22,3,512]{2,1,0:T(4,128)(2,1)}, u32[]{:S(2)}, u32[]{:S(2)}) collective-permute-start(bf16[22,3,512]{2,1,0:T(4,128)(2,1)} %get-tuple-element.423), channel_id=1, source_target_pairs={{1,0},{2,1},{3,2},{4,3},{5,4},{6,5},{7,6},{8,7},{9,8},{10,9},{11,1... | collective-permute-start | bytes 202760 | tf_op jit(solution)/shard_map/ppermute | solution.py:23
  55.8 3.6 copy-start.4
  76.9 3.6 copy-start.4
  82.9 2.8 copy-start.16
  82.9 3.4 copy-start.17
  112.3 4.7 %copy-start.2 = (bf16[512,4,64]{0,2,1:T(8,128)(2,1)S(1)}, bf16[512,4,64]{0,2,1:T(8,128)(2,1)}, u32[]{:S(2)}) copy-start(bf16[512,4,64]{0,2,1:T(8,128)(2,1)} %copy.92) | copy-start | bytes 786436 | tf_op jit(solution)/shard_map/while
  117.0 5.5 %copy-start.5 = (bf16[512,4,64]{0,2,1:T(8,128)(2,1)S(1)}, bf16[512,4,64]{0,2,1:T(8,128)(2,1)}, u32[]{:S(2)}) copy-start(bf16[512,4,64]{0,2,1:T(8,128)(2,1)} %copy.90) | copy-start | bytes 786436 | tf_op jit(solution)/shard_map/while
  122.5 4.2 %copy-start.3 = (bf16[836,4,64]{2,1,0:T(4,128)(2,1)S(1)}, bf16[836,4,64]{2,1,0:T(4,128)(2,1)}, u32[]{:S(2)}) copy-start(bf16[836,4,64]{2,1,0:T(4,128)(2,1)} %get-tuple-element.570) | copy-start | bytes 1284100 | tf_op jit(solution)/shard_map/while
  122.5 5.2 %copy-start.27 = (f32[4,512,836]{1,2,0:T(8,128)S(1)}, f32[4,512,836]{1,2,0:T(8,128)}, u32[]{:S(2)}) copy-start(f32[4,512,836]{1,2,0:T(8,128)} %get-tuple-element.567) | copy-start | bytes 20545540 | tf_op jit(solution)/shard_map/while
  165.1 4.7 %copy-start.2 = (bf16[512,4,64]{0,2,1:T(8,128)(2,1)S(1)}, bf16[512,4,64]{0,2,1:T(8,128)(2,1)}, u32[]{:S(2)}) copy-start(bf16[512,4,64]{0,2,1:T(8,128)(2,1)} %copy.92) | copy-start | bytes 786436 | tf_op jit(solution)/shard_map/while
  169.9 5.5 %copy-start.5 = (bf16[512,4,64]{0,2,1:T(8,128)(2,1)S(1)}, bf16[512,4,64]{0,2,1:T(8,128)(2,1)}, u32[]{:S(2)}) copy-start(bf16[512,4,64]{0,2,1:T(8,128)(2,1)} %copy.90) | copy-start | bytes 786436 | tf_op jit(solution)/shard_map/while
  175.4 4.2 %copy-start.3 = (bf16[836,4,64]{2,1,0:T(4,128)(2,1)S(1)}, bf16[836,4,64]{2,1,0:T(4,128)(2,1)}, u32[]{:S(2)}) copy-start(bf16[836,4,64]{2,1,0:T(4,128)(2,1)} %get-tuple-element.570) | copy-start | bytes 1284100 | tf_op jit(solution)/shard_map/while
  175.4 5.2 %copy-start.27 = (f32[4,512,836]{1,2,0:T(8,128)S(1)}, f32[4,512,836]{1,2,0:T(8,128)}, u32[]{:S(2)}) copy-start(f32[4,512,836]{1,2,0:T(8,128)} %get-tuple-element.567) | copy-start | bytes 20545540 | tf_op jit(solution)/shard_map/while
  201.9 4.9 %copy-start.7 = (bf16[1024,768]{1,0:T(8,128)(2,1)S(1)}, bf16[1024,768]{1,0:T(8,128)(2,1)}, u32[]{:S(2)}) copy-start(bf16[1024,768]{1,0:T(8,128)(2,1)} %copy-done.6) | copy-start | bytes 4718596
  201.9 4.9 %copy-start.13 = (bf16[16,64,256]{2,1,0:T(8,128)(2,1)S(1)}, bf16[16,64,256]{2,1,0:T(8,128)(2,1)}, u32[]{:S(2)}) copy-start(bf16[16,64,256]{2,1,0:T(8,128)(2,1)} %copy-done.12) | copy-start | bytes 1572868
  201.9 6.5 %copy-start.1 = (f32[22,70,512]{2,1,0:T(8,128)S(1)}, f32[22,70,512]{2,1,0:T(8,128)}, u32[]{:S(2)}) copy-start(f32[22,70,512]{2,1,0:T(8,128)} %get-tuple-element.345) | copy-start | bytes 9461764
  204.9 7.7 %collective-permute-start.4 = (bf16[22,3,512]{2,1,0:T(4,128)(2,1)S(1)}, bf16[22,3,512]{2,1,0:T(4,128)(2,1)S(1)}, u32[]{:S(2)}, u32[]{:S(2)}) collective-permute-start(bf16[22,3,512]{2,1,0:T(4,128)(2,1)S(1)} %get-tuple-element.417), channel_id=1, source_target_pairs={{0,1},{1,2},{2,3},{3,4},{4,5},{5,6},{6,7},{7,8},{8,9},{9,10},{10,1... | collective-permute-start | bytes 202760 | tf_op jit(solution)/shard_map/ppermute | solution.py:33
  210.3 7.3 %collective-permute-start.5 = (bf16[22,3,512]{2,1,0:T(4,128)(2,1)}, bf16[22,3,512]{2,1,0:T(4,128)(2,1)S(1)}, u32[]{:S(2)}, u32[]{:S(2)}) collective-permute-start(bf16[22,3,512]{2,1,0:T(4,128)(2,1)} %get-tuple-element.416), channel_id=1, source_target_pairs={{1,0},{2,1},{3,2},{4,3},{5,4},{6,5},{7,6},{8,7},{9,8},{10,9},{11,1... | collective-permute-start | bytes 202760 | tf_op jit(solution)/shard_map/ppermute | solution.py:33
  218.9 4.5 %copy-start.9 = (bf16[16,64,256]{2,1,0:T(8,128)(2,1)S(1)}, bf16[16,64,256]{2,1,0:T(8,128)(2,1)}, u32[]{:S(2)}) copy-start(bf16[16,64,256]{2,1,0:T(8,128)(2,1)} %copy-done.8) | copy-start | bytes 1572868
  219.1 8.0 %collective-permute-start.6 = (bf16[3,64,512]{2,1,0:T(8,128)(2,1)S(1)}, bf16[3,64,512]{2,1,0:T(8,128)(2,1)S(1)}, u32[]{:S(2)}, u32[]{:S(2)}) collective-permute-start(bf16[3,64,512]{2,1,0:T(8,128)(2,1)S(1)} %get-tuple-element.421), channel_id=1, source_target_pairs={{0,16},{16,32},{32,48},{48,64},{64,80},{80,96},{96,112},{1,17},{17... | collective-permute-start | bytes 589832 | tf_op jit(solution)/shard_map/ppermute | solution.py:33
  225.7 8.4 %copy-start.15 = (bf16[16,64,256]{2,1,0:T(8,128)(2,1)S(1)}, bf16[16,64,256]{2,1,0:T(8,128)(2,1)}, u32[]{:S(2)}) copy-start(bf16[16,64,256]{2,1,0:T(8,128)(2,1)} %copy-done.14) | copy-start | bytes 1572868
  225.7 8.4 %copy-start.19 = (bf16[1,16,2,32,256]{4,3,2,1,0:T(8,128)(2,1)S(1)}, bf16[1,16,2,32,256]{4,3,2,1,0:T(8,128)(2,1)}, u32[]{:S(2)}) copy-start(bf16[1,16,2,32,256]{4,3,2,1,0:T(8,128)(2,1)} %copy.56) | copy-start | bytes 1572868
  225.7 8.1 %collective-permute-start.7 = (bf16[3,64,512]{2,1,0:T(8,128)(2,1)S(1)}, bf16[3,64,512]{2,1,0:T(8,128)(2,1)S(1)}, u32[]{:S(2)}, u32[]{:S(2)}) collective-permute-start(bf16[3,64,512]{2,1,0:T(8,128)(2,1)S(1)} %get-tuple-element.420), channel_id=1, source_target_pairs={{16,0},{32,16},{48,32},{64,48},{80,64},{96,80},{112,96},{17,1},{33... | collective-permute-start | bytes 589832 | tf_op jit(solution)/shard_map/ppermute | solution.py:33
  235.6 2.4 copy-start.25
  235.6 70.6 %copy-start.10 = (bf16[16,64,256]{2,1,0:T(8,128)(2,1)S(1)}, bf16[16,64,256]{2,1,0:T(8,128)(2,1)}, u32[]{:S(2)}) copy-start(bf16[16,64,256]{2,1,0:T(8,128)(2,1)} %copy-done.8) | copy-start | bytes 1572868
  (10 other events, 15.2 us)
Sparse Core Ops, SparseCore 0:
  235.7 155.4 all-reduce.2
where the time goes:
time: 404 us; the launch traced here: 402 us
  waiting for transfers between devices  105 us (26%)
  local copies, waits for them, and re-layouts  100 us (25%)
  blocking collectives  67.4 us (17%)
  matrix products  46.1 us (11%)
  other arithmetic  34.7 us (9%)
  starting transfers between devices  23.9 us (6%)
  between operations  14.6 us (4%)
  loops' own time  10.5 us (3%)
    psum x1, waiting for transfers between devices, body(): totals = lax.psum((g_qkv, g_out, g_up, g_down, g_scales), ('row', 'col'))  83.8 us
    psum x1, blocking collectives, body(): totals = lax.psum((g_qkv, g_out, g_up, g_down, g_scales), ('row', 'col'))  67.4 us
    dynamic_update_slice x2, local copies, waits for them, and re-layouts, backward_block(): lax.dynamic_update_slice(accum, current + grad_slab, (row_start, col_star...  16.1 us
    and x8, local copies, waits for them, and re-layouts, band_table(): allowed = row_ok[:, None, :, None] & col_ok[None, :, None, :]  15.2 us
    sub x2, matrix products, softmax_weights(): expon = jnp.exp(scores - top)  11 us
    ppermute x2, starting transfers between devices, extended_2(): lax.ppermute(tail, axis, [(i, (i + 1) % count) for i in range(ends)])  10.7 us
    ppermute x4, waiting for transfers between devices, passed_along(): return lax.ppermute(x, axis, pairs)  10 us
    ppermute x4, starting transfers between devices, passed_along(): return lax.ppermute(x, axis, pairs)  9.95 us
  transfers between devices with their start and end apart: 9, of which 6 were waited for; matrix products, arithmetic and copies ran while one was open for 3% of the time, Pallas kernels for 0%

commit v1 on v0

v1 whole, which is shorter than its diff:
```python
import functools
import math

import jax
import jax.numpy as jnp
from jax import lax
from jax.experimental import pallas as pl
from jax.experimental.pallas import tpu as pltpu
from jax.sharding import Mesh, PartitionSpec as P

HEADS = 4
C = 256
FF = 768
TR, TC = 16, 64
ER, EC = 22, 80
KR, KC = 14, 16
NK = KR * KC
NB = 16
CHUNK = 48
EPS = 1e-6
NEG = -1e30
BF = jnp.bfloat16
F32 = jnp.float32
GA = math.sqrt(2.0 / math.pi)
GB = GA * 0.044715

ROW = ("x", "zh")
COL = ("y", "zl", "core")
CHIPS = ("x", "zh", "y", "zl")


def nt(a, b):
    return lax.dot_general(a, b, (((1,), (1,)), ((), ())), preferred_element_type=F32)


def tn(a, b):
    return lax.dot_general(a, b, (((0,), (0,)), ((), ())), preferred_element_type=F32)


def nn(a, b):
    return jnp.dot(a, b, preferred_element_type=F32)


def norm(x):
    inverse = lax.rsqrt(jnp.mean(x * x, axis=-1, keepdims=True) + EPS)
    return x * inverse, inverse


def head_masks():
    lane = lax.broadcasted_iota(jnp.int32, (1, C), 1)
    return [(jnp.right_shift(lane, 6) == h).astype(F32) for h in range(HEADS)]


def expand(x, masks):
    return jnp.concatenate([x * m for m in masks], axis=0).astype(BF)


def pick(x, masks):
    out = x[0:64] * masks[0]
    for h in range(1, HEADS):
        out = out + x[64 * h : 64 * h + 64] * masks[h]
    return out


def main_kernel(
    pos,
    tok_ext,
    tok,
    gout,
    scales,
    w_qkv,
    w_out,
    w_up,
    w_down,
    o_gr,
    o_dq,
    o_core,
    o_left,
    o_right,
    o_top,
    o_bottom,
    o_keep,
    o_send,
    bias,
    kv,
    dkv,
    q,
    att,
    gatt,
    dq,
    probs,
    h1e,
    h1l,
    attb,
    h2,
    activ,
    gpre,
    gmat,
    gdown,
    pk,
    side,
    gsc2,
    *,
    rows_total,
    cols_total,
):
    base_r, base_c, core = pos[0], pos[1], pos[2]
    masks = head_masks()

    key = lax.broadcasted_iota(jnp.int32, (NK, 1), 0)
    lane = jnp.bitwise_and(lax.broadcasted_iota(jnp.int32, (1, 256), 1), 63)
    for rb in range(2):
        k_row = base_r + rb * 8 - 3 + jnp.right_shift(key, 4)
        q_row = base_r + rb * 8 + jnp.right_shift(lane, 3)
        s_row = jnp.clip(q_row - 3, 0, rows_total - 7)
        row_ok = (k_row >= s_row) & (k_row <= s_row + 6)
        for kind, c0 in enumerate((0, 8, 56)):
            k_col = base_c + c0 - 3 + jnp.bitwise_and(key, 15)
            q_col = base_c + c0 + jnp.bitwise_and(lane, 7)
            s_col = jnp.clip(q_col - 3, 0, cols_total - 7)
            ok = row_ok & (k_col >= s_col) & (k_col <= s_col + 6)
            bias[rb * 3 + kind] = jnp.where(ok, 0.0, NEG)

    s0 = scales[0:1, :]
    s1 = scales[1:2, :]

    def project(i, carry):
        x = tok_ext[pl.ds(i * 2, 2)].reshape(2 * EC, C).astype(F32)
        h = (norm(x)[0] * s0).astype(BF)
        h1e[pl.ds(pl.multiple_of(i * 2 * EC, 16), 2 * EC), :] = h
        kv[pl.ds(i * 2, 2)] = nn(h, w_qkv[:, C:]).reshape(2, EC, 2 * C)
        dkv[pl.ds(i * 2, 2)] = jnp.zeros((2, EC, 2 * C), F32)
        return carry

    lax.fori_loop(0, ER // 2, project, 0)

    def project_q(i, carry):
        at = pl.ds(pl.multiple_of(i * 256, 256), 256)
        h = (norm(tok[at, :].astype(F32))[0] * s0).astype(BF)
        h1l[at, :] = h
        got = nn(h, w_qkv[:, :C]).astype(BF).astype(F32) * 0.125
        q[pl.ds(i * 4, 4)] = got.reshape(4, TC, C)
        return carry

    lax.fori_loop(0, 4, project_q, 0)

    def place(i):
        rb = jnp.right_shift(i, 3)
        cb = jnp.bitwise_and(i, 7)
        return rb, cb, pl.multiple_of(rb * 8, 8), pl.multiple_of(cb * 8, 8)

    def block_of(ref, r0, c0):
        return ref[pl.ds(r0, 8), pl.ds(c0, 8), :].reshape(64, C)

    def slab_of(r0, c0):
        return kv[pl.ds(r0, KR), pl.ds(c0, KC), :].astype(BF).reshape(NK, 2 * C)

    def forward(i, carry):
        rb, cb, r0, c0 = place(i)
        slab = slab_of(r0, c0)
        qe = expand(block_of(q, r0, c0), masks)
        kind = jnp.where(cb == 0, 0, jnp.where(cb == 7, 2, 1))
        s = nt(slab[:, :C], qe) + bias[rb * 3 + kind]
        e = jnp.exp(s - jnp.max(s, axis=0, keepdims=True))
        p = (e * (1.0 / jnp.sum(e, axis=0, keepdims=True))).astype(BF)
        probs[i] = p
        out = pick(tn(p, slab[:, C:]), masks)
        att[pl.ds(r0, 8), pl.ds(c0, 8), :] = out.reshape(8, 8, C)
        return carry

    lax.fori_loop(0, NB, forward, 0)

    gsc2[...] = jnp.zeros_like(gsc2)

    def feed(i, carry):
        at = pl.ds(pl.multiple_of(i * 256, 256), 256)
        a = att[pl.ds(i * 4, 4)].reshape(256, C).astype(BF)
        attb[at, :] = a
        resid = (tok[at, :].astype(F32) + nn(a, w_out[...])).astype(BF).astype(F32)
        n2, inv2 = norm(resid)
        h = (n2 * s1).astype(BF)
        h2[at, :] = h
        x = nn(h, w_up[...])
        g = gout[at, :]
        ga = nt(g, w_down[...])
        xx = x * x
        t = jnp.tanh(x * (GA + GB * xx))
        half = 0.5 + 0.5 * t
        act = x * half
        activ[at, :] = act.astype(BF)
        gp = (ga * (half + act * (1.0 - t) * (GA + (3.0 * GB) * xx))).astype(BF)
        gpre[at, :] = gp
        gh = nt(gp, w_up[...])
        gn = gh * s1
        back = inv2 * (gn - n2 * jnp.mean(gn * n2, axis=-1, keepdims=True))
        gsc2[...] += jnp.sum(gh * n2, axis=0, keepdims=True)
        gr = (g.astype(F32) + back).astype(BF)
        o_gr[at, :] = gr
        gatt[pl.ds(i * 4, 4)] = nt(gr, w_out[...]).astype(BF).astype(F32).reshape(4, TC, C)
        return carry

    lax.fori_loop(0, 4, feed, 0)

    def put(first, value):
        for n in range(value.shape[1] // 128):
            gmat[first + n] = value[:, n * 128 : n * 128 + 128]

    put(6, tn(attb[...], o_gr[...]))
    put(8, tn(h2[...], gpre[...]))
    for n in range(3):
        got = tn(activ[:, n * 256 : n * 256 + 256], gout[...])
        gdown[0, n * 256 : n * 256 + 256, :] = got[:, :128]
        gdown[1, n * 256 : n * 256 + 256, :] = got[:, 128:]

    def backward(i, carry):
        _, _, r0, c0 = place(i)
        slab = slab_of(r0, c0)
        qe = expand(block_of(q, r0, c0), masks)
        ge = expand(block_of(gatt, r0, c0), masks)
        pb = probs[i]
        p = pb.astype(F32)
        gs = nt(slab[:, C:], ge)
        ds = (p * (gs - jnp.sum(p * gs, axis=0, keepdims=True))).astype(BF)
        got = pick(tn(ds, slab[:, :C]), masks) * 0.125
        dq[pl.ds(r0, 8), pl.ds(c0, 8), :] = got.reshape(8, 8, C)
        at = (pl.ds(r0, KR), pl.ds(c0, KC))
        dkv[at + (slice(0, C),)] += nn(ds, qe).reshape(KR, KC, C)
        dkv[at + (slice(C, 2 * C),)] += nn(pb, ge).reshape(KR, KC, C)
        return carry

    lax.fori_loop(0, NB, backward, 0)

    o_dq[...] = dq[...].reshape(TR * TC, C).astype(BF)
    gq = tn(h1l[...], o_dq[...])
    gkv = tn(h1e[...], dkv[...].reshape(ER * EC, 2 * C).astype(BF))
    put(0, gq)
    put(2, gkv)

    prod = gq * w_qkv[:, :C].astype(F32)
    both = gkv * w_qkv[:, C:].astype(F32)
    lanes = prod[:, :128] + prod[:, 128:]
    for n in range(4):
        lanes = lanes + both[:, n * 128 : n * 128 + 128]
    gsc1 = jnp.sum(lanes.T, axis=0, keepdims=True) / s0
    rows = [gsc1[:, :128], gsc1[:, 128:], gsc2[:, :128], gsc2[:, 128:]]

    for c in range(2):
        for j in range(2):
            for n in range(14):
                pk[c, pl.ds(j * 14 + n, 64, stride=CHUNK), :] = gmat[
                    n, pl.ds(2 * c + j, 64, stride=4), :
                ]
        for j in range(6):
            for n in range(2):
                pk[c, pl.ds(28 + j * 2 + n, 64, stride=CHUNK), :] = gdown[
                    n, pl.ds(6 * c + j, 64, stride=12), :
                ]
        for j in range(4):
            pk[c, pl.ds(40 + j, 64, stride=CHUNK), :] = jnp.broadcast_to(rows[j], (64, 128))
            pk[c, pl.ds(44 + j, 64, stride=CHUNK), :] = jnp.zeros((64, 128), F32)
    o_keep[...] = pk[core].astype(BF)
    o_send[...] = pk[1 - core].astype(BF)

    side[...] = jnp.zeros_like(side)
    for r in range(ER):
        side[0, 3 * r : 3 * r + 3, :] = dkv[r, 0:3, :]
        side[1, 3 * r : 3 * r + 3, :] = dkv[r, TC + 3 : TC + 6, :]
    o_left[...] = side[0].astype(BF)
    o_right[...] = side[1].astype(BF)
    o_top[...] = dkv[0:3, 3 : TC + 3, :].reshape(3 * TC, 2 * C).astype(BF)
    o_bottom[...] = dkv[TR + 3 :, 3 : TC + 3, :].reshape(3 * TC, 2 * C).astype(BF)
    o_core[...] = dkv[3 : TR + 3, 3 : TC + 3, :].reshape(TR * TC, 2 * C).astype(BF)


def rim_kernel(top, bottom, from_left, from_right, o_top, o_bottom, work):
    for src, dst, first in ((top, o_top, 0), (bottom, o_bottom, TR + 3)):
        work[...] = src[...].astype(F32)
        left = from_left[...].astype(F32)
        right = from_right[...].astype(F32)
        for r in range(3):
            k = 3 * (first + r)
            work[r * TC : r * TC + 3, :] += left[k : k + 3, :]
            work[r * TC + TC - 3 : r * TC + TC, :] += right[k : k + 3, :]
        dst[...] = work[...].astype(BF)


def final_kernel(
    tok,
    gr,
    dq,
    core,
    from_left,
    from_right,
    from_above,
    from_below,
    w_qkv,
    scales,
    parts,
    o_tok,
    o_qkv,
    o_out,
    o_up,
    o_down,
    o_scales,
    work,
    left,
    right,
    *,
    loss_scale,
):
    work[...] = core[...].astype(F32)
    work[0 : 3 * TC, :] += from_above[...].astype(F32)
    work[(TR - 3) * TC :, :] += from_below[...].astype(F32)
    left[...] = from_left[...].astype(F32)
    right[...] = from_right[...].astype(F32)
    for r in range(TR):
        k = 3 * (r + 3)
        work[r * TC : r * TC + 3, :] += left[k : k + 3, :]
        work[r * TC + TC - 3 : r * TC + TC, :] += right[k : k + 3, :]
    s0 = scales[0:1, :]

    def step(i, carry):
        at = pl.ds(pl.multiple_of(i * 256, 256), 256)
        gh = nt(dq[at, :], w_qkv[:, :C]) + nt(work[at, :].astype(BF), w_qkv[:, C:])
        n1, inv1 = norm(tok[at, :].astype(F32))
        gn = gh * s0
        back = inv1 * (gn - n1 * jnp.mean(gn * n1, axis=-1, keepdims=True))
        o_tok[at, :] = (gr[at, :].astype(F32) + back).astype(BF)
        return carry

    lax.fori_loop(0, 4, step, 0)

    total = parts[0].astype(F32)
    for k in range(1, 64):
        total = total + parts[k].astype(F32)
    total = total * loss_scale
    for j in range(2):
        for n in range(14):
            row = total[j * 14 + n : j * 14 + n + 1, :]
            if n < 6:
                o_qkv[j : j + 1, n * 128 : n * 128 + 128] = row
            elif n < 8:
                o_out[j : j + 1, (n - 6) * 128 : (n - 6) * 128 + 128] = row
            else:
                o_up[j : j + 1, (n - 8) * 128 : (n - 8) * 128 + 128] = row
    for j in range(6):
        for n in range(2):
            o_down[j : j + 1, n * 128 : n * 128 + 128] = total[28 + 2 * j + n : 29 + 2 * j + n, :]
    for j in range(4):
        o_scales[j // 2 : j // 2 + 1, (j % 2) * 128 : (j % 2) * 128 + 128] = total[
            40 + j : 41 + j, :
        ]


def vm(n):
    return [pl.BlockSpec(memory_space=pltpu.VMEM)] * n


def sds(shape, dtype):
    return jax.ShapeDtypeStruct(shape, dtype)


PARAMS = dict(compiler_params=pltpu.CompilerParams(vmem_limit_bytes=52 * 1024 * 1024))


def along(x, axes, by):
    size = lax.axis_size(axes)
    return lax.ppermute(x, axes, [(i, i + by) for i in range(size) if 0 <= i + by < size])


def body(tokens, grad_out, scales, w_qkv, w_out, w_up, w_down):
    rows_total = TR * lax.axis_size(ROW)
    cols_total = TC * lax.axis_size(COL)
    core_id = lax.axis_index("core")
    pos = jnp.stack([lax.axis_index(ROW) * TR, lax.axis_index(COL) * TC, core_id]).astype(jnp.int32)

    above = along(tokens[TR - 3 :], ROW, 1)
    below = along(tokens[:3], ROW, -1)
    tall = jnp.concatenate([above, tokens, below], axis=0)
    before = along(tall[:, TC - 3 :], COL, 1)
    after = along(tall[:, :3], COL, -1)
    pad = jnp.zeros((ER, EC - TC - 6, C), BF)
    tok_ext = jnp.concatenate([before, tall, after, pad], axis=1)

    flat = TR * TC
    tok = tokens.reshape(flat, C)
    gout = grad_out.reshape(flat, C)
    outs = pl.pallas_call(
        functools.partial(main_kernel, rows_total=rows_total, cols_total=cols_total),
        out_shape=[
            sds((flat, C), BF),
            sds((flat, C), BF),
            sds((flat, 2 * C), BF),
            sds((80, 2 * C), BF),
            sds((80, 2 * C), BF),
            sds((3 * TC, 2 * C), BF),
            sds((3 * TC, 2 * C), BF),
            sds((64 * CHUNK, 128), BF),
            sds((64 * CHUNK, 128), BF),
        ],
        in_specs=[pl.BlockSpec(memory_space=pltpu.SMEM)] + vm(8),
        out_specs=vm(9),
        scratch_shapes=[
            pltpu.VMEM((6, NK, 256), F32),
            pltpu.VMEM((ER, EC, 2 * C), F32),
            pltpu.VMEM((ER, EC, 2 * C), F32),
            pltpu.VMEM((TR, TC, C), F32),
            pltpu.VMEM((TR, TC, C), F32),
            pltpu.VMEM((TR, TC, C), F32),
            pltpu.VMEM((TR, TC, C), F32),
            pltpu.VMEM((NB, NK, 256), BF),
            pltpu.VMEM((ER * EC, C), BF),
            pltpu.VMEM((flat, C), BF),
            pltpu.VMEM((flat, C), BF),
            pltpu.VMEM((flat, C), BF),
            pltpu.VMEM((flat, FF), BF),
            pltpu.VMEM((flat, FF), BF),
            pltpu.VMEM((14, 256, 128), F32),
            pltpu.VMEM((2, FF, 128), F32),
            pltpu.VMEM((2, 64 * CHUNK, 128), F32),
            pltpu.VMEM((2, 80, 2 * C), F32),
            pltpu.VMEM((1, C), F32),
        ],
        name="block_backward",
        **PARAMS,
    )(pos, tok_ext, tok, gout, scales, w_qkv, w_out, w_up, w_down)
    gr, dq, core, left, right, top, bottom, keep, send = outs

    from_right = along(left, COL, -1)
    from_left = along(right, COL, 1)
    got = lax.ppermute(send, "core", [(0, 1), (1, 0)])
    top, bottom = pl.pallas_call(
        rim_kernel,
        out_shape=[sds((3 * TC, 2 * C), BF)] * 2,
        in_specs=vm(4),
        out_specs=vm(2),
        scratch_shapes=[pltpu.VMEM((3 * TC, 2 * C), F32)],
        name="rims",
        **PARAMS,
    )(top, bottom, from_left, from_right)
    from_below = along(top, ROW, -1)
    from_above = along(bottom, ROW, 1)
    mine = (keep + got).reshape(64, CHUNK, 128)
    parts = lax.all_to_all(mine, CHIPS, 0, 0, tiled=True)

    outs = pl.pallas_call(
        functools.partial(final_kernel, loss_scale=1.0 / math.sqrt(rows_total * cols_total)),
        out_shape=[
            sds((flat, C), BF),
            sds((2, 3 * C), F32),
            sds((2, C), F32),
            sds((2, FF), F32),
            sds((6, C), F32),
            sds((2, C), F32),
        ],
        in_specs=vm(11),
        out_specs=vm(6),
        scratch_shapes=[
            pltpu.VMEM((flat, 2 * C), F32),
            pltpu.VMEM((80, 2 * C), F32),
            pltpu.VMEM((80, 2 * C), F32),
        ],
        name="grad_tokens",
        **PARAMS,
    )(tok, gr, dq, core, from_left, from_right, from_above, from_below, w_qkv, scales, parts)
    return (outs[0].reshape(TR, TC, C),) + tuple(outs[1:])


def solution(mesh):
    fine = Mesh(mesh.devices.reshape(4, 2, 4, 2, 2), ("x", "zh", "y", "zl", "core"))
    tile = P(ROW, COL, None)
    share = P(ROW + COL, None)
    return jax.shard_map(
        body,
        mesh=fine,
        in_specs=(tile, tile, P(), P(), P(), P(), P()),
        out_specs=(tile, share, share, share, share, P()),
        check_vma=False,
    )
```

time: 404 us -> 108 us (0.27)
  the two profiles are of different devices: /device:TPU:1 before, /device:TPU:21 now
where the time goes in v1:
time: 108 us
  Pallas kernels  38.7 us (36%)
  starting transfers between devices  37.4 us (35%)
  waiting for transfers between devices  23.8 us (22%)
  other arithmetic  3.74 us (3%)
  local copies, waits for them, and re-layouts  3.12 us (3%)
    pallas_call x1, Pallas kernels, body(): pl.pallas_call(functools.partial(main_kernel, rows_total=rows_total, cols...  34.3 us
    ppermute x8, starting transfers between devices, along(): lax.ppermute(x, axes, [(i, i + by) for i in range(size) if 0 <= i + by <...  27.5 us
    ppermute x8, waiting for transfers between devices, along(): lax.ppermute(x, axes, [(i, i + by) for i in range(size) if 0 <= i + by <...  21.6 us
    all_to_all x1, starting transfers between devices, body(): parts = lax.all_to_all(mine, CHIPS, 0, 0, tiled=True)  9.59 us
    pallas_call x1, Pallas kernels, body(): pl.pallas_call(functools.partial(final_kernel, loss_scale=1.0 / math.sqrt...  4.35 us
    add x1, other arithmetic, body(): mine = (keep + got).reshape(64, CHUNK, 128)  2.25 us
    ppermute x1, waiting for transfers between devices, body(): got = lax.ppermute(send, 'core', [(0, 1), (1, 0)])  2.23 us
  transfers between devices with their start and end apart: 10, of which 7 were waited for; matrix products, arithmetic and copies ran while one was open for 1% of the time, Pallas kernels for 0%

profile of v1, /device:TPU:21, one launch (start us, length us, event | category | flops | bytes accessed | tf_op | source)
XLA Modules:
  0.0 107.6 jit_solution(8566788217306045441)
XLA Ops:
  0.6 1.0 fusion.1
  1.6 5.5 %collective-permute-start = (bf16[3,64,256]{2,1,0:T(8,128)(2,1)S(1)}, bf16[3,64,256]{2,1,0:T(8,128)(2,1)S(1)}, u32[]{:S(2)}, u32[]{:S(2)}) collective-permute-start(bf16[3,64,256]{2,1,0:T(8,128)(2,1)S(1)} %get-tuple-element.43), channel_id=1, source_target_pairs={{0,16},{16,32},{32,48},{48,64},{64,80},{80,96},{96,112},{1,17},{17... | collective-permute-start | bytes 294920 | tf_op jit(solution)/shard_map/ppermute | solution.py:368
  7.1 2.2 %collective-permute-start.1 = (bf16[3,64,256]{2,1,0:T(8,128)(2,1)S(1)}, bf16[3,64,256]{2,1,0:T(8,128)(2,1)S(1)}, u32[]{:S(2)}, u32[]{:S(2)}) collective-permute-start(bf16[3,64,256]{2,1,0:T(8,128)(2,1)S(1)} %get-tuple-element.42), channel_id=1, source_target_pairs={{16,0},{32,16},{48,32},{64,48},{80,64},{96,80},{112,96},{17,1},{33... | collective-permute-start | bytes 294920 | tf_op jit(solution)/shard_map/ppermute | solution.py:368
  9.3 0.0 collective-permute-done
  9.4 1.1 %constant_dynamic-update-slice_fusion.1 = bf16[22,64,256]{2,1,0:T(8,128)(2,1)S(1)} fusion(bf16[22,64,256]{2,1,0:T(8,128)(2,1)S(1)} %constant_dynamic-update-slice_fusion.2, bf16[16,64,256]{2,1,0:T(8,128)(2,1)} %param.7), kind=kLoop, calls=%fused_computation.2 | loop fusion | bytes 1048576
  10.4 0.0 copy-start.1
  10.5 0.0 copy-start.3
  10.5 0.0 copy-start.4
  10.5 0.0 copy-start.6
  10.5 3.5 %collective-permute-done.1 = bf16[3,64,256]{2,1,0:T(8,128)(2,1)S(1)} collective-permute-done((bf16[3,64,256]{2,1,0:T(8,128)(2,1)S(1)}, bf16[3,64,256]{2,1,0:T(8,128)(2,1)S(1)}, u32[]{:S(2)}, u32[]{:S(2)}) %collective-permute-start.1) | collective-permute-done | bytes 98336 | tf_op jit(solution)/shard_map/ppermute | solution.py:368
  14.0 4.6 %collective-permute-start.2 = (bf16[22,3,256]{2,1,0:T(4,128)(2,1)S(1)}, bf16[22,3,256]{2,1,0:T(4,128)(2,1)S(1)}, u32[]{:S(2)}, u32[]{:S(2)}) collective-permute-start(bf16[22,3,256]{2,1,0:T(4,128)(2,1)S(1)} %get-tuple-element.40), channel_id=1, source_target_pairs={{0,1},{1,2},{2,3},{3,4},{4,5},{5,6},{6,7},{7,8},{8,9},{9,10},{10,1... | collective-permute-start | bytes 101384 | tf_op jit(solution)/shard_map/ppermute | solution.py:368
  18.7 1.9 %collective-permute-start.3 = (bf16[22,3,256]{2,1,0:T(4,128)(2,1)S(1)}, bf16[22,3,256]{2,1,0:T(4,128)(2,1)S(1)}, u32[]{:S(2)}, u32[]{:S(2)}) collective-permute-start(bf16[22,3,256]{2,1,0:T(4,128)(2,1)S(1)} %get-tuple-element.41), channel_id=1, source_target_pairs={{1,0},{2,1},{3,2},{4,3},{5,4},{6,5},{7,6},{8,7},{9,8},{10,9},{11,1... | collective-permute-start | bytes 101384 | tf_op jit(solution)/shard_map/ppermute | solution.py:368
  20.6 0.1 pad_add_fusion.pos
  20.7 0.1 pad.3.clone
  20.8 3.3 %collective-permute-done.3 = bf16[22,3,256]{2,1,0:T(4,128)(2,1)S(1)} collective-permute-done((bf16[22,3,256]{2,1,0:T(4,128)(2,1)S(1)}, bf16[22,3,256]{2,1,0:T(4,128)(2,1)S(1)}, u32[]{:S(2)}, u32[]{:S(2)}) %collective-permute-start.3) | collective-permute-done | bytes 33824 | tf_op jit(solution)/shard_map/ppermute | solution.py:368
  24.0 1.4 %maximum_maximum_fusion.tok_ext = bf16[22,80,256]{2,1,0:T(8,128)(2,1)} fusion(bf16[22,3,256]{2,1,0:T(4,128)(2,1)S(1)} %collective-permute-done.3, bf16[22,64,256]{2,1,0:T(8,128)(2,1)S(1)} %constant_dynamic-update-slice_fusion, bf16[22,3,256]{2,1,0:T(4,128)(2,1)S(1)} %collective-permute-done.2, bf16[80]{0:T(256)(128)(2,1)S(1)} %pad.3.clone), kind=kLoop, calls=%fused_computation | loop fusion | flops 3604480 | bytes 1689760 | tf_op jit(solution)/shard_map/concatenate | solution.py:383
  25.5 34.3 %block_backward.1 = (bf16[1024,256]{1,0:T(8,128)(2,1)}, bf16[1024,256]{1,0:T(8,128)(2,1)}, bf16[1024,512]{1,0:T(8,128)(2,1)}, bf16[80,512]{1,0:T(8,128)(2,1)S(1)...) custom-call(s32[3]{0:T(128)S(1)} %pad_add_fusion.pos, ...), custom_call_target="tpu_custom_call" | custom-call | tf_op jit(solution)/shard_map/block_backward/pallas_call | solution.py:388
  59.8 0.3 collective-permute-start.8
  60.0 2.2 %collective-permute-done.8 = bf16[3072,128]{1,0:T(8,128)(2,1)S(1)} collective-permute-done((bf16[3072,128]{1,0:T(8,128)(2,1)}, bf16[3072,128]{1,0:T(8,128)(2,1)S(1)}, u32[]{:S(2)}, u32[]{:S(2)}) %collective-permute-start.8) | collective-permute-done | bytes 786464 | tf_op jit(solution)/shard_map/ppermute | solution.py:431
  62.3 2.2 %add.15 = bf16[3072,128]{1,0:T(8,128)(2,1)} add(bf16[3072,128]{1,0:T(8,128)(2,1)} %get-tuple-element.32, bf16[3072,128]{1,0:T(8,128)(2,1)S(1)} %collective-permute-done.8) | non-fusion elementwise | flops 393216 | bytes 2359296 | tf_op jit(solution)/shard_map/add | solution.py:443
  64.5 9.6 %all-to-all-start = ((bf16[64,48,128]{2,1,0:T(8,128)(2,1)}), bf16[64,48,128]{2,1,0:T(8,128)(2,1)S(1)}, u32[]{:S(2)}, u32[]{:S(2)}) async-start(bf16[64,48,128]{2,1,0:T(8,128)(2,1)} %bitcast.5), calls=%async_computation | async-start | bytes 1572864 | tf_op jit(solution)/shard_map/all_to_all | solution.py:444
  74.1 3.7 %collective-permute-start.4 = (bf16[80,512]{1,0:T(8,128)(2,1)S(1)}, bf16[80,512]{1,0:T(8,128)(2,1)S(1)}, u32[]{:S(2)}, u32[]{:S(2)}) collective-permute-start(bf16[80,512]{1,0:T(8,128)(2,1)S(1)} %get-tuple-element.26), channel_id=1, source_target_pairs={{0,1},{1,2},{2,3},{3,4},{4,5},{5,6},{6,7},{7,8},{8,9},{9,10},{10,1... | collective-permute-start | bytes 245768 | tf_op jit(solution)/shard_map/ppermute | solution.py:368
  77.8 1.9 %collective-permute-start.5 = (bf16[80,512]{1,0:T(8,128)(2,1)S(1)}, bf16[80,512]{1,0:T(8,128)(2,1)S(1)}, u32[]{:S(2)}, u32[]{:S(2)}) collective-permute-start(bf16[80,512]{1,0:T(8,128)(2,1)S(1)} %get-tuple-element.27), channel_id=1, source_target_pairs={{1,0},{2,1},{3,2},{4,3},{5,4},{6,5},{7,6},{8,7},{9,8},{10,9},{11,1... | collective-permute-start | bytes 245768 | tf_op jit(solution)/shard_map/ppermute | solution.py:368
  79.7 5.0 %collective-permute-done.4.from_left = bf16[80,512]{1,0:T(8,128)(2,1)S(1)} collective-permute-done((bf16[80,512]{1,0:T(8,128)(2,1)S(1)}, bf16[80,512]{1,0:T(8,128)(2,1)S(1)}, u32[]{:S(2)}, u32[]{:S(2)}) %collective-permute-start.4) | collective-permute-done | bytes 81952 | tf_op jit(solution)/shard_map/ppermute | solution.py:368
  84.7 2.2 %collective-permute-done.5.from_right = bf16[80,512]{1,0:T(8,128)(2,1)S(1)} collective-permute-done((bf16[80,512]{1,0:T(8,128)(2,1)S(1)}, bf16[80,512]{1,0:T(8,128)(2,1)S(1)}, u32[]{:S(2)}, u32[]{:S(2)}) %collective-permute-start.5) | collective-permute-done | bytes 81952 | tf_op jit(solution)/shard_map/ppermute | solution.py:368
  86.9 0.1 rims.1
  87.0 3.8 %collective-permute-start.6 = (bf16[192,512]{1,0:T(8,128)(2,1)S(1)}, bf16[192,512]{1,0:T(8,128)(2,1)S(1)}, u32[]{:S(2)}, u32[]{:S(2)}) collective-permute-start(bf16[192,512]{1,0:T(8,128)(2,1)S(1)} %get-tuple-element.30), channel_id=1, source_target_pairs={{0,16},{16,32},{32,48},{48,64},{64,80},{80,96},{96,112},{1,17},{17... | collective-permute-start | bytes 589832 | tf_op jit(solution)/shard_map/ppermute | solution.py:368
  90.8 3.9 %collective-permute-start.7 = (bf16[192,512]{1,0:T(8,128)(2,1)S(1)}, bf16[192,512]{1,0:T(8,128)(2,1)S(1)}, u32[]{:S(2)}, u32[]{:S(2)}) collective-permute-start(bf16[192,512]{1,0:T(8,128)(2,1)S(1)} %get-tuple-element.31), channel_id=1, source_target_pairs={{16,0},{32,16},{48,32},{64,48},{80,64},{96,80},{112,96},{17,1},{33... | collective-permute-start | bytes 589832 | tf_op jit(solution)/shard_map/ppermute | solution.py:368
  94.7 3.5 %collective-permute-done.6.from_above = bf16[192,512]{1,0:T(8,128)(2,1)S(1)} collective-permute-done((bf16[192,512]{1,0:T(8,128)(2,1)S(1)}, bf16[192,512]{1,0:T(8,128)(2,1)S(1)}, u32[]{:S(2)}, u32[]{:S(2)}) %collective-permute-start.6) | collective-permute-done | bytes 196640 | tf_op jit(solution)/shard_map/ppermute | solution.py:368
  98.2 4.2 %collective-permute-done.7.from_below = bf16[192,512]{1,0:T(8,128)(2,1)S(1)} collective-permute-done((bf16[192,512]{1,0:T(8,128)(2,1)S(1)}, bf16[192,512]{1,0:T(8,128)(2,1)S(1)}, u32[]{:S(2)}, u32[]{:S(2)}) %collective-permute-start.7) | collective-permute-done | bytes 196640 | tf_op jit(solution)/shard_map/ppermute | solution.py:368
  102.3 0.9 copy-done.7
  103.3 4.3 %grad_tokens.1 = (bf16[1024,256]{1,0:T(8,128)(2,1)}, f32[2,768]{1,0:T(2,128)}, f32[2,256]{1,0:T(2,128)}, f32[2,768]{1,0:T(2,128)}, f32[6,256]{1,0:T(8,128)}, /*index=5*/f32[2,256]{1,0:T(2,128)}) custom-call(bf16[1024,256]{1,0:T(8,128)(2,1)S(1)} %bitcast.8, bf16[1024,256]{1,0:T(8,128)(2,1)S(1)} %copy-done.2, bf16[1024,256]{1,0:T(8,128)(2,1)} %get-tuple-element.24.dq, ...), custom_call_target="tpu_custom_call" | custom-call | tf_op jit(solution)/shard_map/grad_tokens/pallas_call | solution.py:446
  (17 shorter events, 0.1 us)
Async XLA Ops:
  1.6 7.8 %collective-permute-start = (bf16[3,64,256]{2,1,0:T(8,128)(2,1)S(1)}, bf16[3,64,256]{2,1,0:T(8,128)(2,1)S(1)}, u32[]{:S(2)}, u32[]{:S(2)}) collective-permute-start(bf16[3,64,256]{2,1,0:T(8,128)(2,1)S(1)} %get-tuple-element.43), channel_id=1, source_target_pairs={{0,16},{16,32},{32,48},{48,64},{64,80},{80,96},{96,112},{1,17},{17... | collective-permute-start | bytes 294920 | tf_op jit(solution)/shard_map/ppermute | solution.py:368
  7.1 6.9 %collective-permute-start.1 = (bf16[3,64,256]{2,1,0:T(8,128)(2,1)S(1)}, bf16[3,64,256]{2,1,0:T(8,128)(2,1)S(1)}, u32[]{:S(2)}, u32[]{:S(2)}) collective-permute-start(bf16[3,64,256]{2,1,0:T(8,128)(2,1)S(1)} %get-tuple-element.42), channel_id=1, source_target_pairs={{16,0},{32,16},{48,32},{64,48},{80,64},{96,80},{112,96},{17,1},{33... | collective-permute-start | bytes 294920 | tf_op jit(solution)/shard_map/ppermute | solution.py:368
  10.4 15.0 %copy-start.1 = (bf16[256,768]{1,0:T(8,128)(2,1)S(1)}, bf16[256,768]{1,0:T(8,128)(2,1)}, u32[]{:S(2)}) copy-start(bf16[256,768]{1,0:T(8,128)(2,1)} %w_qkv.3) | copy-start | bytes 1179652
  10.5 15.0 %copy-start.3 = (bf16[256,768]{1,0:T(8,128)(2,1)S(1)}, bf16[256,768]{1,0:T(8,128)(2,1)}, u32[]{:S(2)}) copy-start(bf16[256,768]{1,0:T(8,128)(2,1)} %w_up.1) | copy-start | bytes 1179652
  10.5 15.0 %copy-start.4 = (bf16[768,256]{1,0:T(8,128)(2,1)S(1)}, bf16[768,256]{1,0:T(8,128)(2,1)}, u32[]{:S(2)}) copy-start(bf16[768,256]{1,0:T(8,128)(2,1)} %w_down.1) | copy-start | bytes 1179652
  10.5 15.0 %copy-start.5 = (bf16[256,256]{1,0:T(8,128)(2,1)S(1)}, bf16[256,256]{1,0:T(8,128)(2,1)}, u32[]{:S(2)}) copy-start(bf16[256,256]{1,0:T(8,128)(2,1)} %w_out.1) | copy-start | bytes 393220
  10.5 15.0 %copy-start.6 = (f32[2,256]{1,0:T(2,128)S(1)}, f32[2,256]{1,0:T(2,128)}, u32[]{:S(2)}) copy-start(f32[2,256]{1,0:T(2,128)} %scales.3) | copy-start | bytes 6148
  14.0 6.7 %collective-permute-start.2 = (bf16[22,3,256]{2,1,0:T(4,128)(2,1)S(1)}, bf16[22,3,256]{2,1,0:T(4,128)(2,1)S(1)}, u32[]{:S(2)}, u32[]{:S(2)}) collective-permute-start(bf16[22,3,256]{2,1,0:T(4,128)(2,1)S(1)} %get-tuple-element.40), channel_id=1, source_target_pairs={{0,1},{1,2},{2,3},{3,4},{4,5},{5,6},{6,7},{7,8},{8,9},{9,10},{10,1... | collective-permute-start | bytes 101384 | tf_op jit(solution)/shard_map/ppermute | solution.py:368
  18.7 5.4 %collective-permute-start.3 = (bf16[22,3,256]{2,1,0:T(4,128)(2,1)S(1)}, bf16[22,3,256]{2,1,0:T(4,128)(2,1)S(1)}, u32[]{:S(2)}, u32[]{:S(2)}) collective-permute-start(bf16[22,3,256]{2,1,0:T(4,128)(2,1)S(1)} %get-tuple-element.41), channel_id=1, source_target_pairs={{1,0},{2,1},{3,2},{4,3},{5,4},{6,5},{7,6},{8,7},{9,8},{10,9},{11,1... | collective-permute-start | bytes 101384 | tf_op jit(solution)/shard_map/ppermute | solution.py:368
  59.8 2.5 %collective-permute-start.8 = (bf16[3072,128]{1,0:T(8,128)(2,1)}, bf16[3072,128]{1,0:T(8,128)(2,1)S(1)}, u32[]{:S(2)}, u32[]{:S(2)}) collective-permute-start(bf16[3072,128]{1,0:T(8,128)(2,1)} %get-tuple-element.33), channel_id=1, source_target_pairs={{0,1},{1,0},{2,3},{3,2},{4,5},{5,4},{6,7},{7,6},{8,9},{9,8},{10,11... | collective-permute-start | bytes 2359304 | tf_op jit(solution)/shard_map/ppermute | solution.py:431
  64.5 38.8 %copy-start = (bf16[16,64,256]{2,1,0:T(8,128)(2,1)S(1)}, bf16[16,64,256]{2,1,0:T(8,128)(2,1)}, u32[]{:S(2)}) copy-start(bf16[16,64,256]{2,1,0:T(8,128)(2,1)} %param.7) | copy-start | bytes 1572868
  64.5 38.8 %copy-start.2 = (bf16[1024,256]{1,0:T(8,128)(2,1)S(1)}, bf16[1024,256]{1,0:T(8,128)(2,1)}, u32[]{:S(2)}) copy-start(bf16[1024,256]{1,0:T(8,128)(2,1)} %get-tuple-element.23.gr) | copy-start | bytes 1572868
  64.5 37.8 %all-to-all-start = ((bf16[64,48,128]{2,1,0:T(8,128)(2,1)}), bf16[64,48,128]{2,1,0:T(8,128)(2,1)S(1)}, u32[]{:S(2)}, u32[]{:S(2)}) async-start(bf16[64,48,128]{2,1,0:T(8,128)(2,1)} %bitcast.5), calls=%async_computation | async-start | bytes 1572864 | tf_op jit(solution)/shard_map/all_to_all | solution.py:444
  74.1 10.6 %collective-permute-start.4 = (bf16[80,512]{1,0:T(8,128)(2,1)S(1)}, bf16[80,512]{1,0:T(8,128)(2,1)S(1)}, u32[]{:S(2)}, u32[]{:S(2)}) collective-permute-start(bf16[80,512]{1,0:T(8,128)(2,1)S(1)} %get-tuple-element.26), channel_id=1, source_target_pairs={{0,1},{1,2},{2,3},{3,4},{4,5},{5,6},{6,7},{7,8},{8,9},{9,10},{10,1... | collective-permute-start | bytes 245768 | tf_op jit(solution)/shard_map/ppermute | solution.py:368
  77.8 9.1 %collective-permute-start.5 = (bf16[80,512]{1,0:T(8,128)(2,1)S(1)}, bf16[80,512]{1,0:T(8,128)(2,1)S(1)}, u32[]{:S(2)}, u32[]{:S(2)}) collective-permute-start(bf16[80,512]{1,0:T(8,128)(2,1)S(1)} %get-tuple-element.27), channel_id=1, source_target_pairs={{1,0},{2,1},{3,2},{4,3},{5,4},{6,5},{7,6},{8,7},{9,8},{10,9},{11,1... | collective-permute-start | bytes 245768 | tf_op jit(solution)/shard_map/ppermute | solution.py:368
  87.0 11.2 %collective-permute-start.6 = (bf16[192,512]{1,0:T(8,128)(2,1)S(1)}, bf16[192,512]{1,0:T(8,128)(2,1)S(1)}, u32[]{:S(2)}, u32[]{:S(2)}) collective-permute-start(bf16[192,512]{1,0:T(8,128)(2,1)S(1)} %get-tuple-element.30), channel_id=1, source_target_pairs={{0,16},{16,32},{32,48},{48,64},{64,80},{80,96},{96,112},{1,17},{17... | collective-permute-start | bytes 589832 | tf_op jit(solution)/shard_map/ppermute | solution.py:368
  90.8 11.5 %collective-permute-start.7 = (bf16[192,512]{1,0:T(8,128)(2,1)S(1)}, bf16[192,512]{1,0:T(8,128)(2,1)S(1)}, u32[]{:S(2)}, u32[]{:S(2)}) collective-permute-start(bf16[192,512]{1,0:T(8,128)(2,1)S(1)} %get-tuple-element.31), channel_id=1, source_target_pairs={{16,0},{32,16},{48,32},{64,48},{80,64},{96,80},{112,96},{17,1},{33... | collective-permute-start | bytes 589832 | tf_op jit(solution)/shard_map/ppermute | solution.py:368
  102.3 0.9 copy-start.7

commit v2 on v1

v2 whole, which is shorter than its diff:
```python
import functools
import math

import jax
import jax.numpy as jnp
from jax import lax
from jax.experimental import pallas as pl
from jax.experimental.pallas import tpu as pltpu
from jax.sharding import Mesh, PartitionSpec as P

HEADS = 4
C = 256
FF = 768
TR, TC = 16, 64
ER, EC = 22, 72
KR, KC = 14, 16
NK = KR * KC
NB = 16
CHUNK = 48
EPS = 1e-6
NEG = -1e30
BF = jnp.bfloat16
F32 = jnp.float32
GA = math.sqrt(2.0 / math.pi)
GB = GA * 0.044715

ROW = ("x", "zh")
COL = ("y", "zl", "core")
CHIPS = ("x", "zh", "y", "zl")


def nt(a, b):
    return lax.dot_general(a, b, (((1,), (1,)), ((), ())), preferred_element_type=F32)


def tn(a, b):
    return lax.dot_general(a, b, (((0,), (0,)), ((), ())), preferred_element_type=F32)


def nn(a, b):
    return jnp.dot(a, b, preferred_element_type=F32)


def norm(x):
    inverse = lax.rsqrt(jnp.mean(x * x, axis=-1, keepdims=True) + EPS)
    return x * inverse, inverse


def head_masks():
    lane = lax.broadcasted_iota(jnp.int32, (1, C), 1)
    return [(jnp.right_shift(lane, 6) == h).astype(F32) for h in range(HEADS)]


def expand(x, masks):
    return jnp.concatenate([x * m for m in masks], axis=0).astype(BF)


def pick(x, masks):
    out = x[0:64] * masks[0]
    for h in range(1, HEADS):
        out = out + x[64 * h : 64 * h + 64] * masks[h]
    return out


def main_kernel(
    pos,
    tok,
    gout,
    intra,
    inter,
    first,
    second,
    scales,
    w_qkv,
    w_out,
    w_up,
    w_down,
    o_gr,
    o_gh,
    o_intra,
    o_inter,
    o_top,
    o_bottom,
    o_keep,
    o_send,
    bias,
    kv,
    dkv,
    q,
    att,
    gatt,
    dq,
    probs,
    h1l,
    attb,
    h2,
    activ,
    gpre,
    gmat,
    gdown,
    pk,
    side_in,
    side,
    *,
    rows_total,
    cols_total,
):
    base_r, base_c, core, half_row = pos[0], pos[1], pos[2], pos[3]
    even = core == 0
    masks = head_masks()

    key = lax.broadcasted_iota(jnp.int32, (NK, 1), 0)
    lane = jnp.bitwise_and(lax.broadcasted_iota(jnp.int32, (1, 256), 1), 63)
    for rb in range(2):
        k_row = base_r + rb * 8 - 3 + jnp.right_shift(key, 4)
        q_row = base_r + rb * 8 + jnp.right_shift(lane, 3)
        s_row = jnp.clip(q_row - 3, 0, rows_total - 7)
        row_ok = (k_row >= s_row) & (k_row <= s_row + 6)
        for kind, c0 in enumerate((0, 8, 56)):
            k_col = base_c + c0 - 3 + jnp.bitwise_and(key, 15)
            q_col = base_c + c0 + jnp.bitwise_and(lane, 7)
            s_col = jnp.clip(q_col - 3, 0, cols_total - 7)
            ok = row_ok & (k_col >= s_col) & (k_col <= s_col + 6)
            bias[rb * 3 + kind] = jnp.where(ok, 0.0, NEG)

    s0 = scales[0:1, :]
    s1 = scales[1:2, :]

    def hidden(x):
        return (norm(x.astype(F32))[0] * s0).astype(BF)

    kv[:, TC:, :] = jnp.zeros((ER, EC - TC, 2 * C), F32)
    for i in range(4):
        at = slice(256 * i, 256 * i + 256)
        h = hidden(tok[at, :])
        h1l[at, :] = h
        got = nn(h, w_qkv[:, :C]).astype(BF).astype(F32) * 0.125
        q[4 * i : 4 * i + 4] = got.reshape(4, TC, C)
        got = nn(h, w_qkv[:, C:])
        kv[3 + 4 * i : 7 + 4 * i, 3 : TC + 3, :] = got.reshape(4, TC, 2 * C)

    side_in[...] = jnp.zeros_like(side_in)
    upper = half_row == 0
    one = first[...].astype(F32)
    two = second[...].astype(F32)
    h_rows = []
    for at, x in ((0, jnp.where(upper, two, one)), (TR + 3, jnp.where(upper, one, two))):
        h = hidden(x[0 : 3 * TC])
        h_rows.append(h)
        kv[at : at + 3, 3 : TC + 3, :] = nn(h, w_qkv[:, C:]).reshape(3, TC, 2 * C)
        for k in range(2):
            lo = 3 * TC + 16 * k
            side_in[k, 3 * at : 3 * at + 9, :] = x[lo : lo + 9]
    h_above, h_below = h_rows
    for r in range(TR):
        near = intra[r].astype(F32)
        far = inter[r].astype(F32)
        side_in[0, 3 * r + 9 : 3 * r + 12, :] = jnp.where(even, far, near)
        side_in[1, 3 * r + 9 : 3 * r + 12, :] = jnp.where(even, near, far)
    h_side = [hidden(side_in[k]) for k in range(2)]
    for k in range(2):
        got = nn(h_side[k], w_qkv[:, C:])
        lo = k * (TC + 3)
        for r in range(ER):
            kv[r, lo : lo + 3, :] = got[3 * r : 3 * r + 3, :]
    dkv[...] = jnp.zeros_like(dkv)

    blocks = [(rb, cb) for cb in range(8) for rb in range(2)]

    def block_of(ref, r0, c0):
        return ref[r0 : r0 + 8, c0 : c0 + 8, :].reshape(64, C)

    def slab_of(r0, c0):
        return kv[r0 : r0 + KR, c0 : c0 + KC, :].astype(BF).reshape(NK, 2 * C)

    for i, (rb, cb) in enumerate(blocks):
        r0, c0 = 8 * rb, 8 * cb
        slab = slab_of(r0, c0)
        qe = expand(block_of(q, r0, c0), masks)
        kind = 0 if cb == 0 else 2 if cb == 7 else 1
        s = nt(slab[:, :C], qe) + bias[rb * 3 + kind]
        e = jnp.exp(s - jnp.max(s, axis=0, keepdims=True))
        p = (e * (1.0 / jnp.sum(e, axis=0, keepdims=True))).astype(BF)
        probs[i] = p
        out = pick(tn(p, slab[:, C:]), masks)
        att[r0 : r0 + 8, c0 : c0 + 8, :] = out.reshape(8, 8, C)

    gsc2 = jnp.zeros((1, C), F32)
    for i in range(4):
        at = slice(256 * i, 256 * i + 256)
        a = att[4 * i : 4 * i + 4].reshape(256, C).astype(BF)
        attb[at, :] = a
        resid = (tok[at, :].astype(F32) + nn(a, w_out[...])).astype(BF).astype(F32)
        n2, inv2 = norm(resid)
        h = (n2 * s1).astype(BF)
        h2[at, :] = h
        x = nn(h, w_up[...])
        g = gout[at, :]
        ga = nt(g, w_down[...])
        xx = x * x
        t = jnp.tanh(x * (GA + GB * xx))
        half = 0.5 + 0.5 * t
        act = x * half
        activ[at, :] = act.astype(BF)
        gp = (ga * (half + act * (1.0 - t) * (GA + (3.0 * GB) * xx))).astype(BF)
        gpre[at, :] = gp
        gh = nt(gp, w_up[...])
        gn = gh * s1
        back = inv2 * (gn - n2 * jnp.mean(gn * n2, axis=-1, keepdims=True))
        gsc2 = gsc2 + jnp.sum(gh * n2, axis=0, keepdims=True)
        gr = (g.astype(F32) + back).astype(BF)
        o_gr[at, :] = gr
        gatt[4 * i : 4 * i + 4] = nt(gr, w_out[...]).astype(BF).astype(F32).reshape(4, TC, C)

    def put(first, value):
        for n in range(value.shape[1] // 128):
            gmat[first + n] = value[:, n * 128 : n * 128 + 128]

    put(6, tn(attb[...], o_gr[...]))
    put(8, tn(h2[...], gpre[...]))
    for n in range(3):
        got = tn(activ[:, n * 256 : n * 256 + 256], gout[...])
        gdown[0, n * 256 : n * 256 + 256, :] = got[:, :128]
        gdown[1, n * 256 : n * 256 + 256, :] = got[:, 128:]

    for i, (rb, cb) in enumerate(blocks):
        r0, c0 = 8 * rb, 8 * cb
        slab = slab_of(r0, c0)
        qe = expand(block_of(q, r0, c0), masks)
        ge = expand(block_of(gatt, r0, c0), masks)
        pb = probs[i]
        p = pb.astype(F32)
        gs = nt(slab[:, C:], ge)
        ds = (p * (gs - jnp.sum(p * gs, axis=0, keepdims=True))).astype(BF)
        got = pick(tn(ds, slab[:, :C]), masks) * 0.125
        dq[r0 : r0 + 8, c0 : c0 + 8, :] = got.reshape(8, 8, C)
        dkv[r0 : r0 + KR, c0 : c0 + KC, :C] += nn(ds, qe).reshape(KR, KC, C)
        dkv[r0 : r0 + KR, c0 : c0 + KC, C:] += nn(pb, ge).reshape(KR, KC, C)

    side[...] = jnp.zeros_like(side)
    for r in range(ER):
        side[0, 3 * r : 3 * r + 3, :] = dkv[r, 0:3, :]
        side[1, 3 * r : 3 * r + 3, :] = dkv[r, TC + 3 : TC + 6, :]
    top = dkv[0:3, 3 : TC + 3, :].reshape(3 * TC, 2 * C).astype(BF)
    bottom = dkv[TR + 3 :, 3 : TC + 3, :].reshape(3 * TC, 2 * C).astype(BF)
    left = side[0].astype(BF)
    right = side[1].astype(BF)
    g_left = nt(left, w_qkv[:, C:])
    g_right = nt(right, w_qkv[:, C:])
    o_intra[...] = jnp.where(even, g_right, g_left).astype(BF)
    o_inter[...] = jnp.where(even, g_left, g_right).astype(BF)
    o_top[...] = nt(top, w_qkv[:, C:])
    o_bottom[...] = nt(bottom, w_qkv[:, C:])

    gq = jnp.zeros((C, C), F32)
    gkv = tn(h_above, top) + tn(h_below, bottom) + tn(h_side[0], left) + tn(h_side[1], right)
    for i in range(4):
        at = slice(256 * i, 256 * i + 256)
        d_q = dq[4 * i : 4 * i + 4].reshape(256, C).astype(BF)
        d_kv = dkv[3 + 4 * i : 7 + 4 * i, 3 : TC + 3, :].reshape(256, 2 * C).astype(BF)
        o_gh[at, :] = nt(d_q, w_qkv[:, :C]) + nt(d_kv, w_qkv[:, C:])
        h = h1l[at, :]
        gq = gq + tn(h, d_q)
        gkv = gkv + tn(h, d_kv)
    put(0, gq)
    put(2, gkv)

    prod = gq * w_qkv[:, :C].astype(F32)
    both = gkv * w_qkv[:, C:].astype(F32)
    lanes = prod[:, :128] + prod[:, 128:]
    for n in range(4):
        lanes = lanes + both[:, n * 128 : n * 128 + 128]
    gsc1 = jnp.sum(lanes.T, axis=0, keepdims=True) / s0
    rows = [gsc1[:, :128], gsc1[:, 128:], gsc2[:, :128], gsc2[:, 128:]]

    for c in range(2):
        for j in range(2):
            for n in range(14):
                pk[c, pl.ds(j * 14 + n, 64, stride=CHUNK), :] = gmat[
                    n, pl.ds(2 * c + j, 64, stride=4), :
                ]
        for j in range(6):
            for n in range(2):
                pk[c, pl.ds(28 + j * 2 + n, 64, stride=CHUNK), :] = gdown[
                    n, pl.ds(6 * c + j, 64, stride=12), :
                ]
        for j in range(4):
            pk[c, pl.ds(40 + j, 64, stride=CHUNK), :] = jnp.broadcast_to(rows[j], (64, 128))
            pk[c, pl.ds(44 + j, 64, stride=CHUNK), :] = jnp.zeros((64, 128), F32)
    o_keep[...] = pk[core].astype(BF)
    o_send[...] = pk[1 - core].astype(BF)


def rim_kernel(
    pos, top, bottom, intra, inter, keep, got, o_first, o_second, o_mine, work
):
    even = pos[2] == 0
    upper = pos[3] == 0
    near = intra[...].astype(F32)
    far = inter[...].astype(F32)
    left = jnp.where(even, far, near)
    right = jnp.where(even, near, far)
    for n, (src, at) in enumerate(((top, 0), (bottom, TR + 3))):
        work[n] = src[...]
        for r in range(3):
            k = 3 * (at + r)
            work[n, r * TC : r * TC + 3, :] += left[k : k + 3, :]
            work[n, r * TC + TC - 3 : r * TC + TC, :] += right[k : k + 3, :]
    o_first[...] = jnp.where(upper, work[1], work[0]).astype(BF)
    o_second[...] = jnp.where(upper, work[0], work[1]).astype(BF)
    o_mine[...] = (keep[...].astype(F32) + got[...].astype(F32)).astype(BF)


def token_kernel(pos, tok, gr, gh, intra, inter, first, second, scales, o_tok, work):
    even = pos[2] == 0
    upper = pos[3] == 0
    near = intra[...].astype(F32)
    far = inter[...].astype(F32)
    left = jnp.where(even, far, near)
    right = jnp.where(even, near, far)
    work[...] = gh[...]
    one = first[...].astype(F32)
    two = second[...].astype(F32)
    work[0 : 3 * TC, :] += jnp.where(upper, two, one)
    work[(TR - 3) * TC :, :] += jnp.where(upper, one, two)
    for r in range(TR):
        k = 3 * (r + 3)
        work[r * TC : r * TC + 3, :] += left[k : k + 3, :]
        work[r * TC + TC - 3 : r * TC + TC, :] += right[k : k + 3, :]
    s0 = scales[0:1, :]
    for i in range(4):
        at = slice(256 * i, 256 * i + 256)
        n1, inv1 = norm(tok[at, :].astype(F32))
        gn = work[at, :] * s0
        back = inv1 * (gn - n1 * jnp.mean(gn * n1, axis=-1, keepdims=True))
        o_tok[at, :] = (gr[at, :].astype(F32) + back).astype(BF)


def sum_kernel(parts, o_qkv, o_out, o_up, o_down, o_scales, *, loss_scale):
    total = parts[0].astype(F32)
    for k in range(1, 64):
        total = total + parts[k].astype(F32)
    total = total * loss_scale
    for j in range(2):
        for n in range(14):
            row = total[j * 14 + n : j * 14 + n + 1, :]
            if n < 6:
                o_qkv[j : j + 1, n * 128 : n * 128 + 128] = row
            elif n < 8:
                o_out[j : j + 1, (n - 6) * 128 : (n - 6) * 128 + 128] = row
            else:
                o_up[j : j + 1, (n - 8) * 128 : (n - 8) * 128 + 128] = row
    for j in range(6):
        for n in range(2):
            o_down[j : j + 1, n * 128 : n * 128 + 128] = total[28 + 2 * j + n : 29 + 2 * j + n, :]
    for j in range(4):
        o_scales[j // 2 : j // 2 + 1, (j % 2) * 128 : (j % 2) * 128 + 128] = total[
            40 + j : 41 + j, :
        ]


def vm(n):
    return [pl.BlockSpec(memory_space=pltpu.VMEM)] * n


def sds(shape, dtype):
    return jax.ShapeDtypeStruct(shape, dtype)


def params(mib):
    return dict(compiler_params=pltpu.CompilerParams(vmem_limit_bytes=mib * 1024 * 1024))


def swap(x, axes, odd):
    size = lax.axis_size(axes)
    pairs = [(i, i + 1) for i in range(odd, size - 1, 2)]
    return lax.ppermute(x, axes, pairs + [(b, a) for a, b in pairs])


def body(tokens, grad_out, scales, w_qkv, w_out, w_up, w_down):
    rows_total = TR * lax.axis_size(ROW)
    cols_total = TC * lax.axis_size(COL)
    core_id = lax.axis_index("core")
    half_row = lax.axis_index("zh")
    pos = jnp.stack(
        [lax.axis_index(ROW) * TR, lax.axis_index(COL) * TC, core_id, half_row]
    ).astype(jnp.int32)
    flat = TR * TC
    tok = tokens.reshape(flat, C)
    gout = grad_out.reshape(flat, C)
    smem = [pl.BlockSpec(memory_space=pltpu.SMEM)]

    even, upper = core_id == 0, half_row == 0
    head, tail = tokens[:, :3], tokens[:, TC - 3 :]
    inter = swap(jnp.where(even, head, tail), COL, 1)
    intra = swap(jnp.where(even, tail, head), COL, 0)
    before = jnp.where(even, inter, intra)
    after = jnp.where(even, intra, inter)

    def rim(lo):
        gap = jnp.zeros((7, C), BF)
        return jnp.concatenate(
            [
                tok[lo * TC : (lo + 3) * TC],
                before[lo : lo + 3].reshape(9, C),
                gap,
                after[lo : lo + 3].reshape(9, C),
                gap,
            ],
            axis=0,
        )

    top, bottom = rim(0), rim(TR - 3)
    first = swap(jnp.where(upper, bottom, top), ROW, 0)
    second = swap(jnp.where(upper, top, bottom), ROW, 1)

    outs = pl.pallas_call(
        functools.partial(main_kernel, rows_total=rows_total, cols_total=cols_total),
        out_shape=[
            sds((flat, C), BF),
            sds((flat, C), F32),
            sds((80, C), BF),
            sds((80, C), BF),
            sds((3 * TC, C), F32),
            sds((3 * TC, C), F32),
            sds((64 * CHUNK, 128), BF),
            sds((64 * CHUNK, 128), BF),
        ],
        in_specs=smem + vm(11),
        out_specs=vm(8),
        scratch_shapes=[
            pltpu.VMEM((6, NK, 256), F32),
            pltpu.VMEM((ER, EC, 2 * C), F32),
            pltpu.VMEM((ER, EC, 2 * C), F32),
            pltpu.VMEM((TR, TC, C), F32),
            pltpu.VMEM((TR, TC, C), F32),
            pltpu.VMEM((TR, TC, C), F32),
            pltpu.VMEM((TR, TC, C), F32),
            pltpu.VMEM((NB, NK, 256), BF),
            pltpu.VMEM((flat, C), BF),
            pltpu.VMEM((flat, C), BF),
            pltpu.VMEM((flat, C), BF),
            pltpu.VMEM((flat, FF), BF),
            pltpu.VMEM((flat, FF), BF),
            pltpu.VMEM((14, 256, 128), F32),
            pltpu.VMEM((2, FF, 128), F32),
            pltpu.VMEM((2, 64 * CHUNK, 128), F32),
            pltpu.VMEM((2, 80, C), F32),
            pltpu.VMEM((2, 80, 2 * C), F32),
        ],
        name="block_backward",
        **params(44),
    )(pos, tok, gout, intra, inter, first, second, scales, w_qkv, w_out, w_up, w_down)
    gr, gh, g_intra, g_inter, top, bottom, keep, send = outs

    inter = swap(g_inter, COL, 1)
    intra = swap(g_intra, COL, 0)
    got = lax.ppermute(send, "core", [(0, 1), (1, 0)])
    first, second, mine = pl.pallas_call(
        rim_kernel,
        out_shape=[sds((3 * TC, C), BF)] * 2 + [sds((64 * CHUNK, 128), BF)],
        in_specs=smem + vm(6),
        out_specs=vm(3),
        scratch_shapes=[pltpu.VMEM((2, 3 * TC, C), F32)],
        name="rims",
        **params(16),
    )(pos, top, bottom, intra, inter, keep, got)
    first = swap(first, ROW, 0)
    second = swap(second, ROW, 1)
    parts = lax.all_to_all(mine.reshape(64, CHUNK, 128), CHIPS, 0, 0, tiled=True)
    grad_tokens = pl.pallas_call(
        token_kernel,
        out_shape=sds((flat, C), BF),
        in_specs=smem + vm(8),
        out_specs=vm(1)[0],
        scratch_shapes=[pltpu.VMEM((flat, C), F32)],
        cost_estimate=pl.CostEstimate(
            flops=30 * flat * C, bytes_accessed=10 * flat * C, transcendentals=0
        ),
        name="grad_tokens",
        **params(16),
    )(pos, tok, gr, gh, intra, inter, first, second, scales)
    outs = pl.pallas_call(
        functools.partial(sum_kernel, loss_scale=1.0 / math.sqrt(rows_total * cols_total)),
        out_shape=[
            sds((2, 3 * C), F32),
            sds((2, C), F32),
            sds((2, FF), F32),
            sds((6, C), F32),
            sds((2, C), F32),
        ],
        in_specs=vm(1),
        out_specs=vm(5),
        name="weight_sums",
        **params(16),
    )(parts)
    return (grad_tokens.reshape(TR, TC, C),) + tuple(outs)


def solution(mesh):
    fine = Mesh(mesh.devices.reshape(4, 2, 4, 2, 2), ("x", "zh", "y", "zl", "core"))
    tile = P(ROW, COL, None)
    share = P(ROW + COL, None)
    return jax.shard_map(
        body,
        mesh=fine,
        in_specs=(tile, tile, P(), P(), P(), P(), P()),
        out_specs=(tile, share, share, share, share, P()),
        check_vma=False,
    )
```

time: 108 us -> 78.6 us (0.73)
  the two profiles are of different devices: /device:TPU:21 before, /device:TPU:1 now
where the time goes in v2:
time: 78.6 us; the launch traced here: 77.5 us
  starting transfers between devices  31.9 us (41%)
  Pallas kernels  21 us (27%)
  waiting for transfers between devices  19.6 us (25%)
  local copies, waits for them, and re-layouts  3.17 us (4%)
  other arithmetic  1.04 us (1%)
  between operations  0.8 us (1%)
    ppermute x8, waiting for transfers between devices, swap(): return lax.ppermute(x, axes, pairs + [(b, a) for a, b in pairs])  19.6 us
    ppermute x8, starting transfers between devices, swap(): return lax.ppermute(x, axes, pairs + [(b, a) for a, b in pairs])  18.3 us
    pallas_call x1, Pallas kernels, body(): pl.pallas_call(functools.partial(main_kernel, rows_total=rows_total, cols...  16.4 us
    all_to_all x1, starting transfers between devices, body(): lax.all_to_all(mine.reshape(64, CHUNK, 128), CHIPS, 0, 0, tiled=True)  12.8 us
    unnamed x14, local copies, waits for them, and re-layouts  2.01 us
    pallas_call x1, Pallas kernels, body(): pl.pallas_call(token_kernel, out_shape=sds((flat, C), BF), in_specs=smem...  1.98 us
    pallas_call x1, Pallas kernels, body(): pl.pallas_call(rim_kernel, out_shape=[sds((3 * TC, C), BF)] * 2 + [sds((6...  1.88 us
  transfers between devices with their start and end apart: 10, of which 4 were waited for; matrix products, arithmetic and copies ran while one was open for 1% of the time, Pallas kernels for 3%

profile of v2, /device:TPU:1, one launch (start us, length us, event | category | flops | bytes accessed | tf_op | source)
XLA Modules:
  0.0 77.5 jit_solution(7767366118481029908)
XLA Ops:
  0.6 0.9 %broadcast_select_fusion.4 = (bf16[16,3,256]{2,1,0:T(4,128)(2,1)S(1)}, bf16[16,3,256]{2,1,0:T(4,128)(2,1)S(1)}) fusion(pred[]{:T(512)S(6)} %eq.6, bf16[16,64,256]{2,1,0:T(8,128)(2,1)} %param.7), kind=kLoop, calls=%fused_computation.4 | loop fusion | flops 24576 | bytes 98305 | tf_op jit(solution)/shard_map/jit(_where)/select_n | solution.py:395
  1.6 4.9 %collective-permute-start.1 = (bf16[16,3,256]{2,1,0:T(4,128)(2,1)S(1)}, bf16[16,3,256]{2,1,0:T(4,128)(2,1)S(1)}, u32[]{:S(2)}, u32[]{:S(2)}) collective-permute-start(bf16[16,3,256]{2,1,0:T(4,128)(2,1)S(1)} %get-tuple-element.40), channel_id=1, source_target_pairs={{1,2},{3,4},{5,6},{7,8},{9,10},{11,12},{13,14},{2,1},{4,3},{6,5},{... | collective-permute-start | bytes 73736 | tf_op jit(solution)/shard_map/ppermute | solution.py:377
  6.5 0.1 collective-permute-start
  6.6 0.0 copy-start.2
  6.6 1.0 %fusion = (bf16[3,64,256]{2,1,0:T(8,128)(2,1)S(1)}, bf16[3,64,256]{2,1,0:T(8,128)(2,1)S(1)}) fusion(bf16[16,64,256]{2,1,0:T(8,128)(2,1)} %param.7), kind=kLoop, calls=%fused_computation.7 | loop fusion | bytes 393216 | tf_op jit(solution)/shard_map/slice | solution.py:404
  7.6 0.5 collective-permute-done.1.inter
  8.1 0.0 collective-permute-done.intra
  8.1 0.0 copy-start.1
  8.2 0.0 copy-start
  8.3 0.8 %collective-permute-start.3 = (bf16[224,256]{1,0:T(8,128)(2,1)S(1)}, bf16[224,256]{1,0:T(8,128)(2,1)S(1)}, u32[]{:S(2)}, u32[]{:S(2)}) collective-permute-start(bf16[224,256]{1,0:T(8,128)(2,1)S(1)} %get-tuple-element.42), channel_id=1, source_target_pairs={{16,32},{48,64},{80,96},{32,16},{64,48},{96,80},{17,33},{49,65},{8... | collective-permute-start | bytes 344072 | tf_op jit(solution)/shard_map/ppermute | solution.py:377
  9.2 5.2 %collective-permute-start.2 = (bf16[224,256]{1,0:T(8,128)(2,1)S(1)}, bf16[224,256]{1,0:T(8,128)(2,1)S(1)}, u32[]{:S(2)}, u32[]{:S(2)}) collective-permute-start(bf16[224,256]{1,0:T(8,128)(2,1)S(1)} %get-tuple-element.43), channel_id=1, source_target_pairs={{0,16},{32,48},{64,80},{96,112},{16,0},{48,32},{80,64},{112,96},{1... | collective-permute-start | bytes 344072 | tf_op jit(solution)/shard_map/ppermute | solution.py:377
  14.4 0.1 pad_add_fusion.pos
  14.4 0.0 collective-permute-done.3.second
  14.5 5.0 %collective-permute-done.2.first = bf16[224,256]{1,0:T(8,128)(2,1)S(1)} collective-permute-done((bf16[224,256]{1,0:T(8,128)(2,1)S(1)}, bf16[224,256]{1,0:T(8,128)(2,1)S(1)}, u32[]{:S(2)}, u32[]{:S(2)}) %collective-permute-start.2) | collective-permute-done | bytes 114720 | tf_op jit(solution)/shard_map/ppermute | solution.py:377
  19.5 0.0 copy-start.3
  19.5 1.0 %copy-done.3 = bf16[256,768]{1,0:T(8,128)(2,1)S(1)} copy-done((bf16[256,768]{1,0:T(8,128)(2,1)S(1)}, bf16[256,768]{1,0:T(8,128)(2,1)}, u32[]{:S(2)}) %copy-start.3) | copy-done | bytes 393240
  20.5 1.0 %copy-done.4 = bf16[768,256]{1,0:T(8,128)(2,1)S(1)} copy-done((bf16[768,256]{1,0:T(8,128)(2,1)S(1)}, bf16[768,256]{1,0:T(8,128)(2,1)}, u32[]{:S(2)}) %copy-start.4) | copy-done | bytes 393240
  21.5 16.4 %block_backward.1 = (bf16[1024,256]{1,0:T(8,128)(2,1)S(1)}, f32[1024,256]{1,0:T(8,128)S(1)}, bf16[80,256]{1,0:T(8,128)(2,1)S(1)}, bf16[80,256]{1,0:T(8,128)(2,1)...) custom-call(s32[4]{0:T(128)S(1)} %pad_add_fusion.pos, ...), custom_call_target="tpu_custom_call" | custom-call | tf_op jit(solution)/shard_map/block_backward/pallas_call | solution.py:417
  37.9 0.8 collective-permute-start.6
  38.7 0.1 collective-permute-start.4
  38.8 3.9 %collective-permute-start.5 = (bf16[80,256]{1,0:T(8,128)(2,1)S(1)}, bf16[80,256]{1,0:T(8,128)(2,1)S(1)}, u32[]{:S(2)}, u32[]{:S(2)}) collective-permute-start(bf16[80,256]{1,0:T(8,128)(2,1)S(1)} %get-tuple-element.25), channel_id=1, source_target_pairs={{1,2},{3,4},{5,6},{7,8},{9,10},{11,12},{13,14},{2,1},{4,3},{6,5},{... | collective-permute-start | bytes 122888 | tf_op jit(solution)/shard_map/ppermute | solution.py:377
  42.7 0.0 collective-permute-done.4.intra
  42.7 1.7 %collective-permute-done.5.inter = bf16[80,256]{1,0:T(8,128)(2,1)S(1)} collective-permute-done((bf16[80,256]{1,0:T(8,128)(2,1)S(1)}, bf16[80,256]{1,0:T(8,128)(2,1)S(1)}, u32[]{:S(2)}, u32[]{:S(2)}) %collective-permute-start.5) | collective-permute-done | bytes 40992 | tf_op jit(solution)/shard_map/ppermute | solution.py:377
  44.3 0.0 collective-permute-done.6.got
  44.4 1.9 %rims.1 = (bf16[192,256]{1,0:T(8,128)(2,1)S(1)}, bf16[192,256]{1,0:T(8,128)(2,1)S(1)}, bf16[3072,128]{1,0:T(8,128)(2,1)}) custom-call(s32[4]{0:T(128)S(1)} %pad_add_fusion.pos, f32[192,256]{1,0:T(8,128)S(1)} %get-tuple-element.26.top, f32[192,256]{1,0:T(8,128)S(1)} %get-tuple-element.27.bottom, bf16[80,256]{1,0:T(8,128)(2,1)S(1)} %collective-permute-done.4.intra, ...), custom_call_target="tpu_custom_call" | custom-call | tf_op jit(solution)/shard_map/rims/pallas_call | solution.py:459
  46.2 12.8 %all-to-all-start = ((bf16[64,48,128]{2,1,0:T(8,128)(2,1)}), bf16[64,48,128]{2,1,0:T(8,128)(2,1)S(1)}, u32[]{:S(2)}, u32[]{:S(2)}) async-start(bf16[64,48,128]{2,1,0:T(8,128)(2,1)} %bitcast.9), calls=%async_computation | async-start | bytes 1572864 | tf_op jit(solution)/shard_map/all_to_all | solution.py:470
  59.1 2.6 %collective-permute-start.7 = (bf16[192,256]{1,0:T(8,128)(2,1)S(1)}, bf16[192,256]{1,0:T(8,128)(2,1)S(1)}, u32[]{:S(2)}, u32[]{:S(2)}) collective-permute-start(bf16[192,256]{1,0:T(8,128)(2,1)S(1)} %get-tuple-element.30), channel_id=1, source_target_pairs={{0,16},{32,48},{64,80},{96,112},{16,0},{48,32},{80,64},{112,96},{1... | collective-permute-start | bytes 294920 | tf_op jit(solution)/shard_map/ppermute | solution.py:377
  61.7 0.7 collective-permute-start.8
  62.3 12.4 %collective-permute-done.7.first = bf16[192,256]{1,0:T(8,128)(2,1)S(1)} collective-permute-done((bf16[192,256]{1,0:T(8,128)(2,1)S(1)}, bf16[192,256]{1,0:T(8,128)(2,1)S(1)}, u32[]{:S(2)}, u32[]{:S(2)}) %collective-permute-start.7) | collective-permute-done | bytes 98336 | tf_op jit(solution)/shard_map/ppermute | solution.py:377
  74.7 0.0 collective-permute-done.8.second
  74.8 2.0 %grad_tokens.1 = bf16[1024,256]{1,0:T(8,128)(2,1)} custom-call(s32[4]{0:T(128)S(1)} %pad_add_fusion.pos, bf16[1024,256]{1,0:T(8,128)(2,1)S(1)} %bitcast.11, bf16[1024,256]{1,0:T(8,128)(2,1)S(1)} %get-tuple-element.22.gr, f32[1024,256]{1,0:T(8,128)S(1)} %get-tuple-element.23.gh, bf16[80,256]{1,0:T(8,128)(2,1)S(1)} %collective-permute-done.4.intra, ...), custom_call_target="tpu_custom_call" | custom-call | flops 7864320 | bytes 2621440 | tf_op jit(solution)/shard_map/grad_tokens/pallas_call | solution.py:471
  76.7 0.7 weight_sums.1
  (19 shorter events, 0.2 us)
Async XLA Ops:
  1.6 6.5 %collective-permute-start.1 = (bf16[16,3,256]{2,1,0:T(4,128)(2,1)S(1)}, bf16[16,3,256]{2,1,0:T(4,128)(2,1)S(1)}, u32[]{:S(2)}, u32[]{:S(2)}) collective-permute-start(bf16[16,3,256]{2,1,0:T(4,128)(2,1)S(1)} %get-tuple-element.40), channel_id=1, source_target_pairs={{1,2},{3,4},{5,6},{7,8},{9,10},{11,12},{13,14},{2,1},{4,3},{6,5},{... | collective-permute-start | bytes 73736 | tf_op jit(solution)/shard_map/ppermute | solution.py:377
  6.5 1.6 %collective-permute-start = (bf16[16,3,256]{2,1,0:T(4,128)(2,1)S(1)}, bf16[16,3,256]{2,1,0:T(4,128)(2,1)S(1)}, u32[]{:S(2)}, u32[]{:S(2)}) collective-permute-start(bf16[16,3,256]{2,1,0:T(4,128)(2,1)S(1)} %get-tuple-element.41), channel_id=1, source_target_pairs={{0,1},{2,3},{4,5},{6,7},{8,9},{10,11},{12,13},{14,15},{1,0},{3,2},... | collective-permute-start | bytes 73736 | tf_op jit(solution)/shard_map/ppermute | solution.py:377
  6.6 12.9 %copy-start.2 = (bf16[256,768]{1,0:T(8,128)(2,1)S(1)}, bf16[256,768]{1,0:T(8,128)(2,1)}, u32[]{:S(2)}) copy-start(bf16[256,768]{1,0:T(8,128)(2,1)} %w_qkv.1) | copy-start | bytes 1179652
  8.1 11.4 %copy-start.5 = (bf16[256,256]{1,0:T(8,128)(2,1)S(1)}, bf16[256,256]{1,0:T(8,128)(2,1)}, u32[]{:S(2)}) copy-start(bf16[256,256]{1,0:T(8,128)(2,1)} %w_out.1) | copy-start | bytes 393220
  8.1 11.4 %copy-start.1 = (bf16[16,64,256]{2,1,0:T(8,128)(2,1)S(1)}, bf16[16,64,256]{2,1,0:T(8,128)(2,1)}, u32[]{:S(2)}) copy-start(bf16[16,64,256]{2,1,0:T(8,128)(2,1)} %param.8) | copy-start | bytes 1572868
  8.2 11.3 %copy-start = (bf16[16,64,256]{2,1,0:T(8,128)(2,1)S(1)}, bf16[16,64,256]{2,1,0:T(8,128)(2,1)}, u32[]{:S(2)}) copy-start(bf16[16,64,256]{2,1,0:T(8,128)(2,1)} %param.7) | copy-start | bytes 1572868
  8.3 6.1 %collective-permute-start.3 = (bf16[224,256]{1,0:T(8,128)(2,1)S(1)}, bf16[224,256]{1,0:T(8,128)(2,1)S(1)}, u32[]{:S(2)}, u32[]{:S(2)}) collective-permute-start(bf16[224,256]{1,0:T(8,128)(2,1)S(1)} %get-tuple-element.42), channel_id=1, source_target_pairs={{16,32},{48,64},{80,96},{32,16},{64,48},{96,80},{17,33},{49,65},{8... | collective-permute-start | bytes 344072 | tf_op jit(solution)/shard_map/ppermute | solution.py:377
  9.2 10.3 %collective-permute-start.2 = (bf16[224,256]{1,0:T(8,128)(2,1)S(1)}, bf16[224,256]{1,0:T(8,128)(2,1)S(1)}, u32[]{:S(2)}, u32[]{:S(2)}) collective-permute-start(bf16[224,256]{1,0:T(8,128)(2,1)S(1)} %get-tuple-element.43), channel_id=1, source_target_pairs={{0,16},{32,48},{64,80},{96,112},{16,0},{48,32},{80,64},{112,96},{1... | collective-permute-start | bytes 344072 | tf_op jit(solution)/shard_map/ppermute | solution.py:377
  14.4 5.1 %copy-start.6 = (f32[2,256]{1,0:T(2,128)S(1)}, f32[2,256]{1,0:T(2,128)}, u32[]{:S(2)}) copy-start(f32[2,256]{1,0:T(2,128)} %scales.3) | copy-start | bytes 6148
  19.5 1.0 %copy-start.3 = (bf16[256,768]{1,0:T(8,128)(2,1)S(1)}, bf16[256,768]{1,0:T(8,128)(2,1)}, u32[]{:S(2)}) copy-start(bf16[256,768]{1,0:T(8,128)(2,1)} %w_up.1) | copy-start | bytes 1179652
  20.5 1.0 %copy-start.4 = (bf16[768,256]{1,0:T(8,128)(2,1)S(1)}, bf16[768,256]{1,0:T(8,128)(2,1)}, u32[]{:S(2)}) copy-start(bf16[768,256]{1,0:T(8,128)(2,1)} %w_down.1) | copy-start | bytes 1179652
  37.9 6.4 %collective-permute-start.6 = (bf16[3072,128]{1,0:T(8,128)(2,1)S(1)}, bf16[3072,128]{1,0:T(8,128)(2,1)S(1)}, u32[]{:S(2)}, u32[]{:S(2)}) collective-permute-start(bf16[3072,128]{1,0:T(8,128)(2,1)S(1)} %get-tuple-element.29), channel_id=1, source_target_pairs={{0,1},{1,0},{2,3},{3,2},{4,5},{5,4},{6,7},{7,6},{8,9},{9,8},{10,11... | collective-permute-start | bytes 2359304 | tf_op jit(solution)/shard_map/ppermute | solution.py:458
  38.7 4.0 %collective-permute-start.4 = (bf16[80,256]{1,0:T(8,128)(2,1)S(1)}, bf16[80,256]{1,0:T(8,128)(2,1)S(1)}, u32[]{:S(2)}, u32[]{:S(2)}) collective-permute-start(bf16[80,256]{1,0:T(8,128)(2,1)S(1)} %get-tuple-element.24), channel_id=1, source_target_pairs={{0,1},{2,3},{4,5},{6,7},{8,9},{10,11},{12,13},{14,15},{1,0},{3,2},... | collective-permute-start | bytes 122888 | tf_op jit(solution)/shard_map/ppermute | solution.py:377
  38.8 5.6 %collective-permute-start.5 = (bf16[80,256]{1,0:T(8,128)(2,1)S(1)}, bf16[80,256]{1,0:T(8,128)(2,1)S(1)}, u32[]{:S(2)}, u32[]{:S(2)}) collective-permute-start(bf16[80,256]{1,0:T(8,128)(2,1)S(1)} %get-tuple-element.25), channel_id=1, source_target_pairs={{1,2},{3,4},{5,6},{7,8},{9,10},{11,12},{13,14},{2,1},{4,3},{6,5},{... | collective-permute-start | bytes 122888 | tf_op jit(solution)/shard_map/ppermute | solution.py:377
  46.2 30.5 %all-to-all-start = ((bf16[64,48,128]{2,1,0:T(8,128)(2,1)}), bf16[64,48,128]{2,1,0:T(8,128)(2,1)S(1)}, u32[]{:S(2)}, u32[]{:S(2)}) async-start(bf16[64,48,128]{2,1,0:T(8,128)(2,1)} %bitcast.9), calls=%async_computation | async-start | bytes 1572864 | tf_op jit(solution)/shard_map/all_to_all | solution.py:470
  59.1 15.7 %collective-permute-start.7 = (bf16[192,256]{1,0:T(8,128)(2,1)S(1)}, bf16[192,256]{1,0:T(8,128)(2,1)S(1)}, u32[]{:S(2)}, u32[]{:S(2)}) collective-permute-start(bf16[192,256]{1,0:T(8,128)(2,1)S(1)} %get-tuple-element.30), channel_id=1, source_target_pairs={{0,16},{32,48},{64,80},{96,112},{16,0},{48,32},{80,64},{112,96},{1... | collective-permute-start | bytes 294920 | tf_op jit(solution)/shard_map/ppermute | solution.py:377
  61.7 13.1 %collective-permute-start.8 = (bf16[192,256]{1,0:T(8,128)(2,1)S(1)}, bf16[192,256]{1,0:T(8,128)(2,1)S(1)}, u32[]{:S(2)}, u32[]{:S(2)}) collective-permute-start(bf16[192,256]{1,0:T(8,128)(2,1)S(1)} %get-tuple-element.31), channel_id=1, source_target_pairs={{16,32},{48,64},{80,96},{32,16},{64,48},{96,80},{17,33},{49,65},{8... | collective-permute-start | bytes 294920 | tf_op jit(solution)/shard_map/ppermute | solution.py:377

commit v3 on v2

--- a/solution.py
+++ b/solution.py
@@ -71,16 +71,14 @@
     first,
     second,
     scales,
-    w_qkv,
-    w_out,
-    w_up,
-    w_down,
+    w_wide,
+    w_tall,
     o_gr,
     o_gh,
     o_intra,
     o_inter,
-    o_top,
-    o_bottom,
+    o_first,
+    o_second,
     o_keep,
     o_send,
     bias,
@@ -108,6 +106,8 @@
     base_r, base_c, core, half_row = pos[0], pos[1], pos[2], pos[3]
     even = core == 0
     masks = head_masks()
+    w_qkv, w_up = w_wide.at[0:C], w_wide.at[C : 2 * C]
+    w_out, w_down = w_tall.at[0:C], w_tall.at[C : C + FF]
 
     key = lax.broadcasted_iota(jnp.int32, (NK, 1), 0)
     lane = jnp.bitwise_and(lax.broadcasted_iota(jnp.int32, (1, 256), 1), 63)
@@ -249,8 +249,10 @@
     g_right = nt(right, w_qkv[:, C:])
     o_intra[...] = jnp.where(even, g_right, g_left).astype(BF)
     o_inter[...] = jnp.where(even, g_left, g_right).astype(BF)
-    o_top[...] = nt(top, w_qkv[:, C:])
-    o_bottom[...] = nt(bottom, w_qkv[:, C:])
+    g_top = nt(top, w_qkv[:, C:])
+    g_bottom = nt(bottom, w_qkv[:, C:])
+    o_first[...] = jnp.where(upper, g_bottom, g_top).astype(BF)
+    o_second[...] = jnp.where(upper, g_top, g_bottom).astype(BF)
 
     gq = jnp.zeros((C, C), F32)
     gkv = tn(h_above, top) + tn(h_below, bottom) + tn(h_side[0], left) + tn(h_side[1], right)
@@ -291,42 +293,49 @@
     o_send[...] = pk[1 - core].astype(BF)
 
 
-def rim_kernel(
-    pos, top, bottom, intra, inter, keep, got, o_first, o_second, o_mine, work
-):
+def add_kernel(keep, got, o_mine):
+    o_mine[...] = (keep[...].astype(F32) + got[...].astype(F32)).astype(BF)
+
+
+def sides_of(pos, intra, inter):
     even = pos[2] == 0
-    upper = pos[3] == 0
     near = intra[...].astype(F32)
     far = inter[...].astype(F32)
-    left = jnp.where(even, far, near)
-    right = jnp.where(even, near, far)
-    for n, (src, at) in enumerate(((top, 0), (bottom, TR + 3))):
-        work[n] = src[...]
-        for r in range(3):
-            k = 3 * (at + r)
-            work[n, r * TC : r * TC + 3, :] += left[k : k + 3, :]
-            work[n, r * TC + TC - 3 : r * TC + TC, :] += right[k : k + 3, :]
+    return jnp.where(even, far, near), jnp.where(even, near, far)
+
+
+def corner_kernel(pos, intra, inter, _first, _second, o_first, o_second, work):
+    upper = pos[3] == 0
+    work[...] = jnp.zeros_like(work)
+    for k, x in enumerate(sides_of(pos, intra, inter)):
+        work[0, 16 * k : 16 * k + 9, :] = x[0:9]
+        work[1, 16 * k : 16 * k + 9, :] = x[3 * (TR + 3) : 3 * ER]
     o_first[...] = jnp.where(upper, work[1], work[0]).astype(BF)
     o_second[...] = jnp.where(upper, work[0], work[1]).astype(BF)
-    o_mine[...] = (keep[...].astype(F32) + got[...].astype(F32)).astype(BF)
-
-
-def token_kernel(pos, tok, gr, gh, intra, inter, first, second, scales, o_tok, work):
-    even = pos[2] == 0
+
+
+def token_kernel(
+    pos, tok, gr, gh, intra, inter, first, second, c_first, c_second, scales, o_tok, work
+):
     upper = pos[3] == 0
-    near = intra[...].astype(F32)
-    far = inter[...].astype(F32)
-    left = jnp.where(even, far, near)
-    right = jnp.where(even, near, far)
+    left, right = sides_of(pos, intra, inter)
     work[...] = gh[...]
     one = first[...].astype(F32)
     two = second[...].astype(F32)
     work[0 : 3 * TC, :] += jnp.where(upper, two, one)
     work[(TR - 3) * TC :, :] += jnp.where(upper, one, two)
+    one = c_first[...].astype(F32)
+    two = c_second[...].astype(F32)
+    corners = jnp.where(upper, two, one), jnp.where(upper, one, two)
     for r in range(TR):
         k = 3 * (r + 3)
-        work[r * TC : r * TC + 3, :] += left[k : k + 3, :]
-        work[r * TC + TC - 3 : r * TC + TC, :] += right[k : k + 3, :]
+        add_left, add_right = left[k : k + 3, :], right[k : k + 3, :]
+        if r < 3 or r >= TR - 3:
+            n, j = (0, 3 * r) if r < 3 else (1, 3 * (r - TR + 3))
+            add_left = add_left + corners[n][j : j + 3, :]
+            add_right = add_right + corners[n][16 + j : 19 + j, :]
+        work[r * TC : r * TC + 3, :] += add_left
+        work[r * TC + TC - 3 : r * TC + TC, :] += add_right
     s0 = scales[0:1, :]
     for i in range(4):
         at = slice(256 * i, 256 * i + 256)
@@ -411,6 +420,9 @@
         )
 
     top, bottom = rim(0), rim(TR - 3)
+    top, bottom, w_up, w_down = lax.optimization_barrier((top, bottom, w_up, w_down))
+    w_wide = jnp.concatenate([w_qkv, w_up], axis=0)
+    w_tall = jnp.concatenate([w_out, w_down], axis=0)
     first = swap(jnp.where(upper, bottom, top), ROW, 0)
     second = swap(jnp.where(upper, top, bottom), ROW, 1)
 
@@ -421,12 +433,12 @@
             sds((flat, C), F32),
             sds((80, C), BF),
             sds((80, C), BF),
-            sds((3 * TC, C), F32),
-            sds((3 * TC, C), F32),
+            sds((3 * TC, C), BF),
+            sds((3 * TC, C), BF),
             sds((64 * CHUNK, 128), BF),
             sds((64 * CHUNK, 128), BF),
         ],
-        in_specs=smem + vm(11),
+        in_specs=smem + vm(9),
         out_specs=vm(8),
         scratch_shapes=[
             pltpu.VMEM((6, NK, 256), F32),
@@ -450,28 +462,41 @@
         ],
         name="block_backward",
         **params(44),
-    )(pos, tok, gout, intra, inter, first, second, scales, w_qkv, w_out, w_up, w_down)
-    gr, gh, g_intra, g_inter, top, bottom, keep, send = outs
-
-    inter = swap(g_inter, COL, 1)
-    intra = swap(g_intra, COL, 0)
+    )(pos, tok, gout, intra, inter, first, second, scales, w_wide, w_tall)
+    gr, gh, intra, inter, first, second, keep, send = outs
+
+    inter = swap(inter, COL, 1)
+    intra = swap(intra, COL, 0)
     got = lax.ppermute(send, "core", [(0, 1), (1, 0)])
-    first, second, mine = pl.pallas_call(
-        rim_kernel,
-        out_shape=[sds((3 * TC, C), BF)] * 2 + [sds((64 * CHUNK, 128), BF)],
-        in_specs=smem + vm(6),
-        out_specs=vm(3),
-        scratch_shapes=[pltpu.VMEM((2, 3 * TC, C), F32)],
-        name="rims",
-        **params(16),
-    )(pos, top, bottom, intra, inter, keep, got)
     first = swap(first, ROW, 0)
     second = swap(second, ROW, 1)
+    mine = pl.pallas_call(
+        add_kernel,
+        out_shape=sds((64 * CHUNK, 128), BF),
+        in_specs=vm(2),
+        out_specs=vm(1)[0],
+        name="add_core",
+        **params(16),
+    )(keep, got)
     parts = lax.all_to_all(mine.reshape(64, CHUNK, 128), CHIPS, 0, 0, tiled=True)
+    c_first, c_second = pl.pallas_call(
+        corner_kernel,
+        out_shape=[sds((32, C), BF)] * 2,
+        in_specs=smem + vm(2) + [pl.BlockSpec(memory_space=pl.ANY)] * 2,
+        out_specs=vm(2),
+        scratch_shapes=[pltpu.VMEM((2, 32, C), F32)],
+        cost_estimate=pl.CostEstimate(
+            flops=100 * 10**9, bytes_accessed=4 * 80 * C, transcendentals=0
+        ),
+        name="corners",
+        **params(16),
+    )(pos, intra, inter, first, second)
+    c_first = swap(c_first, ROW, 0)
+    c_second = swap(c_second, ROW, 1)
     grad_tokens = pl.pallas_call(
         token_kernel,
         out_shape=sds((flat, C), BF),
-        in_specs=smem + vm(8),
+        in_specs=smem + vm(10),
         out_specs=vm(1)[0],
         scratch_shapes=[pltpu.VMEM((flat, C), F32)],
         cost_estimate=pl.CostEstimate(
@@ -479,7 +504,8 @@
         ),
         name="grad_tokens",
         **params(16),
-    )(pos, tok, gr, gh, intra, inter, first, second, scales)
+    )(pos, tok, gr, gh, intra, inter, first, second, c_first, c_second, scales)
+    parts, grad_tokens = lax.optimization_barrier((parts, grad_tokens))
     outs = pl.pallas_call(
         functools.partial(sum_kernel, loss_scale=1.0 / math.sqrt(rows_total * cols_total)),
         out_shape=[

time: 78.6 us -> 75.1 us (0.955)
  waiting for transfers between devices: 19.6 us -> 14.8 us
  starting transfers between devices: 31.9 us -> 35.2 us
  local copies, waits for them, and re-layouts: 3.17 us -> 1.15 us
    ppermute x8 -> x10, waiting for transfers between devices: 19.6 us -> 7.07 us  [swap(): return lax.ppermute(x, axes, pairs + [(b, a) for a, b in pairs])]
    all_to_all x1, waiting for transfers between devices: 0.01 us -> 7.75 us  [body(): lax.all_to_all(mine.reshape(64, CHUNK, 128), CHIPS, 0, 0, tiled=True)]
    ppermute x8 -> x10, starting transfers between devices: 18.3 us -> 22.7 us  [swap(): return lax.ppermute(x, axes, pairs + [(b, a) for a, b in pairs])]
    unnamed x14, local copies, waits for them, and re-layouts: 2.01 us -> 0.04 us
    all_to_all x1, starting transfers between devices: 12.8 us -> 11.8 us  [body(): lax.all_to_all(mine.reshape(64, CHUNK, 128), CHIPS, 0, 0, tiled=True)]
    pallas_call x1 -> x2, Pallas kernels: 1.88 us -> 1.63 us  [the longest x1 1.07 us: body(): pl.pallas_call(add_kernel, out_shape=sds((64 * CHUNK, 128), BF), in_specs...]
  transfers between devices with their start and end apart: 10 -> 12, of which waited for: 4 -> 4; matrix products, arithmetic and copies ran while one was open for 1% -> 2% of each run, Pallas kernels for 3% -> 5%
where the time goes in v3:
time: 75.1 us; the launch traced here: 74.2 us
  starting transfers between devices  35.2 us (47%)
  Pallas kernels  20.9 us (28%)
  waiting for transfers between devices  14.8 us (20%)
  other arithmetic  1.2 us (2%)
  local copies, waits for them, and re-layouts  1.15 us (2%)
  between operations  0.89 us (1%)
    ppermute x10, starting transfers between devices, swap(): return lax.ppermute(x, axes, pairs + [(b, a) for a, b in pairs])  22.7 us
    pallas_call x1, Pallas kernels, body(): pl.pallas_call(functools.partial(main_kernel, rows_total=rows_total, cols...  16.6 us
    all_to_all x1, starting transfers between devices, body(): lax.all_to_all(mine.reshape(64, CHUNK, 128), CHIPS, 0, 0, tiled=True)  11.8 us
    all_to_all x1, waiting for transfers between devices, body(): lax.all_to_all(mine.reshape(64, CHUNK, 128), CHIPS, 0, 0, tiled=True)  7.75 us
    ppermute x10, waiting for transfers between devices, swap(): return lax.ppermute(x, axes, pairs + [(b, a) for a, b in pairs])  7.07 us
    pallas_call x1, Pallas kernels, body(): pl.pallas_call(token_kernel, out_shape=sds((flat, C), BF), in_specs=smem...  1.98 us
  transfers between devices with their start and end apart: 12, of which 4 were waited for; matrix products, arithmetic and copies ran while one was open for 2% of the time, Pallas kernels for 5%

profile of v3, /device:TPU:1, one launch (start us, length us, event | category | flops | bytes accessed | tf_op | source)
XLA Modules:
  0.0 74.2 jit_solution(8858851929210728006)
XLA Ops:
  0.7 1.0 %broadcast_select_fusion.4 = (bf16[16,3,256]{2,1,0:T(4,128)(2,1)S(1)}, bf16[16,3,256]{2,1,0:T(4,128)(2,1)S(1)}) fusion(pred[]{:T(512)S(6)} %eq.6, bf16[16,64,256]{2,1,0:T(8,128)(2,1)} %param.7), kind=kLoop, calls=%fused_computation.6 | loop fusion | flops 24576 | bytes 98305 | tf_op jit(solution)/shard_map/jit(_where)/select_n | solution.py:404
  1.6 4.9 %collective-permute-start.1 = (bf16[16,3,256]{2,1,0:T(4,128)(2,1)S(1)}, bf16[16,3,256]{2,1,0:T(4,128)(2,1)S(1)}, u32[]{:S(2)}, u32[]{:S(2)}) collective-permute-start(bf16[16,3,256]{2,1,0:T(4,128)(2,1)S(1)} %get-tuple-element.50), channel_id=1, source_target_pairs={{1,2},{3,4},{5,6},{7,8},{9,10},{11,12},{13,14},{2,1},{4,3},{6,5},{... | collective-permute-start | bytes 73736 | tf_op jit(solution)/shard_map/ppermute | solution.py:386
  6.6 0.1 collective-permute-start
  6.7 1.0 %fusion = (bf16[3,64,256]{2,1,0:T(8,128)(2,1)S(1)}, bf16[3,64,256]{2,1,0:T(8,128)(2,1)S(1)}) fusion(bf16[16,64,256]{2,1,0:T(8,128)(2,1)} %param.7), kind=kLoop, calls=%fused_computation.9 | loop fusion | bytes 393216 | tf_op jit(solution)/shard_map/slice | solution.py:413
  7.7 0.1 pad_add_fusion.pos
  7.7 0.4 collective-permute-done.1.inter
  8.2 0.0 collective-permute-done.intra
  8.4 0.0 copy-start.6
  8.4 0.8 %collective-permute-start.3 = (bf16[224,256]{1,0:T(8,128)(2,1)S(1)}, bf16[224,256]{1,0:T(8,128)(2,1)S(1)}, u32[]{:S(2)}, u32[]{:S(2)}) collective-permute-start(bf16[224,256]{1,0:T(8,128)(2,1)S(1)} %get-tuple-element.52), channel_id=1, source_target_pairs={{16,32},{48,64},{80,96},{32,16},{64,48},{96,80},{17,33},{49,65},{8... | collective-permute-start | bytes 344072 | tf_op jit(solution)/shard_map/ppermute | solution.py:386
  9.2 0.0 copy-start
  9.2 0.0 copy-start.1
  9.3 0.0 copy-start.2
  9.3 5.2 %collective-permute-start.2 = (bf16[224,256]{1,0:T(8,128)(2,1)S(1)}, bf16[224,256]{1,0:T(8,128)(2,1)S(1)}, u32[]{:S(2)}, u32[]{:S(2)}) collective-permute-start(bf16[224,256]{1,0:T(8,128)(2,1)S(1)} %get-tuple-element.53), channel_id=1, source_target_pairs={{0,16},{32,48},{64,80},{96,112},{16,0},{48,32},{80,64},{112,96},{1... | collective-permute-start | bytes 344072 | tf_op jit(solution)/shard_map/ppermute | solution.py:386
  14.5 0.1 pad_maximum_fusion.w_wide
  14.6 0.0 collective-permute-done.3.second
  14.6 5.0 %collective-permute-done.2.first = bf16[224,256]{1,0:T(8,128)(2,1)S(1)} collective-permute-done((bf16[224,256]{1,0:T(8,128)(2,1)S(1)}, bf16[224,256]{1,0:T(8,128)(2,1)S(1)}, u32[]{:S(2)}, u32[]{:S(2)}) %collective-permute-start.2) | collective-permute-done | bytes 114720 | tf_op jit(solution)/shard_map/ppermute | solution.py:386
  19.7 16.6 %block_backward.1 = (bf16[1024,256]{1,0:T(8,128)(2,1)S(1)}, f32[1024,256]{1,0:T(8,128)S(1)}, bf16[80,256]{1,0:T(8,128)(2,1)S(1)}, bf16[80,256]{1,0:T(8,128)(2,1)...) custom-call(s32[4]{0:T(128)S(1)} %pad_add_fusion.pos, ...), custom_call_target="tpu_custom_call" | custom-call | tf_op jit(solution)/shard_map/block_backward/pallas_call | solution.py:429
  36.2 0.7 collective-permute-start.4
  37.0 3.7 %collective-permute-start.7 = (bf16[192,256]{1,0:T(8,128)(2,1)S(1)}, bf16[192,256]{1,0:T(8,128)(2,1)S(1)}, u32[]{:S(2)}, u32[]{:S(2)}) collective-permute-start(bf16[192,256]{1,0:T(8,128)(2,1)S(1)} %get-tuple-element.37), channel_id=1, source_target_pairs={{0,16},{32,48},{64,80},{96,112},{16,0},{48,32},{80,64},{112,96},{1... | collective-permute-start | bytes 294920 | tf_op jit(solution)/shard_map/ppermute | solution.py:386
  40.7 0.7 collective-permute-start.8
  41.4 0.4 collective-permute-start.5
  41.8 3.6 %collective-permute-start.6 = (bf16[80,256]{1,0:T(8,128)(2,1)S(1)}, bf16[80,256]{1,0:T(8,128)(2,1)S(1)}, u32[]{:S(2)}, u32[]{:S(2)}) collective-permute-start(bf16[80,256]{1,0:T(8,128)(2,1)S(1)} %get-tuple-element.36), channel_id=1, source_target_pairs={{1,2},{3,4},{5,6},{7,8},{9,10},{11,12},{13,14},{2,1},{4,3},{6,5},{... | collective-permute-start | bytes 122888 | tf_op jit(solution)/shard_map/ppermute | solution.py:386
  45.4 0.0 collective-permute-done.4.got
  45.4 1.1 %add_core.1 = bf16[3072,128]{1,0:T(8,128)(2,1)} custom-call(bf16[3072,128]{1,0:T(8,128)(2,1)S(1)} %get-tuple-element.31.keep, bf16[3072,128]{1,0:T(8,128)(2,1)S(1)} %collective-permute-done.4.got), custom_call_target="tpu_custom_call" | custom-call | tf_op jit(solution)/shard_map/add_core/pallas_call | solution.py:473
  46.5 11.8 %all-to-all-start = ((bf16[64,48,128]{2,1,0:T(8,128)(2,1)}), bf16[64,48,128]{2,1,0:T(8,128)(2,1)S(1)}, u32[]{:S(2)}, u32[]{:S(2)}) async-start(bf16[64,48,128]{2,1,0:T(8,128)(2,1)} %bitcast.8), calls=%async_computation | async-start | bytes 1572864 | tf_op jit(solution)/shard_map/all_to_all | solution.py:481
  58.3 0.6 corners.1
  58.8 2.6 %collective-permute-start.9 = (bf16[32,256]{1,0:T(8,128)(2,1)S(1)}, bf16[32,256]{1,0:T(8,128)(2,1)S(1)}, u32[]{:S(2)}, u32[]{:S(2)}) collective-permute-start(bf16[32,256]{1,0:T(8,128)(2,1)S(1)} %get-tuple-element.39), channel_id=1, source_target_pairs={{0,16},{32,48},{64,80},{96,112},{16,0},{48,32},{80,64},{112,96},{1... | collective-permute-start | bytes 49160 | tf_op jit(solution)/shard_map/ppermute | solution.py:386
  61.4 0.7 collective-permute-start.10
  62.1 1.6 %collective-permute-done.9.c_first = bf16[32,256]{1,0:T(8,128)(2,1)S(1)} collective-permute-done((bf16[32,256]{1,0:T(8,128)(2,1)S(1)}, bf16[32,256]{1,0:T(8,128)(2,1)S(1)}, u32[]{:S(2)}, u32[]{:S(2)}) %collective-permute-start.9) | collective-permute-done | bytes 16416 | tf_op jit(solution)/shard_map/ppermute | solution.py:386
  63.7 2.0 %grad_tokens.1 = bf16[1024,256]{1,0:T(8,128)(2,1)} custom-call(s32[4]{0:T(128)S(1)} %pad_add_fusion.pos, bf16[1024,256]{1,0:T(8,128)(2,1)S(1)} %bitcast.11, bf16[1024,256]{1,0:T(8,128)(2,1)S(1)} %get-tuple-element.33.gr, f32[1024,256]{1,0:T(8,128)S(1)} %get-tuple-element.34.gh, bf16[80,256]{1,0:T(8,128)(2,1)S(1)} %collective-permute-done.5.intra, ...), custom_call_target="tpu_custom_call" | custom-call | flops 7864320 | bytes 2621440 | tf_op jit(solution)/shard_map/grad_tokens/pallas_call | solution.py:496
  65.7 7.8 %all-to-all-done.parts = bf16[64,48,128]{2,1,0:T(8,128)(2,1)S(1)} async-done(((bf16[64,48,128]{2,1,0:T(8,128)(2,1)}), bf16[64,48,128]{2,1,0:T(8,128)(2,1)S(1)}, u32[]{:S(2)}, u32[]{:S(2)}) %all-to-all-start) | async-done | bytes 786464 | tf_op jit(solution)/shard_map/all_to_all | solution.py:481
  73.4 0.7 weight_sums.1
  (26 shorter events, 0.3 us)
Async XLA Ops:
  0.6 13.9 %copy-start.3 = (bf16[256,768]{1,0:T(8,128)(2,1)S(1)}, bf16[256,768]{1,0:T(8,128)(2,1)}, u32[]{:S(2)}) copy-start(bf16[256,768]{1,0:T(8,128)(2,1)} %param.12) | copy-start | bytes 1179652
  0.6 13.9 %copy-start.4 = (bf16[256,768]{1,0:T(8,128)(2,1)S(1)}, bf16[256,768]{1,0:T(8,128)(2,1)}, u32[]{:S(2)}) copy-start(bf16[256,768]{1,0:T(8,128)(2,1)} %param.10) | copy-start | bytes 1179652
  1.6 6.5 %collective-permute-start.1 = (bf16[16,3,256]{2,1,0:T(4,128)(2,1)S(1)}, bf16[16,3,256]{2,1,0:T(4,128)(2,1)S(1)}, u32[]{:S(2)}, u32[]{:S(2)}) collective-permute-start(bf16[16,3,256]{2,1,0:T(4,128)(2,1)S(1)} %get-tuple-element.50), channel_id=1, source_target_pairs={{1,2},{3,4},{5,6},{7,8},{9,10},{11,12},{13,14},{2,1},{4,3},{6,5},{... | collective-permute-start | bytes 73736 | tf_op jit(solution)/shard_map/ppermute | solution.py:386
  6.6 1.6 %collective-permute-start = (bf16[16,3,256]{2,1,0:T(4,128)(2,1)S(1)}, bf16[16,3,256]{2,1,0:T(4,128)(2,1)S(1)}, u32[]{:S(2)}, u32[]{:S(2)}) collective-permute-start(bf16[16,3,256]{2,1,0:T(4,128)(2,1)S(1)} %get-tuple-element.51), channel_id=1, source_target_pairs={{0,1},{2,3},{4,5},{6,7},{8,9},{10,11},{12,13},{14,15},{1,0},{3,2},... | collective-permute-start | bytes 73736 | tf_op jit(solution)/shard_map/ppermute | solution.py:386
  8.4 6.2 %copy-start.5 = (bf16[768,256]{1,0:T(8,128)(2,1)S(1)}, bf16[768,256]{1,0:T(8,128)(2,1)}, u32[]{:S(2)}) copy-start(bf16[768,256]{1,0:T(8,128)(2,1)} %param.13) | copy-start | bytes 1179652
  8.4 6.2 %copy-start.6 = (bf16[256,256]{1,0:T(8,128)(2,1)S(1)}, bf16[256,256]{1,0:T(8,128)(2,1)}, u32[]{:S(2)}) copy-start(bf16[256,256]{1,0:T(8,128)(2,1)} %param.11) | copy-start | bytes 393220
  8.4 6.2 %collective-permute-start.3 = (bf16[224,256]{1,0:T(8,128)(2,1)S(1)}, bf16[224,256]{1,0:T(8,128)(2,1)S(1)}, u32[]{:S(2)}, u32[]{:S(2)}) collective-permute-start(bf16[224,256]{1,0:T(8,128)(2,1)S(1)} %get-tuple-element.52), channel_id=1, source_target_pairs={{16,32},{48,64},{80,96},{32,16},{64,48},{96,80},{17,33},{49,65},{8... | collective-permute-start | bytes 344072 | tf_op jit(solution)/shard_map/ppermute | solution.py:386
  9.2 10.4 %copy-start = (bf16[16,64,256]{2,1,0:T(8,128)(2,1)S(1)}, bf16[16,64,256]{2,1,0:T(8,128)(2,1)}, u32[]{:S(2)}) copy-start(bf16[16,64,256]{2,1,0:T(8,128)(2,1)} %param.7) | copy-start | bytes 1572868
  9.2 10.4 %copy-start.1 = (bf16[16,64,256]{2,1,0:T(8,128)(2,1)S(1)}, bf16[16,64,256]{2,1,0:T(8,128)(2,1)}, u32[]{:S(2)}) copy-start(bf16[16,64,256]{2,1,0:T(8,128)(2,1)} %param.8) | copy-start | bytes 1572868
  9.3 10.4 %copy-start.2 = (f32[2,256]{1,0:T(2,128)S(1)}, f32[2,256]{1,0:T(2,128)}, u32[]{:S(2)}) copy-start(f32[2,256]{1,0:T(2,128)} %scales.3) | copy-start | bytes 6148
  9.3 10.4 %collective-permute-start.2 = (bf16[224,256]{1,0:T(8,128)(2,1)S(1)}, bf16[224,256]{1,0:T(8,128)(2,1)S(1)}, u32[]{:S(2)}, u32[]{:S(2)}) collective-permute-start(bf16[224,256]{1,0:T(8,128)(2,1)S(1)} %get-tuple-element.53), channel_id=1, source_target_pairs={{0,16},{32,48},{64,80},{96,112},{16,0},{48,32},{80,64},{112,96},{1... | collective-permute-start | bytes 344072 | tf_op jit(solution)/shard_map/ppermute | solution.py:386
  36.2 9.1 %collective-permute-start.4 = (bf16[3072,128]{1,0:T(8,128)(2,1)S(1)}, bf16[3072,128]{1,0:T(8,128)(2,1)S(1)}, u32[]{:S(2)}, u32[]{:S(2)}) collective-permute-start(bf16[3072,128]{1,0:T(8,128)(2,1)S(1)} %get-tuple-element.32), channel_id=1, source_target_pairs={{0,1},{1,0},{2,3},{3,2},{4,5},{5,4},{6,7},{7,6},{8,9},{9,8},{10,11... | collective-permute-start | bytes 2359304 | tf_op jit(solution)/shard_map/ppermute | solution.py:470
  37.0 21.3 %collective-permute-start.7 = (bf16[192,256]{1,0:T(8,128)(2,1)S(1)}, bf16[192,256]{1,0:T(8,128)(2,1)S(1)}, u32[]{:S(2)}, u32[]{:S(2)}) collective-permute-start(bf16[192,256]{1,0:T(8,128)(2,1)S(1)} %get-tuple-element.37), channel_id=1, source_target_pairs={{0,16},{32,48},{64,80},{96,112},{16,0},{48,32},{80,64},{112,96},{1... | collective-permute-start | bytes 294920 | tf_op jit(solution)/shard_map/ppermute | solution.py:386
  40.7 17.5 %collective-permute-start.8 = (bf16[192,256]{1,0:T(8,128)(2,1)S(1)}, bf16[192,256]{1,0:T(8,128)(2,1)S(1)}, u32[]{:S(2)}, u32[]{:S(2)}) collective-permute-start(bf16[192,256]{1,0:T(8,128)(2,1)S(1)} %get-tuple-element.38), channel_id=1, source_target_pairs={{16,32},{48,64},{80,96},{32,16},{64,48},{96,80},{17,33},{49,65},{8... | collective-permute-start | bytes 294920 | tf_op jit(solution)/shard_map/ppermute | solution.py:386
  41.4 16.8 %collective-permute-start.5 = (bf16[80,256]{1,0:T(8,128)(2,1)S(1)}, bf16[80,256]{1,0:T(8,128)(2,1)S(1)}, u32[]{:S(2)}, u32[]{:S(2)}) collective-permute-start(bf16[80,256]{1,0:T(8,128)(2,1)S(1)} %get-tuple-element.35), channel_id=1, source_target_pairs={{0,1},{2,3},{4,5},{6,7},{8,9},{10,11},{12,13},{14,15},{1,0},{3,2},... | collective-permute-start | bytes 122888 | tf_op jit(solution)/shard_map/ppermute | solution.py:386
  41.8 16.4 %collective-permute-start.6 = (bf16[80,256]{1,0:T(8,128)(2,1)S(1)}, bf16[80,256]{1,0:T(8,128)(2,1)S(1)}, u32[]{:S(2)}, u32[]{:S(2)}) collective-permute-start(bf16[80,256]{1,0:T(8,128)(2,1)S(1)} %get-tuple-element.36), channel_id=1, source_target_pairs={{1,2},{3,4},{5,6},{7,8},{9,10},{11,12},{13,14},{2,1},{4,3},{6,5},{... | collective-permute-start | bytes 122888 | tf_op jit(solution)/shard_map/ppermute | solution.py:386
  46.5 27.0 %all-to-all-start = ((bf16[64,48,128]{2,1,0:T(8,128)(2,1)}), bf16[64,48,128]{2,1,0:T(8,128)(2,1)S(1)}, u32[]{:S(2)}, u32[]{:S(2)}) async-start(bf16[64,48,128]{2,1,0:T(8,128)(2,1)} %bitcast.8), calls=%async_computation | async-start | bytes 1572864 | tf_op jit(solution)/shard_map/all_to_all | solution.py:481
  58.8 4.9 %collective-permute-start.9 = (bf16[32,256]{1,0:T(8,128)(2,1)S(1)}, bf16[32,256]{1,0:T(8,128)(2,1)S(1)}, u32[]{:S(2)}, u32[]{:S(2)}) collective-permute-start(bf16[32,256]{1,0:T(8,128)(2,1)S(1)} %get-tuple-element.39), channel_id=1, source_target_pairs={{0,16},{32,48},{64,80},{96,112},{16,0},{48,32},{80,64},{112,96},{1... | collective-permute-start | bytes 49160 | tf_op jit(solution)/shard_map/ppermute | solution.py:386
  61.4 2.3 %collective-permute-start.10 = (bf16[32,256]{1,0:T(8,128)(2,1)S(1)}, bf16[32,256]{1,0:T(8,128)(2,1)S(1)}, u32[]{:S(2)}, u32[]{:S(2)}) collective-permute-start(bf16[32,256]{1,0:T(8,128)(2,1)S(1)} %get-tuple-element.40), channel_id=1, source_target_pairs={{16,32},{48,64},{80,96},{32,16},{64,48},{96,80},{17,33},{49,65},{8... | collective-permute-start | bytes 49160 | tf_op jit(solution)/shard_map/ppermute | solution.py:386

commit v4 on v3

--- a/solution.py
+++ b/solution.py
@@ -16,6 +16,7 @@
 KR, KC = 14, 16
 NK = KR * KC
 NB = 16
+HALO = 2 * 3 * TC + 2 * 80
 CHUNK = 48
 EPS = 1e-6
 NEG = -1e30
@@ -75,8 +76,7 @@
     w_tall,
     o_gr,
     o_gh,
-    o_intra,
-    o_inter,
+    o_side,
     o_first,
     o_second,
     o_keep,
@@ -97,8 +97,8 @@
     gmat,
     gdown,
     pk,
-    side_in,
-    side,
+    halo,
+    rims,
     *,
     rows_total,
     cols_total,
@@ -139,30 +139,31 @@
         got = nn(h, w_qkv[:, C:])
         kv[3 + 4 * i : 7 + 4 * i, 3 : TC + 3, :] = got.reshape(4, TC, 2 * C)
 
-    side_in[...] = jnp.zeros_like(side_in)
+    halo[...] = jnp.zeros_like(halo)
     upper = half_row == 0
     one = first[...].astype(F32)
     two = second[...].astype(F32)
-    h_rows = []
-    for at, x in ((0, jnp.where(upper, two, one)), (TR + 3, jnp.where(upper, one, two))):
-        h = hidden(x[0 : 3 * TC])
-        h_rows.append(h)
-        kv[at : at + 3, 3 : TC + 3, :] = nn(h, w_qkv[:, C:]).reshape(3, TC, 2 * C)
+    sides = ((0, jnp.where(upper, two, one)), (TR + 3, jnp.where(upper, one, two)))
+    for n, (at, x) in enumerate(sides):
+        halo[192 * n : 192 * n + 192, :] = x[0 : 3 * TC]
         for k in range(2):
             lo = 3 * TC + 16 * k
-            side_in[k, 3 * at : 3 * at + 9, :] = x[lo : lo + 9]
-    h_above, h_below = h_rows
+            halo[384 + 80 * k + 3 * at : 384 + 80 * k + 3 * at + 9, :] = x[lo : lo + 9]
     for r in range(TR):
         near = intra[r].astype(F32)
         far = inter[r].astype(F32)
-        side_in[0, 3 * r + 9 : 3 * r + 12, :] = jnp.where(even, far, near)
-        side_in[1, 3 * r + 9 : 3 * r + 12, :] = jnp.where(even, near, far)
-    h_side = [hidden(side_in[k]) for k in range(2)]
+        lo = 384 + 3 * r + 9
+        halo[lo : lo + 3, :] = jnp.where(even, far, near)
+        halo[lo + 80 : lo + 83, :] = jnp.where(even, near, far)
+    h_halo = hidden(halo[...])
+    got = nn(h_halo, w_qkv[:, C:])
+    kv[0:3, 3 : TC + 3, :] = got[0:192].reshape(3, TC, 2 * C)
+    kv[TR + 3 :, 3 : TC + 3, :] = got[192:384].reshape(3, TC, 2 * C)
     for k in range(2):
-        got = nn(h_side[k], w_qkv[:, C:])
         lo = k * (TC + 3)
         for r in range(ER):
-            kv[r, lo : lo + 3, :] = got[3 * r : 3 * r + 3, :]
+            at = 384 + 80 * k + 3 * r
+            kv[r, lo : lo + 3, :] = got[at : at + 3, :]
     dkv[...] = jnp.zeros_like(dkv)
 
     blocks = [(rb, cb) for cb in range(8) for rb in range(2)]
@@ -186,9 +187,9 @@
         att[r0 : r0 + 8, c0 : c0 + 8, :] = out.reshape(8, 8, C)
 
     gsc2 = jnp.zeros((1, C), F32)
-    for i in range(4):
-        at = slice(256 * i, 256 * i + 256)
-        a = att[4 * i : 4 * i + 4].reshape(256, C).astype(BF)
+    for i in range(2):
+        at = slice(512 * i, 512 * i + 512)
+        a = att[8 * i : 8 * i + 8].reshape(512, C).astype(BF)
         attb[at, :] = a
         resid = (tok[at, :].astype(F32) + nn(a, w_out[...])).astype(BF).astype(F32)
         n2, inv2 = norm(resid)
@@ -210,7 +211,7 @@
         gsc2 = gsc2 + jnp.sum(gh * n2, axis=0, keepdims=True)
         gr = (g.astype(F32) + back).astype(BF)
         o_gr[at, :] = gr
-        gatt[4 * i : 4 * i + 4] = nt(gr, w_out[...]).astype(BF).astype(F32).reshape(4, TC, C)
+        gatt[8 * i : 8 * i + 8] = nt(gr, w_out[...]).astype(BF).astype(F32).reshape(8, TC, C)
 
     def put(first, value):
         for n in range(value.shape[1] // 128):
@@ -237,25 +238,31 @@
         dkv[r0 : r0 + KR, c0 : c0 + KC, :C] += nn(ds, qe).reshape(KR, KC, C)
         dkv[r0 : r0 + KR, c0 : c0 + KC, C:] += nn(pb, ge).reshape(KR, KC, C)
 
-    side[...] = jnp.zeros_like(side)
-    for r in range(ER):
-        side[0, 3 * r : 3 * r + 3, :] = dkv[r, 0:3, :]
-        side[1, 3 * r : 3 * r + 3, :] = dkv[r, TC + 3 : TC + 6, :]
-    top = dkv[0:3, 3 : TC + 3, :].reshape(3 * TC, 2 * C).astype(BF)
-    bottom = dkv[TR + 3 :, 3 : TC + 3, :].reshape(3 * TC, 2 * C).astype(BF)
-    left = side[0].astype(BF)
-    right = side[1].astype(BF)
-    g_left = nt(left, w_qkv[:, C:])
-    g_right = nt(right, w_qkv[:, C:])
-    o_intra[...] = jnp.where(even, g_right, g_left).astype(BF)
-    o_inter[...] = jnp.where(even, g_left, g_right).astype(BF)
-    g_top = nt(top, w_qkv[:, C:])
-    g_bottom = nt(bottom, w_qkv[:, C:])
+    rims[0:192, :] = dkv[0:3, 3 : TC + 3, :].reshape(192, 2 * C)
+    rims[192:384, :] = dkv[TR + 3 :, 3 : TC + 3, :].reshape(192, 2 * C)
+    for k in range(2):
+        lo = k * (TC + 3)
+        for r in range(ER):
+            at = 384 + 80 * k + 3 * r
+            rims[at : at + 3, :] = dkv[r, lo : lo + 3, :]
+        rims[384 + 80 * k + 3 * ER : 464 + 80 * k, :] = jnp.zeros((80 - 3 * ER, 2 * C), F32)
+    d_rims = rims[...].astype(BF)
+    g_rims = nt(d_rims, w_qkv[:, C:])
+    g_left, g_right = g_rims[384:464], g_rims[464:544]
+    o_side[0:48, :] = g_left[9:57]
+    o_side[48:96, :] = g_right[9:57]
+    work = halo
+    for n, src in enumerate((g_rims[0:192], g_rims[192:384])):
+        work[n * 224 : n * 224 + 192, :] = src
+        for k, x in enumerate((g_left, g_right)):
+            at = n * 224 + 192 + 16 * k
+            work[at : at + 16, :] = x[0:16] if n == 0 else x[3 * (TR + 3) : 3 * (TR + 3) + 16]
+    g_top, g_bottom = work[0:224, :], work[224:448, :]
     o_first[...] = jnp.where(upper, g_bottom, g_top).astype(BF)
     o_second[...] = jnp.where(upper, g_top, g_bottom).astype(BF)
 
     gq = jnp.zeros((C, C), F32)
-    gkv = tn(h_above, top) + tn(h_below, bottom) + tn(h_side[0], left) + tn(h_side[1], right)
+    gkv = tn(h_halo, d_rims)
     for i in range(4):
         at = slice(256 * i, 256 * i + 256)
         d_q = dq[4 * i : 4 * i + 4].reshape(256, C).astype(BF)
@@ -297,45 +304,33 @@
     o_mine[...] = (keep[...].astype(F32) + got[...].astype(F32)).astype(BF)
 
 
-def sides_of(pos, intra, inter):
-    even = pos[2] == 0
+def side_kernel(pos, side, first, second, o_intra, o_inter, work):
+    even, upper = pos[2] == 0, pos[3] == 0
+    one = first[192:224, :].astype(F32)
+    two = second[192:224, :].astype(F32)
+    above, below = jnp.where(upper, two, one), jnp.where(upper, one, two)
+    work[...] = side[...]
+    for k in range(2):
+        work[48 * k : 48 * k + 9, :] += above[16 * k : 16 * k + 9]
+        work[48 * k + 39 : 48 * k + 48, :] += below[16 * k : 16 * k + 9]
+    left, right = work[0:48, :], work[48:96, :]
+    o_intra[...] = jnp.where(even, right, left).astype(BF)
+    o_inter[...] = jnp.where(even, left, right).astype(BF)
+
+
+def token_kernel(pos, tok, gr, gh, intra, inter, first, second, scales, o_tok, work):
+    even, upper = pos[2] == 0, pos[3] == 0
     near = intra[...].astype(F32)
     far = inter[...].astype(F32)
-    return jnp.where(even, far, near), jnp.where(even, near, far)
-
-
-def corner_kernel(pos, intra, inter, _first, _second, o_first, o_second, work):
-    upper = pos[3] == 0
-    work[...] = jnp.zeros_like(work)
-    for k, x in enumerate(sides_of(pos, intra, inter)):
-        work[0, 16 * k : 16 * k + 9, :] = x[0:9]
-        work[1, 16 * k : 16 * k + 9, :] = x[3 * (TR + 3) : 3 * ER]
-    o_first[...] = jnp.where(upper, work[1], work[0]).astype(BF)
-    o_second[...] = jnp.where(upper, work[0], work[1]).astype(BF)
-
-
-def token_kernel(
-    pos, tok, gr, gh, intra, inter, first, second, c_first, c_second, scales, o_tok, work
-):
-    upper = pos[3] == 0
-    left, right = sides_of(pos, intra, inter)
+    left, right = jnp.where(even, far, near), jnp.where(even, near, far)
     work[...] = gh[...]
-    one = first[...].astype(F32)
-    two = second[...].astype(F32)
+    one = first[0 : 3 * TC, :].astype(F32)
+    two = second[0 : 3 * TC, :].astype(F32)
     work[0 : 3 * TC, :] += jnp.where(upper, two, one)
     work[(TR - 3) * TC :, :] += jnp.where(upper, one, two)
-    one = c_first[...].astype(F32)
-    two = c_second[...].astype(F32)
-    corners = jnp.where(upper, two, one), jnp.where(upper, one, two)
     for r in range(TR):
-        k = 3 * (r + 3)
-        add_left, add_right = left[k : k + 3, :], right[k : k + 3, :]
-        if r < 3 or r >= TR - 3:
-            n, j = (0, 3 * r) if r < 3 else (1, 3 * (r - TR + 3))
-            add_left = add_left + corners[n][j : j + 3, :]
-            add_right = add_right + corners[n][16 + j : 19 + j, :]
-        work[r * TC : r * TC + 3, :] += add_left
-        work[r * TC + TC - 3 : r * TC + TC, :] += add_right
+        work[r * TC : r * TC + 3, :] += left[3 * r : 3 * r + 3]
+        work[r * TC + TC - 3 : r * TC + TC, :] += right[3 * r : 3 * r + 3]
     s0 = scales[0:1, :]
     for i in range(4):
         at = slice(256 * i, 256 * i + 256)
@@ -431,15 +426,14 @@
         out_shape=[
             sds((flat, C), BF),
             sds((flat, C), F32),
-            sds((80, C), BF),
-            sds((80, C), BF),
-            sds((3 * TC, C), BF),
-            sds((3 * TC, C), BF),
+            sds((96, C), F32),
+            sds((224, C), BF),
+            sds((224, C), BF),
             sds((64 * CHUNK, 128), BF),
             sds((64 * CHUNK, 128), BF),
         ],
         in_specs=smem + vm(9),
-        out_specs=vm(8),
+        out_specs=vm(7),
         scratch_shapes=[
             pltpu.VMEM((6, NK, 256), F32),
             pltpu.VMEM((ER, EC, 2 * C), F32),
@@ -457,16 +451,14 @@
             pltpu.VMEM((14, 256, 128), F32),
             pltpu.VMEM((2, FF, 128), F32),
             pltpu.VMEM((2, 64 * CHUNK, 128), F32),
-            pltpu.VMEM((2, 80, C), F32),
-            pltpu.VMEM((2, 80, 2 * C), F32),
+            pltpu.VMEM((HALO, C), F32),
+            pltpu.VMEM((HALO, 2 * C), F32),
         ],
         name="block_backward",
         **params(44),
     )(pos, tok, gout, intra, inter, first, second, scales, w_wide, w_tall)
-    gr, gh, intra, inter, first, second, keep, send = outs
-
-    inter = swap(inter, COL, 1)
-    intra = swap(intra, COL, 0)
+    gr, gh, side, first, second, keep, send = outs
+
     got = lax.ppermute(send, "core", [(0, 1), (1, 0)])
     first = swap(first, ROW, 0)
     second = swap(second, ROW, 1)
@@ -479,24 +471,24 @@
         **params(16),
     )(keep, got)
     parts = lax.all_to_all(mine.reshape(64, CHUNK, 128), CHIPS, 0, 0, tiled=True)
-    c_first, c_second = pl.pallas_call(
-        corner_kernel,
-        out_shape=[sds((32, C), BF)] * 2,
-        in_specs=smem + vm(2) + [pl.BlockSpec(memory_space=pl.ANY)] * 2,
+    intra, inter = pl.pallas_call(
+        side_kernel,
+        out_shape=[sds((48, C), BF)] * 2,
+        in_specs=smem + vm(3),
         out_specs=vm(2),
-        scratch_shapes=[pltpu.VMEM((2, 32, C), F32)],
+        scratch_shapes=[pltpu.VMEM((96, C), F32)],
         cost_estimate=pl.CostEstimate(
-            flops=100 * 10**9, bytes_accessed=4 * 80 * C, transcendentals=0
+            flops=100 * 10**9, bytes_accessed=4 * 96 * C, transcendentals=0
         ),
-        name="corners",
+        name="sides",
         **params(16),
-    )(pos, intra, inter, first, second)
-    c_first = swap(c_first, ROW, 0)
-    c_second = swap(c_second, ROW, 1)
+    )(pos, side, first, second)
+    inter = swap(inter, COL, 1)
+    intra = swap(intra, COL, 0)
     grad_tokens = pl.pallas_call(
         token_kernel,
         out_shape=sds((flat, C), BF),
-        in_specs=smem + vm(10),
+        in_specs=smem + vm(8),
         out_specs=vm(1)[0],
         scratch_shapes=[pltpu.VMEM((flat, C), F32)],
         cost_estimate=pl.CostEstimate(
@@ -504,7 +496,7 @@
         ),
         name="grad_tokens",
         **params(16),
-    )(pos, tok, gr, gh, intra, inter, first, second, c_first, c_second, scales)
+    )(pos, tok, gr, gh, intra, inter, first, second, scales)
     parts, grad_tokens = lax.optimization_barrier((parts, grad_tokens))
     outs = pl.pallas_call(
         functools.partial(sum_kernel, loss_scale=1.0 / math.sqrt(rows_total * cols_total)),

time: 75.1 us -> 70 us (0.932)
  starting transfers between devices: 35.2 us -> 32.3 us
  waiting for transfers between devices: 14.8 us -> 13.6 us
  Pallas kernels: 20.9 us -> 19.8 us
    all_to_all x1, waiting for transfers between devices: 7.75 us -> 3.84 us  [body(): lax.all_to_all(mine.reshape(64, CHUNK, 128), CHIPS, 0, 0, tiled=True)]
    ppermute x10 -> x8, starting transfers between devices: 22.7 us -> 19.5 us  [swap(): return lax.ppermute(x, axes, pairs + [(b, a) for a, b in pairs])]
    ppermute x10 -> x8, waiting for transfers between devices: 7.07 us -> 9.77 us  [swap(): return lax.ppermute(x, axes, pairs + [(b, a) for a, b in pairs])]
    pallas_call x1, Pallas kernels: 16.6 us -> 15.4 us  [body(): pl.pallas_call(functools.partial(main_kernel, rows_total=rows_total, cols...]
  transfers between devices with their start and end apart: 12 -> 10, of which waited for: 4 -> 4; matrix products, arithmetic and copies ran while one was open for 2% -> 2% of each run, Pallas kernels for 5% -> 5%
where the time goes in v4:
time: 70 us; the launch traced here: 68.9 us
  starting transfers between devices  32.3 us (46%)
  Pallas kernels  19.8 us (28%)
  waiting for transfers between devices  13.6 us (19%)
  other arithmetic  1.2 us (2%)
  local copies, waits for them, and re-layouts  1.15 us (2%)
  between operations  0.87 us (1%)
    ppermute x8, starting transfers between devices, swap(): return lax.ppermute(x, axes, pairs + [(b, a) for a, b in pairs])  19.5 us
    pallas_call x1, Pallas kernels, body(): pl.pallas_call(functools.partial(main_kernel, rows_total=rows_total, cols...  15.4 us
    all_to_all x1, starting transfers between devices, body(): lax.all_to_all(mine.reshape(64, CHUNK, 128), CHIPS, 0, 0, tiled=True)  12 us
    ppermute x8, waiting for transfers between devices, swap(): return lax.ppermute(x, axes, pairs + [(b, a) for a, b in pairs])  9.77 us
    all_to_all x1, waiting for transfers between devices, body(): lax.all_to_all(mine.reshape(64, CHUNK, 128), CHIPS, 0, 0, tiled=True)  3.84 us
    pallas_call x1, Pallas kernels, body(): pl.pallas_call(token_kernel, out_shape=sds((flat, C), BF), in_specs=smem...  1.97 us
  transfers between devices with their start and end apart: 10, of which 4 were waited for; matrix products, arithmetic and copies ran while one was open for 2% of the time, Pallas kernels for 5%

profile of v4, /device:TPU:1, one launch (start us, length us, event | category | flops | bytes accessed | tf_op | source)
XLA Modules:
  0.0 68.9 jit_solution(9055638217313189123)
XLA Ops:
  0.7 1.0 %broadcast_select_fusion.4 = (bf16[16,3,256]{2,1,0:T(4,128)(2,1)S(1)}, bf16[16,3,256]{2,1,0:T(4,128)(2,1)S(1)}) fusion(pred[]{:T(512)S(6)} %eq.6, bf16[16,64,256]{2,1,0:T(8,128)(2,1)} %param.7), kind=kLoop, calls=%fused_computation.6 | loop fusion | flops 24576 | bytes 98305 | tf_op jit(solution)/shard_map/jit(_where)/select_n | solution.py:399
  1.6 4.9 %collective-permute-start.1 = (bf16[16,3,256]{2,1,0:T(4,128)(2,1)S(1)}, bf16[16,3,256]{2,1,0:T(4,128)(2,1)S(1)}, u32[]{:S(2)}, u32[]{:S(2)}) collective-permute-start(bf16[16,3,256]{2,1,0:T(4,128)(2,1)S(1)} %get-tuple-element.48), channel_id=1, source_target_pairs={{1,2},{3,4},{5,6},{7,8},{9,10},{11,12},{13,14},{2,1},{4,3},{6,5},{... | collective-permute-start | bytes 73736 | tf_op jit(solution)/shard_map/ppermute | solution.py:381
  6.6 0.1 collective-permute-start
  6.7 1.0 %fusion = (bf16[3,64,256]{2,1,0:T(8,128)(2,1)S(1)}, bf16[3,64,256]{2,1,0:T(8,128)(2,1)S(1)}) fusion(bf16[16,64,256]{2,1,0:T(8,128)(2,1)} %param.7), kind=kLoop, calls=%fused_computation.9 | loop fusion | bytes 393216 | tf_op jit(solution)/shard_map/slice | solution.py:408
  7.7 0.1 pad_add_fusion.pos
  7.7 0.4 collective-permute-done.1.inter
  8.2 0.0 collective-permute-done.intra
  8.4 0.0 copy-start.6
  8.4 0.8 %collective-permute-start.3 = (bf16[224,256]{1,0:T(8,128)(2,1)S(1)}, bf16[224,256]{1,0:T(8,128)(2,1)S(1)}, u32[]{:S(2)}, u32[]{:S(2)}) collective-permute-start(bf16[224,256]{1,0:T(8,128)(2,1)S(1)} %get-tuple-element.50), channel_id=1, source_target_pairs={{16,32},{48,64},{80,96},{32,16},{64,48},{96,80},{17,33},{49,65},{8... | collective-permute-start | bytes 344072 | tf_op jit(solution)/shard_map/ppermute | solution.py:381
  9.2 0.0 copy-start
  9.2 0.0 copy-start.1
  9.3 0.0 copy-start.2
  9.3 5.2 %collective-permute-start.2 = (bf16[224,256]{1,0:T(8,128)(2,1)S(1)}, bf16[224,256]{1,0:T(8,128)(2,1)S(1)}, u32[]{:S(2)}, u32[]{:S(2)}) collective-permute-start(bf16[224,256]{1,0:T(8,128)(2,1)S(1)} %get-tuple-element.51), channel_id=1, source_target_pairs={{0,16},{32,48},{64,80},{96,112},{16,0},{48,32},{80,64},{112,96},{1... | collective-permute-start | bytes 344072 | tf_op jit(solution)/shard_map/ppermute | solution.py:381
  14.5 0.1 pad_maximum_fusion.w_wide
  14.6 0.0 collective-permute-done.3.second
  14.6 5.0 %collective-permute-done.2.first = bf16[224,256]{1,0:T(8,128)(2,1)S(1)} collective-permute-done((bf16[224,256]{1,0:T(8,128)(2,1)S(1)}, bf16[224,256]{1,0:T(8,128)(2,1)S(1)}, u32[]{:S(2)}, u32[]{:S(2)}) %collective-permute-start.2) | collective-permute-done | bytes 114720 | tf_op jit(solution)/shard_map/ppermute | solution.py:381
  19.7 15.4 %block_backward.1 = (bf16[1024,256]{1,0:T(8,128)(2,1)S(1)}, f32[1024,256]{1,0:T(8,128)S(1)}, f32[96,256]{1,0:T(8,128)S(1)}, bf16[224,256]{1,0:T(8,128)(2,1)S(1)}...) custom-call(s32[4]{0:T(128)S(1)} %pad_add_fusion.pos, ...), custom_call_target="tpu_custom_call" | custom-call | tf_op jit(solution)/shard_map/block_backward/pallas_call | solution.py:424
  35.1 0.7 %collective-permute-start.4 = (bf16[3072,128]{1,0:T(8,128)(2,1)S(1)}, bf16[3072,128]{1,0:T(8,128)(2,1)S(1)}, u32[]{:S(2)}, u32[]{:S(2)}) collective-permute-start(bf16[3072,128]{1,0:T(8,128)(2,1)S(1)} %get-tuple-element.31), channel_id=1, source_target_pairs={{0,1},{1,0},{2,3},{3,2},{4,5},{5,4},{6,7},{7,6},{8,9},{9,8},{10,11... | collective-permute-start | bytes 2359304 | tf_op jit(solution)/shard_map/ppermute | solution.py:462
  35.8 3.7 %collective-permute-start.5 = (bf16[224,256]{1,0:T(8,128)(2,1)S(1)}, bf16[224,256]{1,0:T(8,128)(2,1)S(1)}, u32[]{:S(2)}, u32[]{:S(2)}) collective-permute-start(bf16[224,256]{1,0:T(8,128)(2,1)S(1)} %get-tuple-element.35), channel_id=1, source_target_pairs={{0,16},{32,48},{64,80},{96,112},{16,0},{48,32},{80,64},{112,96},{1... | collective-permute-start | bytes 344072 | tf_op jit(solution)/shard_map/ppermute | solution.py:381
  39.5 0.7 collective-permute-start.6
  40.2 0.0 collective-permute-done.4.got
  40.2 1.1 %add_core.1 = bf16[3072,128]{1,0:T(8,128)(2,1)} custom-call(bf16[3072,128]{1,0:T(8,128)(2,1)S(1)} %get-tuple-element.30.keep, bf16[3072,128]{1,0:T(8,128)(2,1)S(1)} %collective-permute-done.4.got), custom_call_target="tpu_custom_call" | custom-call | tf_op jit(solution)/shard_map/add_core/pallas_call | solution.py:465
  41.3 12.0 %all-to-all-start = ((bf16[64,48,128]{2,1,0:T(8,128)(2,1)}), bf16[64,48,128]{2,1,0:T(8,128)(2,1)S(1)}, u32[]{:S(2)}, u32[]{:S(2)}) async-start(bf16[64,48,128]{2,1,0:T(8,128)(2,1)} %bitcast.8), calls=%async_computation | async-start | bytes 1572864 | tf_op jit(solution)/shard_map/all_to_all | solution.py:473
  53.3 0.0 collective-permute-done.5.first
  53.3 0.0 collective-permute-done.6.second
  53.3 0.6 sides.1
  53.9 1.0 %collective-permute-start.7 = (bf16[48,256]{1,0:T(8,128)(2,1)S(1)}, bf16[48,256]{1,0:T(8,128)(2,1)S(1)}, u32[]{:S(2)}, u32[]{:S(2)}) collective-permute-start(bf16[48,256]{1,0:T(8,128)(2,1)S(1)} %get-tuple-element.37), channel_id=1, source_target_pairs={{0,1},{2,3},{4,5},{6,7},{8,9},{10,11},{12,13},{14,15},{1,0},{3,2},... | collective-permute-start | bytes 73736 | tf_op jit(solution)/shard_map/ppermute | solution.py:381
  54.9 3.1 %collective-permute-start.8 = (bf16[48,256]{1,0:T(8,128)(2,1)S(1)}, bf16[48,256]{1,0:T(8,128)(2,1)S(1)}, u32[]{:S(2)}, u32[]{:S(2)}) collective-permute-start(bf16[48,256]{1,0:T(8,128)(2,1)S(1)} %get-tuple-element.38), channel_id=1, source_target_pairs={{1,2},{3,4},{5,6},{7,8},{9,10},{11,12},{13,14},{2,1},{4,3},{6,5},{... | collective-permute-start | bytes 73736 | tf_op jit(solution)/shard_map/ppermute | solution.py:381
  58.0 4.3 %collective-permute-done.8.inter = bf16[48,256]{1,0:T(8,128)(2,1)S(1)} collective-permute-done((bf16[48,256]{1,0:T(8,128)(2,1)S(1)}, bf16[48,256]{1,0:T(8,128)(2,1)S(1)}, u32[]{:S(2)}, u32[]{:S(2)}) %collective-permute-start.8) | collective-permute-done | bytes 24608 | tf_op jit(solution)/shard_map/ppermute | solution.py:381
  62.3 2.0 %grad_tokens.1 = bf16[1024,256]{1,0:T(8,128)(2,1)} custom-call(s32[4]{0:T(128)S(1)} %pad_add_fusion.pos, bf16[1024,256]{1,0:T(8,128)(2,1)S(1)} %bitcast.11, bf16[1024,256]{1,0:T(8,128)(2,1)S(1)} %get-tuple-element.32.gr, f32[1024,256]{1,0:T(8,128)S(1)} %get-tuple-element.33.gh, bf16[48,256]{1,0:T(8,128)(2,1)S(1)} %collective-permute-done.7.intra, ...), custom_call_target="tpu_custom_call" | custom-call | flops 7864320 | bytes 2621440 | tf_op jit(solution)/shard_map/grad_tokens/pallas_call | solution.py:488
  64.3 3.8 %all-to-all-done.parts = bf16[64,48,128]{2,1,0:T(8,128)(2,1)S(1)} async-done(((bf16[64,48,128]{2,1,0:T(8,128)(2,1)}), bf16[64,48,128]{2,1,0:T(8,128)(2,1)S(1)}, u32[]{:S(2)}, u32[]{:S(2)}) %all-to-all-start) | async-done | bytes 786464 | tf_op jit(solution)/shard_map/all_to_all | solution.py:473
  68.1 0.7 %weight_sums.1 = (f32[2,768]{1,0:T(2,128)}, f32[2,256]{1,0:T(2,128)}, f32[2,768]{1,0:T(2,128)}, f32[6,256]{1,0:T(8,128)}, f32[2,256]{1,0:T(2,128)}) custom-call(bf16[64,48,128]{2,1,0:T(8,128)(2,1)S(1)} %all-to-all-done.parts), custom_call_target="tpu_custom_call" | custom-call | tf_op jit(solution)/shard_map/weight_sums/pallas_call | solution.py:501
  (22 shorter events, 0.3 us)
Async XLA Ops:
  0.6 13.9 %copy-start.3 = (bf16[256,768]{1,0:T(8,128)(2,1)S(1)}, bf16[256,768]{1,0:T(8,128)(2,1)}, u32[]{:S(2)}) copy-start(bf16[256,768]{1,0:T(8,128)(2,1)} %param.12) | copy-start | bytes 1179652
  0.6 13.9 %copy-start.4 = (bf16[256,768]{1,0:T(8,128)(2,1)S(1)}, bf16[256,768]{1,0:T(8,128)(2,1)}, u32[]{:S(2)}) copy-start(bf16[256,768]{1,0:T(8,128)(2,1)} %param.10) | copy-start | bytes 1179652
  1.6 6.5 %collective-permute-start.1 = (bf16[16,3,256]{2,1,0:T(4,128)(2,1)S(1)}, bf16[16,3,256]{2,1,0:T(4,128)(2,1)S(1)}, u32[]{:S(2)}, u32[]{:S(2)}) collective-permute-start(bf16[16,3,256]{2,1,0:T(4,128)(2,1)S(1)} %get-tuple-element.48), channel_id=1, source_target_pairs={{1,2},{3,4},{5,6},{7,8},{9,10},{11,12},{13,14},{2,1},{4,3},{6,5},{... | collective-permute-start | bytes 73736 | tf_op jit(solution)/shard_map/ppermute | solution.py:381
  6.6 1.6 %collective-permute-start = (bf16[16,3,256]{2,1,0:T(4,128)(2,1)S(1)}, bf16[16,3,256]{2,1,0:T(4,128)(2,1)S(1)}, u32[]{:S(2)}, u32[]{:S(2)}) collective-permute-start(bf16[16,3,256]{2,1,0:T(4,128)(2,1)S(1)} %get-tuple-element.49), channel_id=1, source_target_pairs={{0,1},{2,3},{4,5},{6,7},{8,9},{10,11},{12,13},{14,15},{1,0},{3,2},... | collective-permute-start | bytes 73736 | tf_op jit(solution)/shard_map/ppermute | solution.py:381
  8.4 6.2 %copy-start.5 = (bf16[768,256]{1,0:T(8,128)(2,1)S(1)}, bf16[768,256]{1,0:T(8,128)(2,1)}, u32[]{:S(2)}) copy-start(bf16[768,256]{1,0:T(8,128)(2,1)} %param.13) | copy-start | bytes 1179652
  8.4 6.2 %copy-start.6 = (bf16[256,256]{1,0:T(8,128)(2,1)S(1)}, bf16[256,256]{1,0:T(8,128)(2,1)}, u32[]{:S(2)}) copy-start(bf16[256,256]{1,0:T(8,128)(2,1)} %param.11) | copy-start | bytes 393220
  8.4 6.2 %collective-permute-start.3 = (bf16[224,256]{1,0:T(8,128)(2,1)S(1)}, bf16[224,256]{1,0:T(8,128)(2,1)S(1)}, u32[]{:S(2)}, u32[]{:S(2)}) collective-permute-start(bf16[224,256]{1,0:T(8,128)(2,1)S(1)} %get-tuple-element.50), channel_id=1, source_target_pairs={{16,32},{48,64},{80,96},{32,16},{64,48},{96,80},{17,33},{49,65},{8... | collective-permute-start | bytes 344072 | tf_op jit(solution)/shard_map/ppermute | solution.py:381
  9.2 10.4 %copy-start = (bf16[16,64,256]{2,1,0:T(8,128)(2,1)S(1)}, bf16[16,64,256]{2,1,0:T(8,128)(2,1)}, u32[]{:S(2)}) copy-start(bf16[16,64,256]{2,1,0:T(8,128)(2,1)} %param.7) | copy-start | bytes 1572868
  9.2 10.4 %copy-start.1 = (bf16[16,64,256]{2,1,0:T(8,128)(2,1)S(1)}, bf16[16,64,256]{2,1,0:T(8,128)(2,1)}, u32[]{:S(2)}) copy-start(bf16[16,64,256]{2,1,0:T(8,128)(2,1)} %param.8) | copy-start | bytes 1572868
  9.3 10.4 %copy-start.2 = (f32[2,256]{1,0:T(2,128)S(1)}, f32[2,256]{1,0:T(2,128)}, u32[]{:S(2)}) copy-start(f32[2,256]{1,0:T(2,128)} %scales.3) | copy-start | bytes 6148
  9.3 10.4 %collective-permute-start.2 = (bf16[224,256]{1,0:T(8,128)(2,1)S(1)}, bf16[224,256]{1,0:T(8,128)(2,1)S(1)}, u32[]{:S(2)}, u32[]{:S(2)}) collective-permute-start(bf16[224,256]{1,0:T(8,128)(2,1)S(1)} %get-tuple-element.51), channel_id=1, source_target_pairs={{0,16},{32,48},{64,80},{96,112},{16,0},{48,32},{80,64},{112,96},{1... | collective-permute-start | bytes 344072 | tf_op jit(solution)/shard_map/ppermute | solution.py:381
  35.1 5.1 %collective-permute-start.4 = (bf16[3072,128]{1,0:T(8,128)(2,1)S(1)}, bf16[3072,128]{1,0:T(8,128)(2,1)S(1)}, u32[]{:S(2)}, u32[]{:S(2)}) collective-permute-start(bf16[3072,128]{1,0:T(8,128)(2,1)S(1)} %get-tuple-element.31), channel_id=1, source_target_pairs={{0,1},{1,0},{2,3},{3,2},{4,5},{5,4},{6,7},{7,6},{8,9},{9,8},{10,11... | collective-permute-start | bytes 2359304 | tf_op jit(solution)/shard_map/ppermute | solution.py:462
  35.8 17.5 %collective-permute-start.5 = (bf16[224,256]{1,0:T(8,128)(2,1)S(1)}, bf16[224,256]{1,0:T(8,128)(2,1)S(1)}, u32[]{:S(2)}, u32[]{:S(2)}) collective-permute-start(bf16[224,256]{1,0:T(8,128)(2,1)S(1)} %get-tuple-element.35), channel_id=1, source_target_pairs={{0,16},{32,48},{64,80},{96,112},{16,0},{48,32},{80,64},{112,96},{1... | collective-permute-start | bytes 344072 | tf_op jit(solution)/shard_map/ppermute | solution.py:381
  39.5 13.8 %collective-permute-start.6 = (bf16[224,256]{1,0:T(8,128)(2,1)S(1)}, bf16[224,256]{1,0:T(8,128)(2,1)S(1)}, u32[]{:S(2)}, u32[]{:S(2)}) collective-permute-start(bf16[224,256]{1,0:T(8,128)(2,1)S(1)} %get-tuple-element.36), channel_id=1, source_target_pairs={{16,32},{48,64},{80,96},{32,16},{64,48},{96,80},{17,33},{49,65},{8... | collective-permute-start | bytes 344072 | tf_op jit(solution)/shard_map/ppermute | solution.py:381
  41.3 26.9 %all-to-all-start = ((bf16[64,48,128]{2,1,0:T(8,128)(2,1)}), bf16[64,48,128]{2,1,0:T(8,128)(2,1)S(1)}, u32[]{:S(2)}, u32[]{:S(2)}) async-start(bf16[64,48,128]{2,1,0:T(8,128)(2,1)} %bitcast.8), calls=%async_computation | async-start | bytes 1572864 | tf_op jit(solution)/shard_map/all_to_all | solution.py:473
  53.9 4.1 %collective-permute-start.7 = (bf16[48,256]{1,0:T(8,128)(2,1)S(1)}, bf16[48,256]{1,0:T(8,128)(2,1)S(1)}, u32[]{:S(2)}, u32[]{:S(2)}) collective-permute-start(bf16[48,256]{1,0:T(8,128)(2,1)S(1)} %get-tuple-element.37), channel_id=1, source_target_pairs={{0,1},{2,3},{4,5},{6,7},{8,9},{10,11},{12,13},{14,15},{1,0},{3,2},... | collective-permute-start | bytes 73736 | tf_op jit(solution)/shard_map/ppermute | solution.py:381
  54.9 7.4 %collective-permute-start.8 = (bf16[48,256]{1,0:T(8,128)(2,1)S(1)}, bf16[48,256]{1,0:T(8,128)(2,1)S(1)}, u32[]{:S(2)}, u32[]{:S(2)}) collective-permute-start(bf16[48,256]{1,0:T(8,128)(2,1)S(1)} %get-tuple-element.38), channel_id=1, source_target_pairs={{1,2},{3,4},{5,6},{7,8},{9,10},{11,12},{13,14},{2,1},{4,3},{6,5},{... | collective-permute-start | bytes 73736 | tf_op jit(solution)/shard_map/ppermute | solution.py:381

commit v5 on v4

--- a/solution.py
+++ b/solution.py
@@ -47,20 +47,28 @@
     return x * inverse, inverse
 
 
-def head_masks():
-    lane = lax.broadcasted_iota(jnp.int32, (1, C), 1)
-    return [(jnp.right_shift(lane, 6) == h).astype(F32) for h in range(HEADS)]
-
-
-def expand(x, masks):
-    return jnp.concatenate([x * m for m in masks], axis=0).astype(BF)
-
-
-def pick(x, masks):
-    out = x[0:64] * masks[0]
-    for h in range(1, HEADS):
-        out = out + x[64 * h : 64 * h + 64] * masks[h]
-    return out
+def first_half():
+    return lax.broadcasted_iota(jnp.int32, (1, 128), 1) < 64
+
+
+def expand(x, low):
+    lo, hi = x[:, :128], x[:, 128:]
+    none = jnp.zeros_like(lo)
+    return jnp.concatenate(
+        [
+            jnp.concatenate([jnp.where(low, lo, 0.0), none], axis=1),
+            jnp.concatenate([jnp.where(low, 0.0, lo), none], axis=1),
+            jnp.concatenate([none, jnp.where(low, hi, 0.0)], axis=1),
+            jnp.concatenate([none, jnp.where(low, 0.0, hi)], axis=1),
+        ],
+        axis=0,
+    ).astype(BF)
+
+
+def pick(x, low):
+    lo = jnp.where(low, x[0:64, :128], x[64:128, :128])
+    hi = jnp.where(low, x[128:192, 128:], x[192:256, 128:])
+    return jnp.concatenate([lo, hi], axis=1)
 
 
 def main_kernel(
@@ -105,7 +113,7 @@
 ):
     base_r, base_c, core, half_row = pos[0], pos[1], pos[2], pos[3]
     even = core == 0
-    masks = head_masks()
+    masks = first_half()
     w_qkv, w_up = w_wide.at[0:C], w_wide.at[C : 2 * C]
     w_out, w_down = w_tall.at[0:C], w_tall.at[C : C + FF]
 
@@ -139,22 +147,15 @@
         got = nn(h, w_qkv[:, C:])
         kv[3 + 4 * i : 7 + 4 * i, 3 : TC + 3, :] = got.reshape(4, TC, 2 * C)
 
-    halo[...] = jnp.zeros_like(halo)
     upper = half_row == 0
     one = first[...].astype(F32)
     two = second[...].astype(F32)
-    sides = ((0, jnp.where(upper, two, one)), (TR + 3, jnp.where(upper, one, two)))
-    for n, (at, x) in enumerate(sides):
-        halo[192 * n : 192 * n + 192, :] = x[0 : 3 * TC]
-        for k in range(2):
-            lo = 3 * TC + 16 * k
-            halo[384 + 80 * k + 3 * at : 384 + 80 * k + 3 * at + 9, :] = x[lo : lo + 9]
-    for r in range(TR):
-        near = intra[r].astype(F32)
-        far = inter[r].astype(F32)
-        lo = 384 + 3 * r + 9
-        halo[lo : lo + 3, :] = jnp.where(even, far, near)
-        halo[lo + 80 : lo + 83, :] = jnp.where(even, near, far)
+    near = intra[...].astype(F32)
+    far = inter[...].astype(F32)
+    halo[0:192, :] = jnp.where(upper, two, one)
+    halo[192:384, :] = jnp.where(upper, one, two)
+    halo[384:464, :] = jnp.where(even, far, near)
+    halo[464:544, :] = jnp.where(even, near, far)
     h_halo = hidden(halo[...])
     got = nn(h_halo, w_qkv[:, C:])
     kv[0:3, 3 : TC + 3, :] = got[0:192].reshape(3, TC, 2 * C)
@@ -300,6 +301,25 @@
     o_send[...] = pk[1 - core].astype(BF)
 
 
+def edge_kernel(pos, tok, first, second, o_intra, o_inter, work):
+    even, upper = pos[2] == 0, pos[3] == 0
+    one = first[...].astype(F32)
+    two = second[...].astype(F32)
+    work[...] = jnp.zeros_like(work)
+    for at, x in ((0, jnp.where(upper, two, one)), (TR + 3, jnp.where(upper, one, two))):
+        for r in range(3):
+            to = 3 * (at + r)
+            work[0, to : to + 3, :] = x[r * TC : r * TC + 3]
+            work[1, to : to + 3, :] = x[r * TC + TC - 3 : r * TC + TC]
+    for r in range(TR):
+        to = 3 * (r + 3)
+        work[0, to : to + 3, :] = tok[r * TC : r * TC + 16, :].astype(F32)[0:3]
+        work[1, to : to + 3, :] = tok[r * TC + TC - 16 : r * TC + TC, :].astype(F32)[13:16]
+    head, tail = work[0], work[1]
+    o_intra[...] = jnp.where(even, tail, head).astype(BF)
+    o_inter[...] = jnp.where(even, head, tail).astype(BF)
+
+
 def add_kernel(keep, got, o_mine):
     o_mine[...] = (keep[...].astype(F32) + got[...].astype(F32)).astype(BF)
 
@@ -394,32 +414,25 @@
     gout = grad_out.reshape(flat, C)
     smem = [pl.BlockSpec(memory_space=pltpu.SMEM)]
 
-    even, upper = core_id == 0, half_row == 0
-    head, tail = tokens[:, :3], tokens[:, TC - 3 :]
-    inter = swap(jnp.where(even, head, tail), COL, 1)
-    intra = swap(jnp.where(even, tail, head), COL, 0)
-    before = jnp.where(even, inter, intra)
-    after = jnp.where(even, intra, inter)
-
-    def rim(lo):
-        gap = jnp.zeros((7, C), BF)
-        return jnp.concatenate(
-            [
-                tok[lo * TC : (lo + 3) * TC],
-                before[lo : lo + 3].reshape(9, C),
-                gap,
-                after[lo : lo + 3].reshape(9, C),
-                gap,
-            ],
-            axis=0,
-        )
-
-    top, bottom = rim(0), rim(TR - 3)
-    top, bottom, w_up, w_down = lax.optimization_barrier((top, bottom, w_up, w_down))
+    upper = half_row == 0
+    top, bottom = tok[: 3 * TC], tok[(TR - 3) * TC :]
+    first, second = jnp.where(upper, bottom, top), jnp.where(upper, top, bottom)
+    first, second, w_up, w_down = lax.optimization_barrier((first, second, w_up, w_down))
     w_wide = jnp.concatenate([w_qkv, w_up], axis=0)
     w_tall = jnp.concatenate([w_out, w_down], axis=0)
-    first = swap(jnp.where(upper, bottom, top), ROW, 0)
-    second = swap(jnp.where(upper, top, bottom), ROW, 1)
+    first = swap(first, ROW, 0)
+    second = swap(second, ROW, 1)
+    intra, inter = pl.pallas_call(
+        edge_kernel,
+        out_shape=[sds((80, C), BF)] * 2,
+        in_specs=smem + vm(3),
+        out_specs=vm(2),
+        scratch_shapes=[pltpu.VMEM((2, 80, C), F32)],
+        name="edges",
+        **params(16),
+    )(pos, tok, first, second)
+    inter = swap(inter, COL, 1)
+    intra = swap(intra, COL, 0)
 
     outs = pl.pallas_call(
         functools.partial(main_kernel, rows_total=rows_total, cols_total=cols_total),

time: 70 us -> 68.7 us (0.981)
  waiting for transfers between devices: 13.6 us -> 10.5 us
  starting transfers between devices: 32.3 us -> 34 us
  other arithmetic: 1.2 us -> 2.35 us
  local copies, waits for them, and re-layouts: 1.15 us -> 0.03 us
    all_to_all x1, waiting for transfers between devices: 3.84 us -> 0.73 us  [body(): lax.all_to_all(mine.reshape(64, CHUNK, 128), CHIPS, 0, 0, tiled=True)]
    all_to_all x1, starting transfers between devices: 12 us -> 13.5 us  [body(): lax.all_to_all(mine.reshape(64, CHUNK, 128), CHIPS, 0, 0, tiled=True)]
    concatenate x1, other arithmetic: 0.05 us -> 1.22 us  [body(): w_wide = jnp.concatenate([w_qkv, w_up], axis=0)]
    slice x2 -> x0, local copies, waits for them, and re-layouts: 0.97 us -> none  [the longest x1 0.96 us: rim(): tok[lo * TC:(lo + 3) * TC]]
    ppermute x8, starting transfers between devices: 19.5 us -> 20.4 us  [swap(): return lax.ppermute(x, axes, pairs + [(b, a) for a, b in pairs])]
where the time goes in v5:
time: 68.7 us; the launch traced here: 67.4 us
  starting transfers between devices  34 us (49%)
  Pallas kernels  19.7 us (29%)
  waiting for transfers between devices  10.5 us (15%)
  other arithmetic  2.35 us (3%)
  between operations  0.84 us (1%)
    ppermute x8, starting transfers between devices, swap(): return lax.ppermute(x, axes, pairs + [(b, a) for a, b in pairs])  20.4 us
    pallas_call x1, Pallas kernels, body(): pl.pallas_call(functools.partial(main_kernel, rows_total=rows_total, cols...  14.8 us
    all_to_all x1, starting transfers between devices, body(): lax.all_to_all(mine.reshape(64, CHUNK, 128), CHIPS, 0, 0, tiled=True)  13.5 us
    ppermute x8, waiting for transfers between devices, swap(): return lax.ppermute(x, axes, pairs + [(b, a) for a, b in pairs])  9.77 us
    pallas_call x1, Pallas kernels, body(): pl.pallas_call(token_kernel, out_shape=sds((flat, C), BF), in_specs=smem...  1.97 us
  transfers between devices with their start and end apart: 10, of which 4 were waited for; matrix products, arithmetic and copies ran while one was open for 2% of the time, Pallas kernels for 5%

profile of v5, /device:TPU:1, one launch (start us, length us, event | category | flops | bytes accessed | tf_op | source)
XLA Modules:
  0.0 67.4 jit_solution(7942702600084236330)
XLA Ops:
  0.6 1.0 %broadcast_select_fusion = (bf16[3,64,256]{2,1,0:T(8,128)(2,1)S(1)}, bf16[3,64,256]{2,1,0:T(8,128)(2,1)S(1)}) fusion(pred[]{:T(512)S(6)} %eq.3, bf16[16,64,256]{2,1,0:T(8,128)(2,1)} %param.7), kind=kLoop, calls=%fused_computation.2 | loop fusion | flops 98304 | bytes 393217 | tf_op jit(solution)/shard_map/jit(_where)/select_n | solution.py:419
  1.7 4.5 %collective-permute-start = (bf16[192,256]{1,0:T(8,128)(2,1)S(1)}, bf16[192,256]{1,0:T(8,128)(2,1)S(1)}, u32[]{:S(2)}, u32[]{:S(2)}) collective-permute-start(bf16[192,256]{1,0:T(8,128)(2,1)S(1)} %bitcast.16), channel_id=1, source_target_pairs={{0,16},{32,48},{64,80},{96,112},{16,0},{48,32},{80,64},{112,96},{1... | collective-permute-start | bytes 294920 | tf_op jit(solution)/shard_map/ppermute | solution.py:401
  6.2 0.7 collective-permute-start.1
  6.9 0.0 copy-start.3
  6.9 0.0 copy-start.4
  6.9 1.2 %pad_maximum_fusion.w_wide = bf16[512,768]{1,0:T(8,128)(2,1)S(1)} fusion(bf16[256,768]{1,0:T(8,128)(2,1)} %param.12, bf16[256,768]{1,0:T(8,128)(2,1)} %param.10), kind=kLoop, calls=%fused_computation | loop fusion | flops 1572864 | bytes 1572864 | tf_op jit(solution)/shard_map/concatenate | solution.py:421
  8.1 0.0 copy-start.1
  8.1 0.0 copy-start.2
  8.1 0.1 pad_add_fusion.pos
  8.2 0.5 collective-permute-done.first
  8.7 0.0 collective-permute-done.1.second
  8.7 0.6 edges.1
  9.3 1.3 %collective-permute-start.2 = (bf16[80,256]{1,0:T(8,128)(2,1)S(1)}, bf16[80,256]{1,0:T(8,128)(2,1)S(1)}, u32[]{:S(2)}, u32[]{:S(2)}) collective-permute-start(bf16[80,256]{1,0:T(8,128)(2,1)S(1)} %get-tuple-element.30), channel_id=1, source_target_pairs={{0,1},{2,3},{4,5},{6,7},{8,9},{10,11},{12,13},{14,15},{1,0},{3,2},... | collective-permute-start | bytes 122888 | tf_op jit(solution)/shard_map/ppermute | solution.py:401
  10.6 2.9 %collective-permute-start.3 = (bf16[80,256]{1,0:T(8,128)(2,1)S(1)}, bf16[80,256]{1,0:T(8,128)(2,1)S(1)}, u32[]{:S(2)}, u32[]{:S(2)}) collective-permute-start(bf16[80,256]{1,0:T(8,128)(2,1)S(1)} %get-tuple-element.31), channel_id=1, source_target_pairs={{1,2},{3,4},{5,6},{7,8},{9,10},{11,12},{13,14},{2,1},{4,3},{6,5},{... | collective-permute-start | bytes 122888 | tf_op jit(solution)/shard_map/ppermute | solution.py:401
  13.6 0.0 collective-permute-done.2.intra
  13.6 2.3 %collective-permute-done.3.inter = bf16[80,256]{1,0:T(8,128)(2,1)S(1)} collective-permute-done((bf16[80,256]{1,0:T(8,128)(2,1)S(1)}, bf16[80,256]{1,0:T(8,128)(2,1)S(1)}, u32[]{:S(2)}, u32[]{:S(2)}) %collective-permute-start.3) | collective-permute-done | bytes 40992 | tf_op jit(solution)/shard_map/ppermute | solution.py:401
  15.9 14.8 %block_backward.1 = (bf16[1024,256]{1,0:T(8,128)(2,1)S(1)}, f32[1024,256]{1,0:T(8,128)S(1)}, f32[96,256]{1,0:T(8,128)S(1)}, bf16[224,256]{1,0:T(8,128)(2,1)S(1)}...) custom-call(s32[4]{0:T(128)S(1)} %pad_add_fusion.pos, ...), custom_call_target="tpu_custom_call" | custom-call | tf_op jit(solution)/shard_map/block_backward/pallas_call | solution.py:437
  30.7 0.1 collective-permute-start.4
  30.8 6.0 %collective-permute-start.5 = (bf16[224,256]{1,0:T(8,128)(2,1)S(1)}, bf16[224,256]{1,0:T(8,128)(2,1)S(1)}, u32[]{:S(2)}, u32[]{:S(2)}) collective-permute-start(bf16[224,256]{1,0:T(8,128)(2,1)S(1)} %get-tuple-element.39), channel_id=1, source_target_pairs={{0,16},{32,48},{64,80},{96,112},{16,0},{48,32},{80,64},{112,96},{1... | collective-permute-start | bytes 344072 | tf_op jit(solution)/shard_map/ppermute | solution.py:401
  36.8 0.7 collective-permute-start.6
  37.5 0.0 collective-permute-done.4.got
  37.5 1.1 %add_core.1 = bf16[3072,128]{1,0:T(8,128)(2,1)} custom-call(bf16[3072,128]{1,0:T(8,128)(2,1)S(1)} %get-tuple-element.34.keep, bf16[3072,128]{1,0:T(8,128)(2,1)S(1)} %collective-permute-done.4.got), custom_call_target="tpu_custom_call" | custom-call | tf_op jit(solution)/shard_map/add_core/pallas_call | solution.py:478
  38.5 13.5 %all-to-all-start = ((bf16[64,48,128]{2,1,0:T(8,128)(2,1)}), bf16[64,48,128]{2,1,0:T(8,128)(2,1)S(1)}, u32[]{:S(2)}, u32[]{:S(2)}) async-start(bf16[64,48,128]{2,1,0:T(8,128)(2,1)} %bitcast.8), calls=%async_computation | async-start | bytes 1572864 | tf_op jit(solution)/shard_map/all_to_all | solution.py:486
  52.1 0.0 collective-permute-done.6.second
  52.1 0.6 sides.1
  52.7 1.3 %collective-permute-start.7 = (bf16[48,256]{1,0:T(8,128)(2,1)S(1)}, bf16[48,256]{1,0:T(8,128)(2,1)S(1)}, u32[]{:S(2)}, u32[]{:S(2)}) collective-permute-start(bf16[48,256]{1,0:T(8,128)(2,1)S(1)} %get-tuple-element.41), channel_id=1, source_target_pairs={{0,1},{2,3},{4,5},{6,7},{8,9},{10,11},{12,13},{14,15},{1,0},{3,2},... | collective-permute-start | bytes 73736 | tf_op jit(solution)/shard_map/ppermute | solution.py:401
  53.9 3.1 %collective-permute-start.8 = (bf16[48,256]{1,0:T(8,128)(2,1)S(1)}, bf16[48,256]{1,0:T(8,128)(2,1)S(1)}, u32[]{:S(2)}, u32[]{:S(2)}) collective-permute-start(bf16[48,256]{1,0:T(8,128)(2,1)S(1)} %get-tuple-element.42), channel_id=1, source_target_pairs={{1,2},{3,4},{5,6},{7,8},{9,10},{11,12},{13,14},{2,1},{4,3},{6,5},{... | collective-permute-start | bytes 73736 | tf_op jit(solution)/shard_map/ppermute | solution.py:401
  57.0 0.0 collective-permute-done.7.intra
  57.0 6.9 %collective-permute-done.8.inter = bf16[48,256]{1,0:T(8,128)(2,1)S(1)} collective-permute-done((bf16[48,256]{1,0:T(8,128)(2,1)S(1)}, bf16[48,256]{1,0:T(8,128)(2,1)S(1)}, u32[]{:S(2)}, u32[]{:S(2)}) %collective-permute-start.8) | collective-permute-done | bytes 24608 | tf_op jit(solution)/shard_map/ppermute | solution.py:401
  64.0 2.0 %grad_tokens.1 = bf16[1024,256]{1,0:T(8,128)(2,1)} custom-call(s32[4]{0:T(128)S(1)} %pad_add_fusion.pos, bf16[1024,256]{1,0:T(8,128)(2,1)S(1)} %bitcast.12, bf16[1024,256]{1,0:T(8,128)(2,1)S(1)} %get-tuple-element.36.gr, f32[1024,256]{1,0:T(8,128)S(1)} %get-tuple-element.37.gh, bf16[48,256]{1,0:T(8,128)(2,1)S(1)} %collective-permute-done.7.intra, ...), custom_call_target="tpu_custom_call" | custom-call | flops 7864320 | bytes 2621440 | tf_op jit(solution)/shard_map/grad_tokens/pallas_call | solution.py:501
  66.0 0.7 %all-to-all-done.parts = bf16[64,48,128]{2,1,0:T(8,128)(2,1)S(1)} async-done(((bf16[64,48,128]{2,1,0:T(8,128)(2,1)}), bf16[64,48,128]{2,1,0:T(8,128)(2,1)S(1)}, u32[]{:S(2)}, u32[]{:S(2)}) %all-to-all-start) | async-done | bytes 786464 | tf_op jit(solution)/shard_map/all_to_all | solution.py:486
  66.7 0.7 %weight_sums.1 = (f32[2,768]{1,0:T(2,128)}, f32[2,256]{1,0:T(2,128)}, f32[2,768]{1,0:T(2,128)}, f32[6,256]{1,0:T(8,128)}, f32[2,256]{1,0:T(2,128)}) custom-call(bf16[64,48,128]{2,1,0:T(8,128)(2,1)S(1)} %all-to-all-done.parts), custom_call_target="tpu_custom_call" | custom-call | tf_op jit(solution)/shard_map/weight_sums/pallas_call | solution.py:514
  (8 shorter events, 0.1 us)
Async XLA Ops:
  0.6 8.1 %copy-start = (bf16[16,64,256]{2,1,0:T(8,128)(2,1)S(1)}, bf16[16,64,256]{2,1,0:T(8,128)(2,1)}, u32[]{:S(2)}) copy-start(bf16[16,64,256]{2,1,0:T(8,128)(2,1)} %param.7) | copy-start | bytes 1572868
  1.7 7.0 %collective-permute-start = (bf16[192,256]{1,0:T(8,128)(2,1)S(1)}, bf16[192,256]{1,0:T(8,128)(2,1)S(1)}, u32[]{:S(2)}, u32[]{:S(2)}) collective-permute-start(bf16[192,256]{1,0:T(8,128)(2,1)S(1)} %bitcast.16), channel_id=1, source_target_pairs={{0,16},{32,48},{64,80},{96,112},{16,0},{48,32},{80,64},{112,96},{1... | collective-permute-start | bytes 294920 | tf_op jit(solution)/shard_map/ppermute | solution.py:401
  6.2 2.5 %collective-permute-start.1 = (bf16[192,256]{1,0:T(8,128)(2,1)S(1)}, bf16[192,256]{1,0:T(8,128)(2,1)S(1)}, u32[]{:S(2)}, u32[]{:S(2)}) collective-permute-start(bf16[192,256]{1,0:T(8,128)(2,1)S(1)} %bitcast.15), channel_id=1, source_target_pairs={{16,32},{48,64},{80,96},{32,16},{64,48},{96,80},{17,33},{49,65},{8... | collective-permute-start | bytes 294920 | tf_op jit(solution)/shard_map/ppermute | solution.py:401
  6.9 6.7 %copy-start.3 = (bf16[768,256]{1,0:T(8,128)(2,1)S(1)}, bf16[768,256]{1,0:T(8,128)(2,1)}, u32[]{:S(2)}) copy-start(bf16[768,256]{1,0:T(8,128)(2,1)} %param.13) | copy-start | bytes 1179652
  6.9 6.7 %copy-start.4 = (bf16[256,256]{1,0:T(8,128)(2,1)S(1)}, bf16[256,256]{1,0:T(8,128)(2,1)}, u32[]{:S(2)}) copy-start(bf16[256,256]{1,0:T(8,128)(2,1)} %param.11) | copy-start | bytes 393220
  8.1 7.8 %copy-start.1 = (bf16[16,64,256]{2,1,0:T(8,128)(2,1)S(1)}, bf16[16,64,256]{2,1,0:T(8,128)(2,1)}, u32[]{:S(2)}) copy-start(bf16[16,64,256]{2,1,0:T(8,128)(2,1)} %param.8) | copy-start | bytes 1572868
  8.1 7.8 %copy-start.2 = (f32[2,256]{1,0:T(2,128)S(1)}, f32[2,256]{1,0:T(2,128)}, u32[]{:S(2)}) copy-start(f32[2,256]{1,0:T(2,128)} %scales.3) | copy-start | bytes 6148
  9.3 4.3 %collective-permute-start.2 = (bf16[80,256]{1,0:T(8,128)(2,1)S(1)}, bf16[80,256]{1,0:T(8,128)(2,1)S(1)}, u32[]{:S(2)}, u32[]{:S(2)}) collective-permute-start(bf16[80,256]{1,0:T(8,128)(2,1)S(1)} %get-tuple-element.30), channel_id=1, source_target_pairs={{0,1},{2,3},{4,5},{6,7},{8,9},{10,11},{12,13},{14,15},{1,0},{3,2},... | collective-permute-start | bytes 122888 | tf_op jit(solution)/shard_map/ppermute | solution.py:401
  10.6 5.3 %collective-permute-start.3 = (bf16[80,256]{1,0:T(8,128)(2,1)S(1)}, bf16[80,256]{1,0:T(8,128)(2,1)S(1)}, u32[]{:S(2)}, u32[]{:S(2)}) collective-permute-start(bf16[80,256]{1,0:T(8,128)(2,1)S(1)} %get-tuple-element.31), channel_id=1, source_target_pairs={{1,2},{3,4},{5,6},{7,8},{9,10},{11,12},{13,14},{2,1},{4,3},{6,5},{... | collective-permute-start | bytes 122888 | tf_op jit(solution)/shard_map/ppermute | solution.py:401
  30.7 6.7 %collective-permute-start.4 = (bf16[3072,128]{1,0:T(8,128)(2,1)S(1)}, bf16[3072,128]{1,0:T(8,128)(2,1)S(1)}, u32[]{:S(2)}, u32[]{:S(2)}) collective-permute-start(bf16[3072,128]{1,0:T(8,128)(2,1)S(1)} %get-tuple-element.35), channel_id=1, source_target_pairs={{0,1},{1,0},{2,3},{3,2},{4,5},{5,4},{6,7},{7,6},{8,9},{9,8},{10,11... | collective-permute-start | bytes 2359304 | tf_op jit(solution)/shard_map/ppermute | solution.py:475
  30.8 21.2 %collective-permute-start.5 = (bf16[224,256]{1,0:T(8,128)(2,1)S(1)}, bf16[224,256]{1,0:T(8,128)(2,1)S(1)}, u32[]{:S(2)}, u32[]{:S(2)}) collective-permute-start(bf16[224,256]{1,0:T(8,128)(2,1)S(1)} %get-tuple-element.39), channel_id=1, source_target_pairs={{0,16},{32,48},{64,80},{96,112},{16,0},{48,32},{80,64},{112,96},{1... | collective-permute-start | bytes 344072 | tf_op jit(solution)/shard_map/ppermute | solution.py:401
  36.8 15.3 %collective-permute-start.6 = (bf16[224,256]{1,0:T(8,128)(2,1)S(1)}, bf16[224,256]{1,0:T(8,128)(2,1)S(1)}, u32[]{:S(2)}, u32[]{:S(2)}) collective-permute-start(bf16[224,256]{1,0:T(8,128)(2,1)S(1)} %get-tuple-element.40), channel_id=1, source_target_pairs={{16,32},{48,64},{80,96},{32,16},{64,48},{96,80},{17,33},{49,65},{8... | collective-permute-start | bytes 344072 | tf_op jit(solution)/shard_map/ppermute | solution.py:401
  38.5 28.1 %all-to-all-start = ((bf16[64,48,128]{2,1,0:T(8,128)(2,1)}), bf16[64,48,128]{2,1,0:T(8,128)(2,1)S(1)}, u32[]{:S(2)}, u32[]{:S(2)}) async-start(bf16[64,48,128]{2,1,0:T(8,128)(2,1)} %bitcast.8), calls=%async_computation | async-start | bytes 1572864 | tf_op jit(solution)/shard_map/all_to_all | solution.py:486
  52.7 4.4 %collective-permute-start.7 = (bf16[48,256]{1,0:T(8,128)(2,1)S(1)}, bf16[48,256]{1,0:T(8,128)(2,1)S(1)}, u32[]{:S(2)}, u32[]{:S(2)}) collective-permute-start(bf16[48,256]{1,0:T(8,128)(2,1)S(1)} %get-tuple-element.41), channel_id=1, source_target_pairs={{0,1},{2,3},{4,5},{6,7},{8,9},{10,11},{12,13},{14,15},{1,0},{3,2},... | collective-permute-start | bytes 73736 | tf_op jit(solution)/shard_map/ppermute | solution.py:401
  53.9 10.1 %collective-permute-start.8 = (bf16[48,256]{1,0:T(8,128)(2,1)S(1)}, bf16[48,256]{1,0:T(8,128)(2,1)S(1)}, u32[]{:S(2)}, u32[]{:S(2)}) collective-permute-start(bf16[48,256]{1,0:T(8,128)(2,1)S(1)} %get-tuple-element.42), channel_id=1, source_target_pairs={{1,2},{3,4},{5,6},{7,8},{9,10},{11,12},{13,14},{2,1},{4,3},{6,5},{... | collective-permute-start | bytes 73736 | tf_op jit(solution)/shard_map/ppermute | solution.py:401

commit v6 on v5

--- a/solution.py
+++ b/solution.py
@@ -167,7 +167,7 @@
             kv[r, lo : lo + 3, :] = got[at : at + 3, :]
     dkv[...] = jnp.zeros_like(dkv)
 
-    blocks = [(rb, cb) for cb in range(8) for rb in range(2)]
+    blocks = [(rb, cb) for odd in range(2) for rb in range(2) for cb in range(odd, 8, 2)]
 
     def block_of(ref, r0, c0):
         return ref[r0 : r0 + 8, c0 : c0 + 8, :].reshape(64, C)
@@ -225,6 +225,22 @@
         gdown[0, n * 256 : n * 256 + 256, :] = got[:, :128]
         gdown[1, n * 256 : n * 256 + 256, :] = got[:, 128:]
 
+    def pack(c, j, n):
+        pk[c, pl.ds(j * 14 + n, 64, stride=CHUNK), :] = gmat[n, pl.ds(2 * c + j, 64, stride=4), :]
+
+    def pack_down(c, j, n):
+        pk[c, pl.ds(28 + j * 2 + n, 64, stride=CHUNK), :] = gdown[
+            n, pl.ds(6 * c + j, 64, stride=12), :
+        ]
+
+    for c in range(2):
+        for j in range(2):
+            for n in range(6, 14):
+                pack(c, j, n)
+        for j in range(6):
+            for n in range(2):
+                pack_down(c, j, n)
+
     for i, (rb, cb) in enumerate(blocks):
         r0, c0 = 8 * rb, 8 * cb
         slab = slab_of(r0, c0)
@@ -264,10 +280,10 @@
 
     gq = jnp.zeros((C, C), F32)
     gkv = tn(h_halo, d_rims)
-    for i in range(4):
-        at = slice(256 * i, 256 * i + 256)
-        d_q = dq[4 * i : 4 * i + 4].reshape(256, C).astype(BF)
-        d_kv = dkv[3 + 4 * i : 7 + 4 * i, 3 : TC + 3, :].reshape(256, 2 * C).astype(BF)
+    for i in range(2):
+        at = slice(512 * i, 512 * i + 512)
+        d_q = dq[8 * i : 8 * i + 8].reshape(512, C).astype(BF)
+        d_kv = dkv[3 + 8 * i : 11 + 8 * i, 3 : TC + 3, :].reshape(512, 2 * C).astype(BF)
         o_gh[at, :] = nt(d_q, w_qkv[:, :C]) + nt(d_kv, w_qkv[:, C:])
         h = h1l[at, :]
         gq = gq + tn(h, d_q)
@@ -285,15 +301,8 @@
 
     for c in range(2):
         for j in range(2):
-            for n in range(14):
-                pk[c, pl.ds(j * 14 + n, 64, stride=CHUNK), :] = gmat[
-                    n, pl.ds(2 * c + j, 64, stride=4), :
-                ]
-        for j in range(6):
-            for n in range(2):
-                pk[c, pl.ds(28 + j * 2 + n, 64, stride=CHUNK), :] = gdown[
-                    n, pl.ds(6 * c + j, 64, stride=12), :
-                ]
+            for n in range(6):
+                pack(c, j, n)
         for j in range(4):
             pk[c, pl.ds(40 + j, 64, stride=CHUNK), :] = jnp.broadcast_to(rows[j], (64, 128))
             pk[c, pl.ds(44 + j, 64, stride=CHUNK), :] = jnp.zeros((64, 128), F32)

time: 68.7 us -> 68.3 us (level)
  no operation moved by 1% of the time
where the time goes in v6:
time: 68.3 us; the launch traced here: 67.1 us
  starting transfers between devices  33.9 us (50%)
  Pallas kernels  19.4 us (28%)
  waiting for transfers between devices  10.5 us (15%)
  other arithmetic  2.35 us (3%)
  between operations  0.84 us (1%)
    ppermute x8, starting transfers between devices, swap(): return lax.ppermute(x, axes, pairs + [(b, a) for a, b in pairs])  20.4 us
    pallas_call x1, Pallas kernels, body(): pl.pallas_call(functools.partial(main_kernel, rows_total=rows_total, cols...  14.5 us
    all_to_all x1, starting transfers between devices, body(): lax.all_to_all(mine.reshape(64, CHUNK, 128), CHIPS, 0, 0, tiled=True)  13.5 us
    ppermute x8, waiting for transfers between devices, swap(): return lax.ppermute(x, axes, pairs + [(b, a) for a, b in pairs])  9.77 us
    pallas_call x1, Pallas kernels, body(): pl.pallas_call(token_kernel, out_shape=sds((flat, C), BF), in_specs=smem...  1.97 us
  transfers between devices with their start and end apart: 10, of which 4 were waited for; matrix products, arithmetic and copies ran while one was open for 2% of the time, Pallas kernels for 5%

profile of v6, /device:TPU:1, one launch (start us, length us, event | category | flops | bytes accessed | tf_op | source)
XLA Modules:
  0.0 67.1 jit_solution(11436458902970802467)
XLA Ops:
  0.6 1.0 %broadcast_select_fusion = (bf16[3,64,256]{2,1,0:T(8,128)(2,1)S(1)}, bf16[3,64,256]{2,1,0:T(8,128)(2,1)S(1)}) fusion(pred[]{:T(512)S(6)} %eq.3, bf16[16,64,256]{2,1,0:T(8,128)(2,1)} %param.7), kind=kLoop, calls=%fused_computation.2 | loop fusion | flops 98304 | bytes 393217 | tf_op jit(solution)/shard_map/jit(_where)/select_n | solution.py:428
  1.7 4.5 %collective-permute-start = (bf16[192,256]{1,0:T(8,128)(2,1)S(1)}, bf16[192,256]{1,0:T(8,128)(2,1)S(1)}, u32[]{:S(2)}, u32[]{:S(2)}) collective-permute-start(bf16[192,256]{1,0:T(8,128)(2,1)S(1)} %bitcast.16), channel_id=1, source_target_pairs={{0,16},{32,48},{64,80},{96,112},{16,0},{48,32},{80,64},{112,96},{1... | collective-permute-start | bytes 294920 | tf_op jit(solution)/shard_map/ppermute | solution.py:410
  6.2 0.7 collective-permute-start.1
  6.9 0.0 copy-start.3
  6.9 0.0 copy-start.4
  6.9 1.2 %pad_maximum_fusion.w_wide = bf16[512,768]{1,0:T(8,128)(2,1)S(1)} fusion(bf16[256,768]{1,0:T(8,128)(2,1)} %param.12, bf16[256,768]{1,0:T(8,128)(2,1)} %param.10), kind=kLoop, calls=%fused_computation | loop fusion | flops 1572864 | bytes 1572864 | tf_op jit(solution)/shard_map/concatenate | solution.py:430
  8.1 0.0 copy-start.1
  8.1 0.0 copy-start.2
  8.1 0.1 pad_add_fusion.pos
  8.2 0.5 collective-permute-done.first
  8.7 0.6 edges.1
  9.3 1.3 %collective-permute-start.2 = (bf16[80,256]{1,0:T(8,128)(2,1)S(1)}, bf16[80,256]{1,0:T(8,128)(2,1)S(1)}, u32[]{:S(2)}, u32[]{:S(2)}) collective-permute-start(bf16[80,256]{1,0:T(8,128)(2,1)S(1)} %get-tuple-element.30), channel_id=1, source_target_pairs={{0,1},{2,3},{4,5},{6,7},{8,9},{10,11},{12,13},{14,15},{1,0},{3,2},... | collective-permute-start | bytes 122888 | tf_op jit(solution)/shard_map/ppermute | solution.py:410
  10.6 2.9 %collective-permute-start.3 = (bf16[80,256]{1,0:T(8,128)(2,1)S(1)}, bf16[80,256]{1,0:T(8,128)(2,1)S(1)}, u32[]{:S(2)}, u32[]{:S(2)}) collective-permute-start(bf16[80,256]{1,0:T(8,128)(2,1)S(1)} %get-tuple-element.31), channel_id=1, source_target_pairs={{1,2},{3,4},{5,6},{7,8},{9,10},{11,12},{13,14},{2,1},{4,3},{6,5},{... | collective-permute-start | bytes 122888 | tf_op jit(solution)/shard_map/ppermute | solution.py:410
  13.6 0.0 collective-permute-done.2.intra
  13.6 2.3 %collective-permute-done.3.inter = bf16[80,256]{1,0:T(8,128)(2,1)S(1)} collective-permute-done((bf16[80,256]{1,0:T(8,128)(2,1)S(1)}, bf16[80,256]{1,0:T(8,128)(2,1)S(1)}, u32[]{:S(2)}, u32[]{:S(2)}) %collective-permute-start.3) | collective-permute-done | bytes 40992 | tf_op jit(solution)/shard_map/ppermute | solution.py:410
  15.9 14.5 %block_backward.1 = (bf16[1024,256]{1,0:T(8,128)(2,1)S(1)}, f32[1024,256]{1,0:T(8,128)S(1)}, f32[96,256]{1,0:T(8,128)S(1)}, bf16[224,256]{1,0:T(8,128)(2,1)S(1)}...) custom-call(s32[4]{0:T(128)S(1)} %pad_add_fusion.pos, ...), custom_call_target="tpu_custom_call" | custom-call | tf_op jit(solution)/shard_map/block_backward/pallas_call | solution.py:446
  30.4 0.1 collective-permute-start.4
  30.5 6.0 %collective-permute-start.5 = (bf16[224,256]{1,0:T(8,128)(2,1)S(1)}, bf16[224,256]{1,0:T(8,128)(2,1)S(1)}, u32[]{:S(2)}, u32[]{:S(2)}) collective-permute-start(bf16[224,256]{1,0:T(8,128)(2,1)S(1)} %get-tuple-element.39), channel_id=1, source_target_pairs={{0,16},{32,48},{64,80},{96,112},{16,0},{48,32},{80,64},{112,96},{1... | collective-permute-start | bytes 344072 | tf_op jit(solution)/shard_map/ppermute | solution.py:410
  36.5 0.7 collective-permute-start.6
  37.1 0.0 collective-permute-done.4.got
  37.2 1.1 %add_core.1 = bf16[3072,128]{1,0:T(8,128)(2,1)} custom-call(bf16[3072,128]{1,0:T(8,128)(2,1)S(1)} %get-tuple-element.34.keep, bf16[3072,128]{1,0:T(8,128)(2,1)S(1)} %collective-permute-done.4.got), custom_call_target="tpu_custom_call" | custom-call | tf_op jit(solution)/shard_map/add_core/pallas_call | solution.py:487
  38.2 13.5 %all-to-all-start = ((bf16[64,48,128]{2,1,0:T(8,128)(2,1)}), bf16[64,48,128]{2,1,0:T(8,128)(2,1)S(1)}, u32[]{:S(2)}, u32[]{:S(2)}) async-start(bf16[64,48,128]{2,1,0:T(8,128)(2,1)} %bitcast.8), calls=%async_computation | async-start | bytes 1572864 | tf_op jit(solution)/shard_map/all_to_all | solution.py:495
  51.7 0.0 collective-permute-done.5.first
  51.7 0.0 collective-permute-done.6.second
  51.7 0.6 sides.1
  52.3 1.3 %collective-permute-start.7 = (bf16[48,256]{1,0:T(8,128)(2,1)S(1)}, bf16[48,256]{1,0:T(8,128)(2,1)S(1)}, u32[]{:S(2)}, u32[]{:S(2)}) collective-permute-start(bf16[48,256]{1,0:T(8,128)(2,1)S(1)} %get-tuple-element.41), channel_id=1, source_target_pairs={{0,1},{2,3},{4,5},{6,7},{8,9},{10,11},{12,13},{14,15},{1,0},{3,2},... | collective-permute-start | bytes 73736 | tf_op jit(solution)/shard_map/ppermute | solution.py:410
  53.6 3.1 %collective-permute-start.8 = (bf16[48,256]{1,0:T(8,128)(2,1)S(1)}, bf16[48,256]{1,0:T(8,128)(2,1)S(1)}, u32[]{:S(2)}, u32[]{:S(2)}) collective-permute-start(bf16[48,256]{1,0:T(8,128)(2,1)S(1)} %get-tuple-element.42), channel_id=1, source_target_pairs={{1,2},{3,4},{5,6},{7,8},{9,10},{11,12},{13,14},{2,1},{4,3},{6,5},{... | collective-permute-start | bytes 73736 | tf_op jit(solution)/shard_map/ppermute | solution.py:410
  56.7 0.0 collective-permute-done.7.intra
  56.7 6.9 %collective-permute-done.8.inter = bf16[48,256]{1,0:T(8,128)(2,1)S(1)} collective-permute-done((bf16[48,256]{1,0:T(8,128)(2,1)S(1)}, bf16[48,256]{1,0:T(8,128)(2,1)S(1)}, u32[]{:S(2)}, u32[]{:S(2)}) %collective-permute-start.8) | collective-permute-done | bytes 24608 | tf_op jit(solution)/shard_map/ppermute | solution.py:410
  63.6 2.0 %grad_tokens.1 = bf16[1024,256]{1,0:T(8,128)(2,1)} custom-call(s32[4]{0:T(128)S(1)} %pad_add_fusion.pos, bf16[1024,256]{1,0:T(8,128)(2,1)S(1)} %bitcast.12, bf16[1024,256]{1,0:T(8,128)(2,1)S(1)} %get-tuple-element.36.gr, f32[1024,256]{1,0:T(8,128)S(1)} %get-tuple-element.37.gh, bf16[48,256]{1,0:T(8,128)(2,1)S(1)} %collective-permute-done.7.intra, ...), custom_call_target="tpu_custom_call" | custom-call | flops 7864320 | bytes 2621440 | tf_op jit(solution)/shard_map/grad_tokens/pallas_call | solution.py:510
  65.6 0.7 %all-to-all-done.parts = bf16[64,48,128]{2,1,0:T(8,128)(2,1)S(1)} async-done(((bf16[64,48,128]{2,1,0:T(8,128)(2,1)}), bf16[64,48,128]{2,1,0:T(8,128)(2,1)S(1)}, u32[]{:S(2)}, u32[]{:S(2)}) %all-to-all-start) | async-done | bytes 786464 | tf_op jit(solution)/shard_map/all_to_all | solution.py:495
  66.4 0.7 %weight_sums.1 = (f32[2,768]{1,0:T(2,128)}, f32[2,256]{1,0:T(2,128)}, f32[2,768]{1,0:T(2,128)}, f32[6,256]{1,0:T(8,128)}, f32[2,256]{1,0:T(2,128)}) custom-call(bf16[64,48,128]{2,1,0:T(8,128)(2,1)S(1)} %all-to-all-done.parts), custom_call_target="tpu_custom_call" | custom-call | tf_op jit(solution)/shard_map/weight_sums/pallas_call | solution.py:523
  (8 shorter events, 0.1 us)
Async XLA Ops:
  0.6 8.1 %copy-start = (bf16[16,64,256]{2,1,0:T(8,128)(2,1)S(1)}, bf16[16,64,256]{2,1,0:T(8,128)(2,1)}, u32[]{:S(2)}) copy-start(bf16[16,64,256]{2,1,0:T(8,128)(2,1)} %param.7) | copy-start | bytes 1572868
  1.7 7.0 %collective-permute-start = (bf16[192,256]{1,0:T(8,128)(2,1)S(1)}, bf16[192,256]{1,0:T(8,128)(2,1)S(1)}, u32[]{:S(2)}, u32[]{:S(2)}) collective-permute-start(bf16[192,256]{1,0:T(8,128)(2,1)S(1)} %bitcast.16), channel_id=1, source_target_pairs={{0,16},{32,48},{64,80},{96,112},{16,0},{48,32},{80,64},{112,96},{1... | collective-permute-start | bytes 294920 | tf_op jit(solution)/shard_map/ppermute | solution.py:410
  6.2 2.5 %collective-permute-start.1 = (bf16[192,256]{1,0:T(8,128)(2,1)S(1)}, bf16[192,256]{1,0:T(8,128)(2,1)S(1)}, u32[]{:S(2)}, u32[]{:S(2)}) collective-permute-start(bf16[192,256]{1,0:T(8,128)(2,1)S(1)} %bitcast.15), channel_id=1, source_target_pairs={{16,32},{48,64},{80,96},{32,16},{64,48},{96,80},{17,33},{49,65},{8... | collective-permute-start | bytes 294920 | tf_op jit(solution)/shard_map/ppermute | solution.py:410
  6.9 6.7 %copy-start.3 = (bf16[768,256]{1,0:T(8,128)(2,1)S(1)}, bf16[768,256]{1,0:T(8,128)(2,1)}, u32[]{:S(2)}) copy-start(bf16[768,256]{1,0:T(8,128)(2,1)} %param.13) | copy-start | bytes 1179652
  6.9 6.7 %copy-start.4 = (bf16[256,256]{1,0:T(8,128)(2,1)S(1)}, bf16[256,256]{1,0:T(8,128)(2,1)}, u32[]{:S(2)}) copy-start(bf16[256,256]{1,0:T(8,128)(2,1)} %param.11) | copy-start | bytes 393220
  8.1 7.8 %copy-start.1 = (bf16[16,64,256]{2,1,0:T(8,128)(2,1)S(1)}, bf16[16,64,256]{2,1,0:T(8,128)(2,1)}, u32[]{:S(2)}) copy-start(bf16[16,64,256]{2,1,0:T(8,128)(2,1)} %param.8) | copy-start | bytes 1572868
  8.1 7.8 %copy-start.2 = (f32[2,256]{1,0:T(2,128)S(1)}, f32[2,256]{1,0:T(2,128)}, u32[]{:S(2)}) copy-start(f32[2,256]{1,0:T(2,128)} %scales.3) | copy-start | bytes 6148
  9.3 4.3 %collective-permute-start.2 = (bf16[80,256]{1,0:T(8,128)(2,1)S(1)}, bf16[80,256]{1,0:T(8,128)(2,1)S(1)}, u32[]{:S(2)}, u32[]{:S(2)}) collective-permute-start(bf16[80,256]{1,0:T(8,128)(2,1)S(1)} %get-tuple-element.30), channel_id=1, source_target_pairs={{0,1},{2,3},{4,5},{6,7},{8,9},{10,11},{12,13},{14,15},{1,0},{3,2},... | collective-permute-start | bytes 122888 | tf_op jit(solution)/shard_map/ppermute | solution.py:410
  10.6 5.3 %collective-permute-start.3 = (bf16[80,256]{1,0:T(8,128)(2,1)S(1)}, bf16[80,256]{1,0:T(8,128)(2,1)S(1)}, u32[]{:S(2)}, u32[]{:S(2)}) collective-permute-start(bf16[80,256]{1,0:T(8,128)(2,1)S(1)} %get-tuple-element.31), channel_id=1, source_target_pairs={{1,2},{3,4},{5,6},{7,8},{9,10},{11,12},{13,14},{2,1},{4,3},{6,5},{... | collective-permute-start | bytes 122888 | tf_op jit(solution)/shard_map/ppermute | solution.py:410
  30.4 6.7 %collective-permute-start.4 = (bf16[3072,128]{1,0:T(8,128)(2,1)S(1)}, bf16[3072,128]{1,0:T(8,128)(2,1)S(1)}, u32[]{:S(2)}, u32[]{:S(2)}) collective-permute-start(bf16[3072,128]{1,0:T(8,128)(2,1)S(1)} %get-tuple-element.35), channel_id=1, source_target_pairs={{0,1},{1,0},{2,3},{3,2},{4,5},{5,4},{6,7},{7,6},{8,9},{9,8},{10,11... | collective-permute-start | bytes 2359304 | tf_op jit(solution)/shard_map/ppermute | solution.py:484
  30.5 21.2 %collective-permute-start.5 = (bf16[224,256]{1,0:T(8,128)(2,1)S(1)}, bf16[224,256]{1,0:T(8,128)(2,1)S(1)}, u32[]{:S(2)}, u32[]{:S(2)}) collective-permute-start(bf16[224,256]{1,0:T(8,128)(2,1)S(1)} %get-tuple-element.39), channel_id=1, source_target_pairs={{0,16},{32,48},{64,80},{96,112},{16,0},{48,32},{80,64},{112,96},{1... | collective-permute-start | bytes 344072 | tf_op jit(solution)/shard_map/ppermute | solution.py:410
  36.5 15.3 %collective-permute-start.6 = (bf16[224,256]{1,0:T(8,128)(2,1)S(1)}, bf16[224,256]{1,0:T(8,128)(2,1)S(1)}, u32[]{:S(2)}, u32[]{:S(2)}) collective-permute-start(bf16[224,256]{1,0:T(8,128)(2,1)S(1)} %get-tuple-element.40), channel_id=1, source_target_pairs={{16,32},{48,64},{80,96},{32,16},{64,48},{96,80},{17,33},{49,65},{8... | collective-permute-start | bytes 344072 | tf_op jit(solution)/shard_map/ppermute | solution.py:410
  38.2 28.1 %all-to-all-start = ((bf16[64,48,128]{2,1,0:T(8,128)(2,1)}), bf16[64,48,128]{2,1,0:T(8,128)(2,1)S(1)}, u32[]{:S(2)}, u32[]{:S(2)}) async-start(bf16[64,48,128]{2,1,0:T(8,128)(2,1)} %bitcast.8), calls=%async_computation | async-start | bytes 1572864 | tf_op jit(solution)/shard_map/all_to_all | solution.py:495
  52.3 4.4 %collective-permute-start.7 = (bf16[48,256]{1,0:T(8,128)(2,1)S(1)}, bf16[48,256]{1,0:T(8,128)(2,1)S(1)}, u32[]{:S(2)}, u32[]{:S(2)}) collective-permute-start(bf16[48,256]{1,0:T(8,128)(2,1)S(1)} %get-tuple-element.41), channel_id=1, source_target_pairs={{0,1},{2,3},{4,5},{6,7},{8,9},{10,11},{12,13},{14,15},{1,0},{3,2},... | collective-permute-start | bytes 73736 | tf_op jit(solution)/shard_map/ppermute | solution.py:410
  53.6 10.1 %collective-permute-start.8 = (bf16[48,256]{1,0:T(8,128)(2,1)S(1)}, bf16[48,256]{1,0:T(8,128)(2,1)S(1)}, u32[]{:S(2)}, u32[]{:S(2)}) collective-permute-start(bf16[48,256]{1,0:T(8,128)(2,1)S(1)} %get-tuple-element.42), channel_id=1, source_target_pairs={{1,2},{3,4},{5,6},{7,8},{9,10},{11,12},{13,14},{2,1},{4,3},{6,5},{... | collective-permute-start | bytes 73736 | tf_op jit(solution)/shard_map/ppermute | solution.py:410
